TPU v7x, 512 devices: a whole 4x4x16 slice. The times are simulated.
512 devices in a mesh: gz: 4 (over z_lo), gy: 4 (over z_hi), gx: 32 (over y, x, core).
Axes of the slice: x: 4, y: 4, z: 16 (z_hi: 4, z_lo: 4; z = z_hi * 4 + z_lo), core: 2. Of those that a mesh axis runs over, the one named last changes fastest.
Arguments:
- section: bfloat16 [4, 1024, 8192], P('gz', 'gy', 'gx'), may hold values from -6 to 6
- first_kernel: float32 [16, 9], replicated, may hold values from -2 to 2
- first_bias: float32 [16], replicated, may hold values from -3 to 3
- second_kernel: bfloat16 [9, 16, 16], replicated, may hold values from -0.5 to 0.5
- second_bias: float32 [16], replicated, may hold values from -3 to 3
- head_weight: float32 [16], replicated, may hold values from -1.5 to 1.5
Outputs:
- spectra: float32 [4, 2, 1024, 8192], P('gz', None, 'gy', 'gx')
All inputs are finite; a program needn't handle non-finite values.
Results may differ from a plain program's by a relative error of at most 0.0075.
Values may be sent and summed in bfloat16 or wider, within the bound.
No kernel may reach another device: no remote copies, remote signals or barrier semaphores. Data moves between devices by JAX's collectives and lax.ppermute only.
A program may use at most 128 MiB of HBM per device.

v0:
```python
import math

import jax
import jax.numpy as jnp
from jax import lax
from jax.sharding import PartitionSpec as P

PATCH = 128


def with_halo(cells, sides, width):
    for axis, dim in sides:
        count = lax.axis_size(axis)
        ends = count - 1
        head = lax.slice_in_dim(cells, 0, width, axis=dim)
        tail = lax.slice_in_dim(cells, cells.shape[dim] - width, cells.shape[dim], axis=dim)
        cells = jnp.concatenate(
            [
                lax.ppermute(tail, axis, [(i, (i + 1) % count) for i in range(ends)]),
                cells,
                lax.ppermute(head, axis, [((i + 1) % count, i) for i in range(ends)]),
            ],
            axis=dim,
        )
    return cells


def from_behind(value, axis, steps):
    count = lax.axis_size(axis)
    leading, last = (max(0, -steps), min(count, count - steps))
    return lax.ppermute(value, axis, [(source, source + steps) for source in range(leading, last)])


def dft_tables(length):
    positions = jnp.arange(length, dtype=jnp.int32)
    phase_step = positions[:, None] * positions[None, :] % length
    angles = phase_step.astype(jnp.float32) * (2.0 * math.pi / length)
    scaling = 1.0 / math.sqrt(length)
    cosine_table = (jnp.cos(angles) * scaling).astype(jnp.bfloat16)
    sine_table = (jnp.sin(angles) * scaling).astype(jnp.bfloat16)
    return (cosine_table, sine_table)


def first_layer(padded, kernel, offsets):
    row_count = padded.shape[0] - 2
    col_count = padded.shape[1] - 2
    values = padded.astype(jnp.float32)
    summed = jnp.zeros((kernel.shape[0], row_count, col_count), jnp.float32)
    for tap_index in range(9):
        row_off = tap_index // 3
        col_off = tap_index % 3
        window = values[row_off : row_off + row_count, col_off : col_off + col_count]
        summed = summed + kernel[:, tap_index][:, None, None] * window[None]
    return jax.nn.relu(summed + offsets[:, None, None]).astype(jnp.bfloat16)


def second_layer(hidden_pad, center, kernel, offsets, head_vec):
    row_count = hidden_pad.shape[1] - 2
    col_count = hidden_pad.shape[2] - 2
    summed = jnp.zeros((kernel.shape[1], row_count, col_count), jnp.float32)
    for tap_index in range(9):
        row_off = tap_index // 3
        col_off = tap_index % 3
        window = hidden_pad[:, row_off : row_off + row_count, col_off : col_off + col_count]
        summed = summed + jnp.einsum(
            "oc,crw->orw", kernel[tap_index], window, preferred_element_type=jnp.float32
        )
    deep = jax.nn.relu(summed + offsets[:, None, None])
    return (center.astype(jnp.float32) + jnp.sum(head_vec[:, None, None] * deep, axis=0)).astype(
        jnp.bfloat16
    )


def spectrum(restored, cosine_table, sine_table):
    length = cosine_table.shape[0]
    row_count, col_count = restored.shape
    tiles = restored.reshape(row_count // length, length, col_count // length, length)
    rows_cos = jnp.einsum(
        "aibj,jk->aibk", tiles, cosine_table, preferred_element_type=jnp.float32
    ).astype(jnp.bfloat16)
    rows_sin = jnp.einsum(
        "aibj,jk->aibk", tiles, sine_table, preferred_element_type=jnp.float32
    ).astype(jnp.bfloat16)
    real_part = jnp.einsum(
        "ij,aibk->ajbk", cosine_table, rows_cos, preferred_element_type=jnp.float32
    ) - jnp.einsum("ij,aibk->ajbk", sine_table, rows_sin, preferred_element_type=jnp.float32)
    imag_part = -(
        jnp.einsum("ij,aibk->ajbk", cosine_table, rows_sin, preferred_element_type=jnp.float32)
        + jnp.einsum("ij,aibk->ajbk", sine_table, rows_cos, preferred_element_type=jnp.float32)
    )
    return jnp.stack(
        [real_part.reshape(row_count, col_count), imag_part.reshape(row_count, col_count)]
    )


def cross(first_spec, second_spec):
    real_out = first_spec[0] * second_spec[0] + first_spec[1] * second_spec[1]
    imag_out = first_spec[1] * second_spec[0] - first_spec[0] * second_spec[1]
    return jnp.stack([real_out, imag_out])


def on_device(section, first_kernel, first_bias, second_kernel, second_bias, head_weight):
    section_image = section[0]
    padded = with_halo(section_image, (("gy", 0), ("gx", 1)), 1)
    hidden = first_layer(padded, first_kernel, first_bias)
    hidden_pad = with_halo(hidden, (("gy", 1), ("gx", 2)), 1)
    restored = second_layer(hidden_pad, section_image, second_kernel, second_bias, head_weight)
    cosine_table, sine_table = dft_tables(PATCH)
    own_spectrum = spectrum(restored, cosine_table, sine_table)
    upper_image = from_behind(restored, "gz", -1)
    next_spectra = spectrum(upper_image, cosine_table, sine_table)
    return cross(own_spectrum, next_spectra)[None]


def solution(mesh):
    placed = (P("gz", "gy", "gx"), P(), P(), P(), P(), P())
    return jax.shard_map(
        on_device, mesh=mesh, in_specs=placed, out_specs=P("gz", None, "gy", "gx"), check_vma=False
    )
```

profile of v0, /device:TPU:16, one launch (start us, length us, event | category | flops | bytes accessed | tf_op | source)
XLA Modules:
  0.0 120.9 jit_solution(11253532472999028444)
XLA Ops:
  0.7 9.1 %collective-permute-start = (bf16[1,256]{1,0:T(2,128)(2,1)S(1)}, bf16[1,256]{1,0:T(2,128)(2,1)S(1)}, u32[]{:S(2)}, u32[]{:S(2)}) collective-permute-start(bf16[1,256]{1,0:T(2,128)(2,1)S(1)} %get-tuple-element.33), channel_id=1, source_target_pairs={{0,32},{32,64},{64,96},{1,33},{33,65},{65,97},{2,34},{34,66},{66,9... | collective-permute-start | bytes 1544 | tf_op jit(solution)/shard_map/ppermute | solution.py:19
  11.1 9.3 %collective-permute-done.1 = bf16[1,256]{1,0:T(2,128)(2,1)S(1)} collective-permute-done((bf16[1,256]{1,0:T(2,128)(2,1)S(1)}, bf16[1,256]{1,0:T(2,128)(2,1)S(1)}, u32[]{:S(2)}, u32[]{:S(2)}) %collective-permute-start.1) | collective-permute-done | bytes 544 | tf_op jit(solution)/shard_map/ppermute | solution.py:21
  21.5 1.9 %collective-permute-start.2 = (bf16[258,1]{1,0:T(8,128)(2,1)S(1)}, bf16[258,1]{1,0:T(8,128)(2,1)S(1)}, u32[]{:S(2)}, u32[]{:S(2)}) collective-permute-start(bf16[258,1]{1,0:T(8,128)(2,1)S(1)} %get-tuple-element.31), channel_id=1, source_target_pairs={{0,1},{1,2},{2,3},{3,4},{4,5},{5,6},{6,7},{7,8},{8,9},{9,10},{10,1... | collective-permute-start | bytes 1556 | tf_op jit(solution)/shard_map/ppermute | solution.py:19
  23.4 5.8 %collective-permute-start.3 = (bf16[258,1]{1,0:T(8,128)(2,1)S(1)}, bf16[258,1]{1,0:T(8,128)(2,1)S(1)}, u32[]{:S(2)}, u32[]{:S(2)}) collective-permute-start(bf16[258,1]{1,0:T(8,128)(2,1)S(1)} %get-tuple-element.32), channel_id=1, source_target_pairs={{1,0},{2,1},{3,2},{4,3},{5,4},{6,5},{7,6},{8,7},{9,8},{10,9},{11,1... | collective-permute-start | bytes 1556 | tf_op jit(solution)/shard_map/ppermute | solution.py:21
  33.2 6.3 %maximum_convert_fusion = bf16[16,256,256]{2,0,1:T(8,128)(2,1)S(1)} fusion(f32[16]{0:T(128)S(1)} %copy-done.3, f32[256,256]{1,0:T(8,128)S(1)} %get-tuple-element.23, f32[16]{0:T(128)S(1)} %get-tuple-element.12, f32[256,256]{1,0:T(8,128)S(1)} %get-tuple-element.24, f32[16]{0:T(128)S(1)} %get-tuple-element.13, f32[256,256]{1,0:T(8,128)S(1)} %get-tuple-element.25, ...), kind=kLoop, calls=%fused_computation.1 | loop fusion | flops 20971520 | bytes 4457088 | tf_op jit(solution)/shard_map/convert_element_type | solution.py:54
  39.5 7.8 %collective-permute-start.4 = (bf16[16,1,256]{2,0,1:T(8,128)(2,1)S(1)}, bf16[16,1,256]{2,0,1:T(8,128)(2,1)S(1)}, u32[]{:S(2)}, u32[]{:S(2)}) collective-permute-start(bf16[16,1,256]{2,0,1:T(8,128)(2,1)S(1)} %get-tuple-element.18), channel_id=1, source_target_pairs={{0,32},{32,64},{64,96},{1,33},{33,65},{65,97},{2,34},{34,66},{66,9... | collective-permute-start | bytes 24584 | tf_op jit(solution)/shard_map/ppermute | solution.py:19
  48.6 2.6 %fusion.49 = f32[256,256,16]{1,2,0:T(8,128)} fusion(bf16[16,256,256]{2,0,1:T(8,128)(2,1)S(1)} %maximum_convert_fusion, bf16[9,16,16]{2,1,0:T(8,128)(2,1)S(1)} %copy-done.2), kind=kOutput, calls=%fused_computation.71 | convolution fusion | flops 33554432 | bytes 6295552 | tf_op jit(solution)/shard_map/oc,crw->orw/dot_general | solution.py:65
  51.2 5.5 %collective-permute-done.5 = bf16[16,1,256]{2,0,1:T(8,128)(2,1)S(1)} collective-permute-done((bf16[16,1,256]{2,0,1:T(8,128)(2,1)S(1)}, bf16[16,1,256]{2,0,1:T(8,128)(2,1)S(1)}, u32[]{:S(2)}, u32[]{:S(2)}) %collective-permute-start.5) | collective-permute-done | bytes 8224 | tf_op jit(solution)/shard_map/ppermute | solution.py:21
  57.0 1.5 %fusion.126 = (bf16[16,258,1]{2,0,1:T(8,128)(2,1)S(1)}, bf16[16,258,1]{2,0,1:T(8,128)(2,1)}) fusion(bf16[16,258,256]{2,0,1:T(8,128)(2,1)S(1)} %pad_maximum_fusion.1), kind=kLoop, calls=%fused_computation.150 | loop fusion | bytes 33024 | tf_op jit(solution)/shard_map/slice | solution.py:15
  58.5 2.1 %copy.31 = bf16[16,258,1]{1,0,2:T(8,128)(2,1)S(1)} copy(bf16[16,258,1]{2,0,1:T(8,128)(2,1)} %get-tuple-element.17) | data formatting | bytes 16512 | tf_op jit(solution)/shard_map/slice | solution.py:16
  60.6 1.9 %collective-permute-start.6 = (bf16[16,258,1]{1,0,2:T(8,128)(2,1)S(1)}, bf16[16,258,1]{1,0,2:T(8,128)(2,1)S(1)}, u32[]{:S(2)}, u32[]{:S(2)}) collective-permute-start(bf16[16,258,1]{1,0,2:T(8,128)(2,1)S(1)} %copy.31), channel_id=1, source_target_pairs={{0,1},{1,2},{2,3},{3,4},{4,5},{5,6},{6,7},{7,8},{8,9},{9,10},{10,1... | collective-permute-start | bytes 24776 | tf_op jit(solution)/shard_map/ppermute | solution.py:19
  63.6 5.9 %collective-permute-start.7 = (bf16[16,258,1]{1,0,2:T(8,128)(2,1)S(1)}, bf16[16,258,1]{1,0,2:T(8,128)(2,1)S(1)}, u32[]{:S(2)}, u32[]{:S(2)}) collective-permute-start(bf16[16,258,1]{1,0,2:T(8,128)(2,1)S(1)} %copy.33), channel_id=1, source_target_pairs={{1,0},{2,1},{3,2},{4,3},{5,4},{6,5},{7,6},{8,7},{9,8},{10,9},{11,1... | collective-permute-start | bytes 24776 | tf_op jit(solution)/shard_map/ppermute | solution.py:21
  69.6 2.7 %fusion.14 = f32[256,256,16]{1,2,0:T(8,128)} fusion(bf16[16,256,256]{2,0,1:T(8,128)(2,1)S(1)} %maximum_convert_fusion, bf16[16,1,256]{2,0,1:T(8,128)(2,1)S(1)} %collective-permute-done.4, bf16[9,16,16]{2,1,0:T(8,128)(2,1)S(1)} %copy-done.2), kind=kOutput, calls=%fused_computation.19 | convolution fusion | flops 37748736 | bytes 6303744 | tf_op jit(solution)/shard_map/oc,crw->orw/dot_general | solution.py:65
  72.2 2.6 %fusion.4 = f32[256,256,16]{1,2,0:T(8,128)} fusion(bf16[16,1,256]{2,0,1:T(8,128)(2,1)S(1)} %collective-permute-done.5, bf16[16,256,256]{2,0,1:T(8,128)(2,1)S(1)} %maximum_convert_fusion, bf16[9,16,16]{2,1,0:T(8,128)(2,1)S(1)} %copy-done.2), kind=kOutput, calls=%fused_computation.8 | convolution fusion | flops 37748736 | bytes 6303744 | tf_op jit(solution)/shard_map/oc,crw->orw/dot_general | solution.py:65
  76.1 2.2 %copy.34 = bf16[16,258,1]{2,0,1:T(8,128)(2,1)} copy(bf16[16,258,1]{1,0,2:T(8,128)(2,1)S(1)} %collective-permute-done.7) | data formatting | bytes 16512 | tf_op jit(solution)/shard_map/ppermute | solution.py:21
  78.2 5.0 %pad_maximum_fusion = (bf16[16,258,257]{2,0,1:T(8,128)(2,1)S(1)}, bf16[16,258,257]{2,0,1:T(8,128)(2,1)S(1)}) fusion(bf16[16,258,1]{2,0,1:T(8,128)(2,1)} %copy.34, bf16[16,1,256]{2,0,1:T(8,128)(2,1)S(1)} %collective-permute-done.5, bf16[16,256,256]{2,0,1:T(8,128)(2,1)S(1)} %maximum_convert_fusion, bf16[16,1,256]{2,0,1:T(8,128)(2,1)S(1)} %collective-permute-done.4, ...), kind=kLoop, calls=%fused_computation.3 | loop fusion | flops 16974336 | bytes 6373632 | tf_op jit(solution)/shard_map/concatenate | solution.py:17
  83.3 2.6 %fusion.10 = f32[256,256,16]{1,2,0:T(8,128)} fusion(bf16[16,258,257]{2,0,1:T(8,128)(2,1)S(1)} %get-tuple-element.15, bf16[9,16,16]{2,1,0:T(8,128)(2,1)S(1)} %copy-done.2), kind=kOutput, calls=%fused_computation.14 | convolution fusion | flops 33554432 | bytes 6295552 | tf_op jit(solution)/shard_map/oc,crw->orw/dot_general | solution.py:65
  85.9 2.6 %fusion.16 = f32[256,256,16]{1,2,0:T(8,128)} fusion(bf16[16,258,257]{2,0,1:T(8,128)(2,1)S(1)} %get-tuple-element.15, bf16[9,16,16]{2,1,0:T(8,128)(2,1)S(1)} %copy-done.2), kind=kOutput, calls=%fused_computation.21 | convolution fusion | flops 33554432 | bytes 6295552 | tf_op jit(solution)/shard_map/oc,crw->orw/dot_general | solution.py:65
  88.5 2.6 %fusion.6 = f32[256,256,16]{1,2,0:T(8,128)} fusion(bf16[16,258,257]{2,0,1:T(8,128)(2,1)S(1)} %get-tuple-element.15, bf16[9,16,16]{2,1,0:T(8,128)(2,1)S(1)} %copy-done.2), kind=kOutput, calls=%fused_computation.10 | convolution fusion | flops 33554432 | bytes 6295552 | tf_op jit(solution)/shard_map/oc,crw->orw/dot_general | solution.py:65
  91.2 2.8 %fusion.12 = f32[256,256,16]{1,2,0:T(8,128)} fusion(bf16[16,258,257]{2,0,1:T(8,128)(2,1)S(1)} %get-tuple-element.14, bf16[9,16,16]{2,1,0:T(8,128)(2,1)S(1)} %copy-done.2), kind=kOutput, calls=%fused_computation.16 | convolution fusion | flops 33554432 | bytes 6295552 | tf_op jit(solution)/shard_map/oc,crw->orw/dot_general | solution.py:65
  93.9 2.8 %fusion.8 = f32[256,256,16]{1,2,0:T(8,128)} fusion(bf16[16,258,257]{2,0,1:T(8,128)(2,1)S(1)} %get-tuple-element.14, bf16[9,16,16]{2,1,0:T(8,128)(2,1)S(1)} %copy-done.2), kind=kOutput, calls=%fused_computation.12 | convolution fusion | flops 33554432 | bytes 6295552 | tf_op jit(solution)/shard_map/oc,crw->orw/dot_general | solution.py:65
  97.2 11.0 %multiply_reduce_fusion = f32[256,256]{1,0:T(8,128)S(1)} fusion(f32[256,256,16]{1,2,0:T(8,128)} %fusion.4, f32[256,256,16]{1,2,0:T(8,128)} %fusion.6, f32[256,256,16]{1,2,0:T(8,128)} %fusion.8, f32[256,256,16]{1,2,0:T(8,128)S(1)} %copy-done, f32[256,256,16]{1,2,0:T(8,128)} %fusion.10, f32[256,256,16]{1,2,0:T(8,128)} %fusion.12, f32[256,256,16]{1,2,0:T(8,128)} %fusion.16, ...), kind=kOutput, calls=%fused_computation | convolution fusion | flops 46071808 | bytes 35918848 | tf_op jit(solution)/shard_map/oc,crw->orw/dot_general | solution.py:65
  109.3 1.5 %collective-permute-start.8 = (bf16[256,256]{1,0:T(8,128)(2,1)S(1)}, bf16[256,256]{1,0:T(8,128)(2,1)S(1)}, u32[]{:S(2)}, u32[]{:S(2)}) collective-permute-start(bf16[256,256]{1,0:T(8,128)(2,1)S(1)} %add_convert_fusion), channel_id=1, source_target_pairs={{128,0},{256,128},{384,256},{129,1},{257,129},{385,257},{130,2},{2... | collective-permute-start | bytes 393224 | tf_op jit(solution)/shard_map/ppermute | solution.py:31
  112.1 4.1 %collective-permute-done.8 = bf16[256,256]{1,0:T(8,128)(2,1)S(1)} collective-permute-done((bf16[256,256]{1,0:T(8,128)(2,1)S(1)}, bf16[256,256]{1,0:T(8,128)(2,1)S(1)}, u32[]{:S(2)}, u32[]{:S(2)}) %collective-permute-start.8) | collective-permute-done | bytes 131104 | tf_op jit(solution)/shard_map/ppermute | solution.py:31
  (52 shorter events, 18.2 us)
Async XLA Ops:
  0.0 33.2 %copy-start.3 = (f32[16]{0:T(128)S(1)}, f32[16]{0:T(128)}, u32[]{:S(2)}) copy-start(f32[16]{0:T(128)} %param.8) | copy-start | bytes 196
  0.7 10.4 %collective-permute-start = (bf16[1,256]{1,0:T(2,128)(2,1)S(1)}, bf16[1,256]{1,0:T(2,128)(2,1)S(1)}, u32[]{:S(2)}, u32[]{:S(2)}) collective-permute-start(bf16[1,256]{1,0:T(2,128)(2,1)S(1)} %get-tuple-element.33), channel_id=1, source_target_pairs={{0,32},{32,64},{64,96},{1,33},{33,65},{65,97},{2,34},{34,66},{66,9... | collective-permute-start | bytes 1544 | tf_op jit(solution)/shard_map/ppermute | solution.py:19
  9.8 10.6 %collective-permute-start.1 = (bf16[1,256]{1,0:T(2,128)(2,1)S(1)}, bf16[1,256]{1,0:T(2,128)(2,1)S(1)}, u32[]{:S(2)}, u32[]{:S(2)}) collective-permute-start(bf16[1,256]{1,0:T(2,128)(2,1)S(1)} %get-tuple-element.34), channel_id=1, source_target_pairs={{32,0},{64,32},{96,64},{33,1},{65,33},{97,65},{34,2},{66,34},{98,6... | collective-permute-start | bytes 1544 | tf_op jit(solution)/shard_map/ppermute | solution.py:21
  21.5 10.1 %collective-permute-start.2 = (bf16[258,1]{1,0:T(8,128)(2,1)S(1)}, bf16[258,1]{1,0:T(8,128)(2,1)S(1)}, u32[]{:S(2)}, u32[]{:S(2)}) collective-permute-start(bf16[258,1]{1,0:T(8,128)(2,1)S(1)} %get-tuple-element.31), channel_id=1, source_target_pairs={{0,1},{1,2},{2,3},{3,4},{4,5},{5,6},{6,7},{7,8},{8,9},{9,10},{10,1... | collective-permute-start | bytes 1556 | tf_op jit(solution)/shard_map/ppermute | solution.py:19
  23.4 8.2 %collective-permute-start.3 = (bf16[258,1]{1,0:T(8,128)(2,1)S(1)}, bf16[258,1]{1,0:T(8,128)(2,1)S(1)}, u32[]{:S(2)}, u32[]{:S(2)}) collective-permute-start(bf16[258,1]{1,0:T(8,128)(2,1)S(1)} %get-tuple-element.32), channel_id=1, source_target_pairs={{1,0},{2,1},{3,2},{4,3},{5,4},{6,5},{7,6},{8,7},{9,8},{10,9},{11,1... | collective-permute-start | bytes 1556 | tf_op jit(solution)/shard_map/ppermute | solution.py:21
  32.7 15.9 %copy-start.2 = (bf16[9,16,16]{2,1,0:T(8,128)(2,1)S(1)}, bf16[9,16,16]{2,1,0:T(8,128)(2,1)}, u32[]{:S(2)}) copy-start(bf16[9,16,16]{2,1,0:T(8,128)(2,1)} %param.9) | copy-start | bytes 13828
  39.5 11.7 %collective-permute-start.4 = (bf16[16,1,256]{2,0,1:T(8,128)(2,1)S(1)}, bf16[16,1,256]{2,0,1:T(8,128)(2,1)S(1)}, u32[]{:S(2)}, u32[]{:S(2)}) collective-permute-start(bf16[16,1,256]{2,0,1:T(8,128)(2,1)S(1)} %get-tuple-element.18), channel_id=1, source_target_pairs={{0,32},{32,64},{64,96},{1,33},{33,65},{65,97},{2,34},{34,66},{66,9... | collective-permute-start | bytes 24584 | tf_op jit(solution)/shard_map/ppermute | solution.py:19
  47.3 9.5 %collective-permute-start.5 = (bf16[16,1,256]{2,0,1:T(8,128)(2,1)S(1)}, bf16[16,1,256]{2,0,1:T(8,128)(2,1)S(1)}, u32[]{:S(2)}, u32[]{:S(2)}) collective-permute-start(bf16[16,1,256]{2,0,1:T(8,128)(2,1)S(1)} %get-tuple-element.19), channel_id=1, source_target_pairs={{32,0},{64,32},{96,64},{33,1},{65,33},{97,65},{34,2},{66,34},{98,6... | collective-permute-start | bytes 24584 | tf_op jit(solution)/shard_map/ppermute | solution.py:21
  60.6 14.2 %collective-permute-start.6 = (bf16[16,258,1]{1,0,2:T(8,128)(2,1)S(1)}, bf16[16,258,1]{1,0,2:T(8,128)(2,1)S(1)}, u32[]{:S(2)}, u32[]{:S(2)}) collective-permute-start(bf16[16,258,1]{1,0,2:T(8,128)(2,1)S(1)} %copy.31), channel_id=1, source_target_pairs={{0,1},{1,2},{2,3},{3,4},{4,5},{5,6},{6,7},{7,8},{8,9},{9,10},{10,1... | collective-permute-start | bytes 24776 | tf_op jit(solution)/shard_map/ppermute | solution.py:19
  63.6 12.4 %collective-permute-start.7 = (bf16[16,258,1]{1,0,2:T(8,128)(2,1)S(1)}, bf16[16,258,1]{1,0,2:T(8,128)(2,1)S(1)}, u32[]{:S(2)}, u32[]{:S(2)}) collective-permute-start(bf16[16,258,1]{1,0,2:T(8,128)(2,1)S(1)} %copy.33), channel_id=1, source_target_pairs={{1,0},{2,1},{3,2},{4,3},{5,4},{6,5},{7,6},{8,7},{9,8},{10,9},{11,1... | collective-permute-start | bytes 24776 | tf_op jit(solution)/shard_map/ppermute | solution.py:21
  93.9 3.3 %copy-start = (f32[256,256,16]{1,2,0:T(8,128)S(1)}, f32[256,256,16]{1,2,0:T(8,128)}, u32[]{:S(2)}) copy-start(f32[256,256,16]{1,2,0:T(8,128)} %fusion.49) | copy-start | bytes 12582916
  93.9 3.3 %copy-start.4 = (f32[16]{0:T(128)S(1)}, f32[16]{0:T(128)}, u32[]{:S(2)}) copy-start(f32[16]{0:T(128)} %param.11) | copy-start | bytes 196
  93.9 3.3 %copy-start.5 = (f32[16]{0:T(128)S(1)}, f32[16]{0:T(128)}, u32[]{:S(2)}) copy-start(f32[16]{0:T(128)} %param.10) | copy-start | bytes 196
  97.2 11.0 %copy-start.1 = (bf16[1,256,256]{2,1,0:T(8,128)(2,1)S(1)}, bf16[1,256,256]{2,1,0:T(8,128)(2,1)}, u32[]{:S(2)}) copy-start(bf16[1,256,256]{2,1,0:T(8,128)(2,1)} %param.6) | copy-start | bytes 393220
  109.3 6.9 %collective-permute-start.8 = (bf16[256,256]{1,0:T(8,128)(2,1)S(1)}, bf16[256,256]{1,0:T(8,128)(2,1)S(1)}, u32[]{:S(2)}, u32[]{:S(2)}) collective-permute-start(bf16[256,256]{1,0:T(8,128)(2,1)S(1)} %add_convert_fusion), channel_id=1, source_target_pairs={{128,0},{256,128},{384,256},{129,1},{257,129},{385,257},{130,2},{2... | collective-permute-start | bytes 393224 | tf_op jit(solution)/shard_map/ppermute | solution.py:31
where the time goes:
time: 121 us
  matrix products  37.5 us (31%)
  starting transfers between devices  36.5 us (30%)
  waiting for transfers between devices  18.9 us (16%)
  other arithmetic  14.5 us (12%)
  local copies, waits for them, and re-layouts  13.1 us (11%)
    dot_general x9, matrix products, second_layer(): jnp.einsum('oc,crw->orw', kernel[tap_index], window, preferred_element_ty...  32.4 us
    ppermute x4, starting transfers between devices, with_halo(): lax.ppermute(tail, axis, [(i, (i + 1) % count) for i in range(ends)])  20.7 us
    ppermute x4, waiting for transfers between devices, with_halo(): lax.ppermute(head, axis, [((i + 1) % count, i) for i in range(ends)])  14.9 us
    ppermute x4, starting transfers between devices, with_halo(): lax.ppermute(head, axis, [((i + 1) % count, i) for i in range(ends)])  14.3 us
    convert_element_type x1, other arithmetic, first_layer(): return jax.nn.relu(summed + offsets[:, None, None]).astype(jnp.bfloat16)  6.27 us
    concatenate x3, other arithmetic, with_halo(): jnp.concatenate([lax.ppermute(tail, axis, [(i, (i + 1) % count) for i in...  6.25 us
    ppermute x1, waiting for transfers between devices, from_behind(): lax.ppermute(value, axis, [(source, source + steps) for source in range(l...  4.06 us
    slice x4, local copies, waits for them, and re-layouts, with_halo(): lax.slice_in_dim(cells, cells.shape[dim] - width, cells.shape[dim], axis=...  2.96 us
  transfers between devices with their start and end apart: 9, of which 3 were waited for; matrix products, arithmetic and copies ran while one was open for 11% of the time, Pallas kernels for 0%

commit v1 on v0

v1 whole, which is shorter than its diff:
```python
import math

import jax
import jax.numpy as jnp
import numpy as np
from jax import lax
from jax.experimental import pallas as pl
from jax.experimental.pallas import tpu as pltpu
from jax.sharding import PartitionSpec as P

PATCH = 128
TILE = 256
CH = 16
BAND = 8
BANDS = TILE // BAND
LANES = 128
K1 = 256
K2 = 512
FAR = -65536.0

F32 = jnp.float32
BF16 = jnp.bfloat16
VMEM = pltpu.MemorySpace.VMEM
SMEM = pltpu.MemorySpace.SMEM
PARAMS = pltpu.CompilerParams(vmem_limit_bytes=40 * 1024 * 1024)


def dft_tables():
    positions = np.arange(PATCH, dtype=np.int32)
    phase = positions[:, None] * positions[None, :] % PATCH
    angles = phase.astype(np.float32) * np.float32(2.0 * math.pi / PATCH)
    scaling = np.float32(1.0 / math.sqrt(PATCH))
    cosine = (np.cos(angles) * scaling).astype(BF16)
    sine = (np.sin(angles) * scaling).astype(BF16)
    across = np.concatenate([cosine, sine], axis=1)
    down = np.block([[cosine.T, -sine.T], [-sine.T, -cosine.T]]).astype(BF16)
    return across, down


def iota(shape, dim):
    return lax.broadcasted_iota(jnp.int32, shape, dim)


def dot(a, b):
    return lax.dot_general(a, b, (((1,), (0,)), ((), ())), preferred_element_type=F32)


def pieces(values):
    high = values.astype(BF16)
    rest = values - high.astype(F32)
    middle = rest.astype(BF16)
    low = (rest - middle.astype(F32)).astype(BF16)
    return high, middle, low


def column(row, spread):
    return jnp.sum(jnp.where(spread, row, 0.0), axis=1, keepdims=True)


def prepare_kernel(first_ref, first_bias_ref, second_ref, second_bias_ref, w1_ref, w2_ref):
    rows = BAND * CH
    row_r = iota((rows, K1), 0) // CH
    col = iota((rows, K1), 1)
    col_i = col % 16
    col_k = col - 240
    stacked = jnp.concatenate(pieces(first_ref[...]), axis=0)
    spread = (iota((rows, 48), 0) % CH == iota((rows, 48), 1) % CH).astype(BF16)
    sel_t = iota((9, K1), 0)
    sel_col = iota((9, K1), 1)
    sel_s = sel_col % 80 // 16
    own_piece = iota((48, K1), 0) // CH == iota((48, K1), 1) // 80
    spread_bias = iota((rows, CH), 0) % CH == iota((rows, CH), 1)
    bias = [column(p.astype(F32), spread_bias) for p in pieces(first_bias_ref[...])]
    for dw in range(3):
        total = jnp.zeros((rows, K1), F32)
        for a in range(3):
            b = sel_s - dw
            select = (sel_t == 3 * a + b) & (b >= 0) & (b <= 2) & (sel_col < 240)
            picked = dot(stacked, select.astype(F32).astype(BF16))
            picked = jnp.where(own_piece, picked, 0.0).astype(BF16)
            total = total + jnp.where(col_i - row_r == a, dot(spread, picked), 0.0)
        total = jnp.where(col >= 240, 0.0, total)
        for k in range(3):
            total = jnp.where(col_k == k, bias[k], total)
        if dw == 0:
            total = jnp.where(col_k == 3, FAR, total)
        if dw == 2:
            total = jnp.where(col_k == 4, FAR, total)
        total = jnp.where((col_k == 5) & (row_r < 7), FAR, total)
        total = jnp.where((col_k == 6) & (row_r == 7), FAR, total)
        w1_ref[dw * rows : (dw + 1) * rows, :] = total.astype(BF16)
    rows = CH * BAND
    row_r = iota((rows, K2), 0) % BAND
    col = iota((rows, K2), 1)
    col_r = col % 160 // CH
    spread = (iota((rows, CH), 0) // BAND == iota((rows, CH), 1)).astype(BF16)
    f_c = iota((CH, K2), 0)
    f_col = iota((CH, K2), 1)
    total = jnp.zeros((rows, K2), F32)
    for a in range(3):
        picked = jnp.zeros((CH, K2), F32)
        for dw in range(3):
            place = (f_col // 160 == dw) & (f_col % CH == f_c)
            picked = picked + dot(second_ref[3 * a + dw], place.astype(F32).astype(BF16))
        total = total + jnp.where(col_r - row_r == a, dot(spread, picked.astype(BF16)), 0.0)
    total = jnp.where(col >= 480, 0.0, total)
    spread_bias = iota((rows, CH), 0) // BAND == iota((rows, CH), 1)
    for k, piece in enumerate(pieces(second_bias_ref[...])):
        total = jnp.where(col == 480 + k, column(piece.astype(F32), spread_bias), total)
    w2_ref[...] = total.astype(BF16)


def shifted(left, own, right):
    wide = jnp.concatenate([left, own, right], axis=1)
    return [wide[:, LANES - 2 + s : LANES - 2 + s + TILE] for s in range(5)]


def edge_rows(flags_ref, top, bottom):
    row = iota((16, TILE), 0)
    lane = iota((16, TILE), 1)
    keep = row < 3
    keep = keep | ((row == 3) & (lane == 0) & (flags_ref[0] > 0))
    keep = keep | ((row == 4) & (lane == TILE - 1) & (flags_ref[1] > 0))
    if top:
        keep = keep | ((row == 5) & (flags_ref[2] > 0))
    if bottom:
        keep = keep | ((row == 6) & (flags_ref[3] > 0))
    return jnp.where(keep, 1.0, 0.0).astype(BF16)


def ones_rows():
    return jnp.where(iota((16, TILE), 0) < 3, 1.0, 0.0).astype(BF16)


def hidden_band(w1, shifts, last_rows):
    raw = [x.astype(BF16) for x in shifts]
    grid = jnp.concatenate(raw * 3 + [last_rows], axis=0)
    return jnp.maximum(dot(w1, grid), 0.0).astype(BF16)


def restored_band(w2, hidden, ones, head_ref, center):
    deep = dot(w2, jnp.concatenate(hidden + [ones, jnp.zeros((16, TILE), BF16)], axis=0))
    total = center
    parts = [head_ref[o] * jnp.maximum(deep[o * BAND : (o + 1) * BAND], 0.0) for o in range(CH)]
    while len(parts) > 1:
        parts = [parts[i] + parts[i + 1] for i in range(0, len(parts), 2)]
    return center + parts[0]


def inner_kernel(
    flags_ref, head_ref, left_ref, own_ref, right_ref, w1_ref, w2_ref, out_ref, raw_ref, hid_ref, res_ref
):
    band_rows = BAND * CH
    for r in range(0, TILE, 16):
        own = own_ref[r : r + 16, :].astype(F32)
        left = left_ref[r : r + 16, :].astype(F32)
        right = right_ref[r : r + 16, :].astype(F32)
        for s, x in enumerate(shifted(left, own, right)):
            raw_ref[s, r : r + 16, :] = x
    ones = ones_rows()
    last_rows = edge_rows(flags_ref, False, False)

    def first(j):
        start = pl.multiple_of((j - 1) * BAND, BAND)
        return hidden_band(
            w1_ref[...], [raw_ref[s, pl.ds(start, 16), :] for s in range(5)], last_rows
        )

    def keep(j, hidden):
        start = pl.multiple_of(j * band_rows, band_rows)
        for dw in range(3):
            hid_ref[dw, pl.ds(start, band_rows), :] = hidden[dw * band_rows : (dw + 1) * band_rows]

    def second(b):
        start = pl.multiple_of((b * BAND + 6) * CH, CH)
        hidden = [hid_ref[dw, pl.ds(start, 160), :] for dw in range(3)]
        center_start = pl.multiple_of(b * BAND, BAND)
        res_ref[pl.ds(center_start, BAND), :] = restored_band(
            w2_ref[...], hidden, ones, head_ref, raw_ref[2, pl.ds(center_start, BAND), :]
        )

    keep(1, first(1))
    keep(2, first(2))

    def body(j, carry):
        second(j - 2)
        keep(j, first(j))
        return carry

    lax.fori_loop(3, BANDS, body, 0, unroll=UNROLL)
    second(BANDS - 2)
    res_ref[0:BAND, :] = jnp.zeros((BAND, TILE), F32)
    res_ref[TILE - BAND :, :] = jnp.zeros((BAND, TILE), F32)
    out_ref[...] = res_ref[...].astype(BF16)


UNROLL = 2


def outer_kernel(
    flags_ref, head_ref, left_ref, own_ref, right_ref, above_ref, below_ref, w1_ref, w2_ref, inner_ref, out_ref
):
    band_rows = BAND * CH
    ones = ones_rows()
    out_ref[16 : TILE - 16, :] = inner_ref[16 : TILE - 16, :]
    for top in (True, False):
        if top:
            near = slice(0, 16)
            far = above_ref[...].astype(F32)[8:16]
        else:
            near = slice(TILE - 16, TILE)
            far = below_ref[...].astype(F32)[0:8]
        own = own_ref[near, :].astype(F32)
        parts = [left_ref[near, :].astype(F32), own, right_ref[near, :].astype(F32)]
        halo = [far[:, :LANES], far[:, LANES : LANES + TILE], far[:, LANES + TILE :]]
        order = (halo, parts) if top else (parts, halo)
        shifts = shifted(*[jnp.concatenate([u, v], axis=0) for u, v in zip(*order)])
        blocks = [
            hidden_band(
                w1_ref[...],
                [x[8 * k : 8 * k + 16] for x in shifts],
                edge_rows(flags_ref, top and k == 0, not top and k == 1),
            )
            for k in range(2)
        ]
        hidden = [
            jnp.concatenate([blk[dw * band_rows : (dw + 1) * band_rows] for blk in blocks], axis=0)[96:]
            for dw in range(3)
        ]
        center = own[0:8] if top else own[8:16]
        band = restored_band(w2_ref[...], hidden, ones, head_ref, center)
        inner = inner_ref[near, :].astype(F32)
        pair = [band, inner[8:16]] if top else [inner[0:8], band]
        out_ref[near, :] = jnp.concatenate(pair, axis=0).astype(BF16)


def transform(image_ref, across_ref, down_ref):
    halves = [
        dot(image_ref[:, q * PATCH : (q + 1) * PATCH], across_ref[...]).astype(BF16) for q in range(2)
    ]
    real, imag = [], []
    for a in range(2):
        rows = slice(a * PATCH, (a + 1) * PATCH)
        cos_rows = jnp.concatenate([h[rows, :PATCH] for h in halves], axis=1)
        sin_rows = jnp.concatenate([h[rows, PATCH:] for h in halves], axis=1)
        both = dot(down_ref[...], jnp.concatenate([cos_rows, sin_rows], axis=0))
        real.append(both[:PATCH])
        imag.append(both[PATCH:])
    return real, imag


def own_kernel(image_ref, across_ref, down_ref, out_ref):
    real, imag = transform(image_ref, across_ref, down_ref)
    for a in range(2):
        rows = slice(a * PATCH, (a + 1) * PATCH)
        out_ref[0, rows, :] = real[a]
        out_ref[1, rows, :] = imag[a]


def cross_kernel(image_ref, across_ref, down_ref, own_ref, out_ref):
    real, imag = transform(image_ref, across_ref, down_ref)
    for a in range(2):
        rows = slice(a * PATCH, (a + 1) * PATCH)
        own_real, own_imag = own_ref[0, rows, :], own_ref[1, rows, :]
        out_ref[0, 0, rows, :] = own_real * real[a] + own_imag * imag[a]
        out_ref[0, 1, rows, :] = own_imag * real[a] - own_real * imag[a]


def full(shape):
    return pl.BlockSpec(shape, lambda i: (0,) * len(shape), memory_space=VMEM)


def smem():
    return pl.BlockSpec(memory_space=SMEM)


LEFT = pl.BlockSpec((TILE, LANES), lambda i: (0, 1), memory_space=VMEM)
RIGHT = pl.BlockSpec((TILE, LANES), lambda i: (0, 0), memory_space=VMEM)


def call(kernel, name, out_shape, in_specs, scratch=(), flops=0):
    return pl.pallas_call(
        kernel,
        name=name,
        grid=(1,),
        out_shape=out_shape,
        in_specs=in_specs,
        out_specs=jax.tree.map(lambda o: full(o.shape), out_shape),
        scratch_shapes=list(scratch),
        compiler_params=PARAMS,
        cost_estimate=pl.CostEstimate(flops=flops, bytes_accessed=1 << 20, transcendentals=0),
    )


def prepare(first_kernel, first_bias, second_kernel, second_bias):
    return call(
        prepare_kernel,
        "weights",
        (jax.ShapeDtypeStruct((3 * BAND * CH, K1), BF16), jax.ShapeDtypeStruct((CH * BAND, K2), BF16)),
        [full((CH, 9)), full((1, CH)), full((9, CH, CH)), full((1, CH))],
        flops=1 << 28,
    )(first_kernel, first_bias[None], second_kernel, second_bias[None])


TILE_SHAPE = jax.ShapeDtypeStruct((TILE, TILE), BF16)
W_SPECS = [full((3 * BAND * CH, K1)), full((CH * BAND, K2))]


def inner(flags, head, left, own, right, w1, w2):
    return call(
        inner_kernel,
        "inner_rows",
        TILE_SHAPE,
        [smem(), smem(), LEFT, full((TILE, TILE)), RIGHT] + W_SPECS,
        scratch=[
            pltpu.VMEM((5, TILE, TILE), F32),
            pltpu.VMEM((3, (BANDS + 1) * BAND * CH, TILE), BF16),
            pltpu.VMEM((TILE, TILE), F32),
        ],
        flops=3 << 30,
    )(flags, head, left, own, right, w1, w2)


def outer(flags, head, left, own, right, above, below, w1, w2, inside):
    return call(
        outer_kernel,
        "outer_rows",
        TILE_SHAPE,
        [smem(), smem(), LEFT, full((TILE, TILE)), RIGHT]
        + [full((16, TILE + 2 * LANES))] * 2
        + W_SPECS
        + [full((TILE, TILE))],
        flops=1 << 28,
    )(flags, head, left, own, right, above, below, w1, w2, inside)


def table_specs():
    return [full((TILE, TILE)), full((PATCH, 2 * PATCH)), full((2 * PATCH, 2 * PATCH))]


def own_spectrum(image, across, down):
    return call(
        own_kernel,
        "own_spectrum",
        jax.ShapeDtypeStruct((2, TILE, TILE), F32),
        table_specs(),
        flops=1 << 29,
    )(image, across, down)


def cross_spectrum(image, across, down, own):
    return call(
        cross_kernel,
        "cross_spectrum",
        jax.ShapeDtypeStruct((1, 2, TILE, TILE), F32),
        table_specs() + [full((2, TILE, TILE))],
        flops=1 << 29,
    )(image, across, down, own)


def from_step(value, axis, step):
    count = lax.axis_size(axis)
    pairs = [(i, i + step) for i in range(count) if 0 <= i + step < count]
    return lax.ppermute(value, axis, pairs)


def on_device(section, first_kernel, first_bias, second_kernel, second_bias, head_weight):
    own = section[0]
    gx, gy = lax.axis_index("gx"), lax.axis_index("gy")
    ends = [gx == 0, gx == lax.axis_size("gx") - 1, gy == 0, gy == lax.axis_size("gy") - 1]
    flags = jnp.stack(ends).astype(jnp.int32)
    left = from_step(own, "gx", 1)
    right = from_step(own, "gx", -1)
    w1, w2 = prepare(first_kernel, first_bias, second_kernel, second_bias)

    def slab(rows):
        return jnp.concatenate([left[rows, LANES:], own[rows], right[rows, :LANES]], axis=1)

    above = from_step(slab(slice(TILE - 16, TILE)), "gy", 1)
    below = from_step(slab(slice(0, 16)), "gy", -1)
    inside = inner(flags, head_weight, left, own, right, w1, w2)
    restored = outer(flags, head_weight, left, own, right, above, below, w1, w2, inside)
    across, down = dft_tables()
    later = from_step(restored, "gz", -1)
    spectrum = own_spectrum(restored, across, down)
    return cross_spectrum(later, across, down, spectrum)


def solution(mesh):
    placed = (P("gz", "gy", "gx"), P(), P(), P(), P(), P())
    return jax.shard_map(
        on_device, mesh=mesh, in_specs=placed, out_specs=P("gz", None, "gy", "gx"), check_vma=False
    )
```

time: 121 us -> 42.9 us (0.35)
  the two profiles are of different devices: /device:TPU:16 before, /device:TPU:152 now
where the time goes in v1:
time: 42.9 us; the launch traced here: 42.5 us
  starting transfers between devices  18.6 us (43%)
  Pallas kernels  12.7 us (30%)
  waiting for transfers between devices  8.91 us (21%)
  local copies, waits for them, and re-layouts  2.08 us (5%)
    ppermute x5, starting transfers between devices, from_step(): return lax.ppermute(value, axis, pairs)  18.6 us
    ppermute x5, waiting for transfers between devices, from_step(): return lax.ppermute(value, axis, pairs)  8.91 us
    pallas_call x1, Pallas kernels, inner(): call(inner_kernel, 'inner_rows', TILE_SHAPE, [smem(), smem(), LEFT, full(...  8.25 us
    pallas_call x1, Pallas kernels, outer(): call(outer_kernel, 'outer_rows', TILE_SHAPE, [smem(), smem(), LEFT, full(...  1.42 us
    pallas_call x1, Pallas kernels, prepare(): call(prepare_kernel, 'weights', (jax.ShapeDtypeStruct((3 * BAND * CH, K1)...  1.38 us
    unnamed x16, local copies, waits for them, and re-layouts  1.36 us
    pallas_call x1, Pallas kernels, cross_spectrum(): call(cross_kernel, 'cross_spectrum', jax.ShapeDtypeStruct((1, 2, TILE, TI...  1.21 us
  transfers between devices with their start and end apart: 5, of which 2 were waited for; matrix products, arithmetic and copies ran while one was open for 2% of the time, Pallas kernels for 24%

profile of v1, /device:TPU:152, one launch (start us, length us, event | category | flops | bytes accessed | tf_op | source)
XLA Modules:
  0.0 42.5 jit_solution(14566829769212760185)
XLA Ops:
  0.0 4.4 %collective-permute-start.1 = (bf16[256,256]{1,0:T(8,128)(2,1)}, bf16[256,256]{1,0:T(8,128)(2,1)S(1)}, u32[]{:S(2)}, u32[]{:S(2)}) collective-permute-start(bf16[256,256]{1,0:T(8,128)(2,1)} %bitcast.11), channel_id=1, source_target_pairs={{1,0},{2,1},{3,2},{4,3},{5,4},{6,5},{7,6},{8,7},{9,8},{10,9},{11,1... | collective-permute-start | bytes 393224 | tf_op jit(solution)/shard_map/ppermute | solution.py:364
  4.4 1.9 %collective-permute-start = (bf16[256,256]{1,0:T(8,128)(2,1)}, bf16[256,256]{1,0:T(8,128)(2,1)S(1)}, u32[]{:S(2)}, u32[]{:S(2)}) collective-permute-start(bf16[256,256]{1,0:T(8,128)(2,1)} %bitcast.12), channel_id=1, source_target_pairs={{0,1},{1,2},{2,3},{3,4},{4,5},{5,6},{6,7},{7,8},{8,9},{9,10},{10,1... | collective-permute-start | bytes 393224 | tf_op jit(solution)/shard_map/ppermute | solution.py:364
  6.4 0.7 %slice_bitcast_fusion = (bf16[16,256]{1,0:T(8,128)(2,1)S(1)}, bf16[16,256]{1,0:T(8,128)(2,1)S(1)}) fusion(bf16[1,256,256]{2,1,0:T(8,128)(2,1)} %param.8), kind=kLoop, calls=%fused_computation.2 | loop fusion | bytes 32768 | tf_op jit(solution)/shard_map/slice | solution.py:377
  7.1 0.7 %copy-done.3 = f32[16,9]{1,0:T(8,128)S(1)} copy-done((f32[16,9]{1,0:T(8,128)S(1)}, f32[16,9]{1,0:T(8,128)}, u32[]{:S(2)}) %copy-start.3) | copy-done | bytes 600
  7.8 0.0 copy-done.4
  7.8 1.4 %weights.1 = (bf16[384,256]{1,0:T(8,128)(2,1)S(1)}, bf16[128,512]{1,0:T(8,128)(2,1)S(1)}) custom-call(f32[16,9]{1,0:T(8,128)S(1)} %copy-done.3, f32[1,16]{1,0:T(1,128)S(1)} %bitcast.15, bf16[9,16,16]{2,1,0:T(8,128)(2,1)S(1)} %copy-done.2, f32[1,16]{1,0:T(1,128)S(1)} %bitcast.16), custom_call_target="tpu_custom_call" | custom-call | flops 268435456 | bytes 1048576 | tf_op jit(solution)/shard_map/weights/pallas_call | solution.py:296
  9.2 0.1 add_convert_fusion.flags_ref
  9.2 0.0 collective-permute-done.1.right_ref
  9.3 3.8 %collective-permute-done.left_ref = bf16[256,256]{1,0:T(8,128)(2,1)S(1)} collective-permute-done((bf16[256,256]{1,0:T(8,128)(2,1)}, bf16[256,256]{1,0:T(8,128)(2,1)S(1)}, u32[]{:S(2)}, u32[]{:S(2)}) %collective-permute-start) | collective-permute-done | bytes 131104 | tf_op jit(solution)/shard_map/ppermute | solution.py:364
  13.0 9.1 %collective-permute-start.2 = (bf16[16,512]{1,0:T(8,128)(2,1)S(1)}, bf16[16,512]{1,0:T(8,128)(2,1)S(1)}, u32[]{:S(2)}, u32[]{:S(2)}) collective-permute-start(bf16[16,512]{1,0:T(8,128)(2,1)S(1)} %pad_maximum_fusion), channel_id=1, source_target_pairs={{0,32},{32,64},{64,96},{1,33},{33,65},{65,97},{2,34},{34,66},{66,9... | collective-permute-start | bytes 49160 | tf_op jit(solution)/shard_map/ppermute | solution.py:364
  22.1 1.9 %collective-permute-start.3 = (bf16[16,512]{1,0:T(8,128)(2,1)S(1)}, bf16[16,512]{1,0:T(8,128)(2,1)S(1)}, u32[]{:S(2)}, u32[]{:S(2)}) collective-permute-start(bf16[16,512]{1,0:T(8,128)(2,1)S(1)} %pad_maximum_fusion.1), channel_id=1, source_target_pairs={{32,0},{64,32},{96,64},{33,1},{65,33},{97,65},{34,2},{66,34},{98,6... | collective-permute-start | bytes 49160 | tf_op jit(solution)/shard_map/ppermute | solution.py:364
  24.1 0.0 copy-start.1
  24.1 0.6 %copy-done.1 = f32[16]{0:T(128)S(1)} copy-done((f32[16]{0:T(128)S(1)}, f32[16]{0:T(128)}, u32[]{:S(2)}) %copy-start.1) | copy-done | bytes 88
  24.7 8.2 %inner_rows.1.inner_ref = bf16[256,256]{1,0:T(8,128)(2,1)S(1)} custom-call(s32[4]{0:T(128)S(1)} %add_convert_fusion.flags_ref, f32[16]{0:T(128)S(1)} %copy-done.1, bf16[256,256]{1,0:T(8,128)(2,1)S(1)} %collective-permute-done.left_ref, bf16[256,256]{1,0:T(8,128)(2,1)S(1)} %bitcast.13, bf16[256,256]{1,0:T(8,128)(2,1)S(1)} %collective-permute-done.1.right_ref, ...), custom_call_target="tpu_custom_call" | custom-call | flops 3221225472 | bytes 1048576 | tf_op jit(solution)/shard_map/inner_rows/pallas_call | solution.py:310
  33.0 0.0 copy-start.6
  33.0 0.0 copy-start.7
  33.0 0.0 collective-permute-done.2.above_ref
  33.0 0.0 collective-permute-done.3.below_ref
  33.0 1.4 %outer_rows.1.image_ref = bf16[256,256]{1,0:T(8,128)(2,1)S(1)} custom-call(s32[4]{0:T(128)S(1)} %add_convert_fusion.flags_ref, f32[16]{0:T(128)S(1)} %copy-done.1, bf16[256,256]{1,0:T(8,128)(2,1)S(1)} %collective-permute-done.left_ref, bf16[256,256]{1,0:T(8,128)(2,1)S(1)} %bitcast.14, bf16[256,256]{1,0:T(8,128)(2,1)S(1)} %collective-permute-done.1.right_ref, ...), custom_call_target="tpu_custom_call" | custom-call | flops 268435456 | bytes 1048576 | tf_op jit(solution)/shard_map/outer_rows/pallas_call | solution.py:325
  34.5 1.3 %collective-permute-start.4 = (bf16[256,256]{1,0:T(8,128)(2,1)S(1)}, bf16[256,256]{1,0:T(8,128)(2,1)S(1)}, u32[]{:S(2)}, u32[]{:S(2)}) collective-permute-start(bf16[256,256]{1,0:T(8,128)(2,1)S(1)} %outer_rows.1.image_ref), channel_id=1, source_target_pairs={{128,0},{256,128},{384,256},{129,1},{257,129},{385,257},{130,2},{2... | collective-permute-start | bytes 393224 | tf_op jit(solution)/shard_map/ppermute | solution.py:364
  35.8 0.0 copy-done.6
  35.8 0.4 own_spectrum.1.own_ref
  36.2 5.1 %collective-permute-done.4.image_ref = bf16[256,256]{1,0:T(8,128)(2,1)S(1)} collective-permute-done((bf16[256,256]{1,0:T(8,128)(2,1)S(1)}, bf16[256,256]{1,0:T(8,128)(2,1)S(1)}, u32[]{:S(2)}, u32[]{:S(2)}) %collective-permute-start.4) | collective-permute-done | bytes 131104 | tf_op jit(solution)/shard_map/ppermute | solution.py:364
  41.3 1.2 %cross_spectrum.1 = f32[1,2,256,256]{3,2,1,0:T(8,128)} custom-call(bf16[256,256]{1,0:T(8,128)(2,1)S(1)} %collective-permute-done.4.image_ref, bf16[128,256]{1,0:T(8,128)(2,1)S(1)} %copy-done.7, bf16[256,256]{1,0:T(8,128)(2,1)S(1)} %copy-done.6, f32[2,256,256]{2,1,0:T(8,128)S(1)} %own_spectrum.1.own_ref), custom_call_target="tpu_custom_call" | custom-call | flops 536870912 | bytes 1048576 | tf_op jit(solution)/shard_map/cross_spectrum/pallas_call | solution.py:352
  (13 shorter events, 0.0 us)
Async XLA Ops:
  0.0 7.1 %copy-start.2 = (bf16[9,16,16]{2,1,0:T(8,128)(2,1)S(1)}, bf16[9,16,16]{2,1,0:T(8,128)(2,1)}, u32[]{:S(2)}) copy-start(bf16[9,16,16]{2,1,0:T(8,128)(2,1)} %second_ref.1) | copy-start | bytes 13828
  0.0 9.2 %collective-permute-start.1 = (bf16[256,256]{1,0:T(8,128)(2,1)}, bf16[256,256]{1,0:T(8,128)(2,1)S(1)}, u32[]{:S(2)}, u32[]{:S(2)}) collective-permute-start(bf16[256,256]{1,0:T(8,128)(2,1)} %bitcast.11), channel_id=1, source_target_pairs={{1,0},{2,1},{3,2},{4,3},{5,4},{6,5},{7,6},{8,7},{9,8},{10,9},{11,1... | collective-permute-start | bytes 393224 | tf_op jit(solution)/shard_map/ppermute | solution.py:364
  4.4 8.6 %collective-permute-start = (bf16[256,256]{1,0:T(8,128)(2,1)}, bf16[256,256]{1,0:T(8,128)(2,1)S(1)}, u32[]{:S(2)}, u32[]{:S(2)}) collective-permute-start(bf16[256,256]{1,0:T(8,128)(2,1)} %bitcast.12), channel_id=1, source_target_pairs={{0,1},{1,2},{2,3},{3,4},{4,5},{5,6},{6,7},{7,8},{8,9},{9,10},{10,1... | collective-permute-start | bytes 393224 | tf_op jit(solution)/shard_map/ppermute | solution.py:364
  7.1 0.7 %copy-start.3 = (f32[16,9]{1,0:T(8,128)S(1)}, f32[16,9]{1,0:T(8,128)}, u32[]{:S(2)}) copy-start(f32[16,9]{1,0:T(8,128)} %first_ref.1) | copy-start | bytes 1732
  7.1 0.7 %copy-start.4 = (f32[16]{0:T(128)S(1)}, f32[16]{0:T(128)}, u32[]{:S(2)}) copy-start(f32[16]{0:T(128)} %param.10) | copy-start | bytes 196
  7.1 0.7 %copy-start.5 = (f32[16]{0:T(128)S(1)}, f32[16]{0:T(128)}, u32[]{:S(2)}) copy-start(f32[16]{0:T(128)} %param.12) | copy-start | bytes 196
  7.8 16.3 %copy-start = (bf16[1,256,256]{2,1,0:T(8,128)(2,1)S(1)}, bf16[1,256,256]{2,1,0:T(8,128)(2,1)}, u32[]{:S(2)}) copy-start(bf16[1,256,256]{2,1,0:T(8,128)(2,1)} %param.8) | copy-start | bytes 393220
  13.0 20.0 %collective-permute-start.2 = (bf16[16,512]{1,0:T(8,128)(2,1)S(1)}, bf16[16,512]{1,0:T(8,128)(2,1)S(1)}, u32[]{:S(2)}, u32[]{:S(2)}) collective-permute-start(bf16[16,512]{1,0:T(8,128)(2,1)S(1)} %pad_maximum_fusion), channel_id=1, source_target_pairs={{0,32},{32,64},{64,96},{1,33},{33,65},{65,97},{2,34},{34,66},{66,9... | collective-permute-start | bytes 49160 | tf_op jit(solution)/shard_map/ppermute | solution.py:364
  22.1 10.9 %collective-permute-start.3 = (bf16[16,512]{1,0:T(8,128)(2,1)S(1)}, bf16[16,512]{1,0:T(8,128)(2,1)S(1)}, u32[]{:S(2)}, u32[]{:S(2)}) collective-permute-start(bf16[16,512]{1,0:T(8,128)(2,1)S(1)} %pad_maximum_fusion.1), channel_id=1, source_target_pairs={{32,0},{64,32},{96,64},{33,1},{65,33},{97,65},{34,2},{66,34},{98,6... | collective-permute-start | bytes 49160 | tf_op jit(solution)/shard_map/ppermute | solution.py:364
  24.1 0.7 %copy-start.1 = (f32[16]{0:T(128)S(1)}, f32[16]{0:T(128)}, u32[]{:S(2)}) copy-start(f32[16]{0:T(128)} %head_ref.3) | copy-start | bytes 196
  33.0 2.8 %copy-start.6 = (bf16[256,256]{1,0:T(8,128)(2,1)S(1)}, bf16[256,256]{1,0:T(8,128)(2,1)}, u32[]{:S(2)}) copy-start(bf16[256,256]{1,0:T(8,128)(2,1)} %constant.20.clone.down_ref) | copy-start | bytes 393220
  33.0 2.8 %copy-start.7 = (bf16[128,256]{1,0:T(8,128)(2,1)S(1)}, bf16[128,256]{1,0:T(8,128)(2,1)}, u32[]{:S(2)}) copy-start(bf16[128,256]{1,0:T(8,128)(2,1)} %constant.19.clone.across_ref) | copy-start | bytes 196612
  34.5 6.9 %collective-permute-start.4 = (bf16[256,256]{1,0:T(8,128)(2,1)S(1)}, bf16[256,256]{1,0:T(8,128)(2,1)S(1)}, u32[]{:S(2)}, u32[]{:S(2)}) collective-permute-start(bf16[256,256]{1,0:T(8,128)(2,1)S(1)} %outer_rows.1.image_ref), channel_id=1, source_target_pairs={{128,0},{256,128},{384,256},{129,1},{257,129},{385,257},{130,2},{2... | collective-permute-start | bytes 393224 | tf_op jit(solution)/shard_map/ppermute | solution.py:364

commit v2 on v1

v2 whole, which is shorter than its diff:
```python
import math

import jax
import jax.numpy as jnp
import numpy as np
from jax import lax
from jax.experimental import pallas as pl
from jax.experimental.pallas import tpu as pltpu
from jax.sharding import PartitionSpec as P

PATCH = 128
TILE = 256
CH = 16
BAND = 8
BANDS = TILE // BAND
LANES = 128
K1 = 256
K2 = 512
FAR = -65536.0

F32 = jnp.float32
BF16 = jnp.bfloat16
VMEM = pltpu.MemorySpace.VMEM
SMEM = pltpu.MemorySpace.SMEM
PARAMS = pltpu.CompilerParams(vmem_limit_bytes=40 * 1024 * 1024)


def dft_tables():
    positions = np.arange(PATCH, dtype=np.int32)
    phase = positions[:, None] * positions[None, :] % PATCH
    angles = phase.astype(np.float32) * np.float32(2.0 * math.pi / PATCH)
    scaling = np.float32(1.0 / math.sqrt(PATCH))
    cosine = (np.cos(angles) * scaling).astype(BF16)
    sine = (np.sin(angles) * scaling).astype(BF16)
    across = np.concatenate([cosine, sine], axis=1)
    down = np.block([[cosine.T, -sine.T], [-sine.T, -cosine.T]]).astype(BF16)
    return across, down


def iota(shape, dim):
    return lax.broadcasted_iota(jnp.int32, shape, dim)


def dot(a, b):
    return lax.dot_general(a, b, (((1,), (0,)), ((), ())), preferred_element_type=F32)


def pieces(values):
    high = values.astype(BF16)
    rest = values - high.astype(F32)
    middle = rest.astype(BF16)
    low = (rest - middle.astype(F32)).astype(BF16)
    return high, middle, low


def column(row, spread):
    return jnp.sum(jnp.where(spread, row, 0.0), axis=1, keepdims=True)


def end_of(axis, last):
    return lax.axis_index(axis) == (lax.axis_size(axis) - 1 if last else 0)


def first_weights_kernel(first_ref, bias_ref, w1_ref, rows_out):
    rows = BAND * CH
    row_r = iota((rows, K1), 0) // CH
    col = iota((rows, K1), 1)
    col_i = col % 16
    stacked = jnp.concatenate(pieces(first_ref[...]), axis=0)
    spread = (iota((rows, 48), 0) % CH == iota((rows, 48), 1) % CH).astype(F32).astype(BF16)
    sel_t = iota((9, K1), 0)
    sel_col = iota((9, K1), 1)
    sel_b = sel_col % 80 // 16
    in_grid = (sel_b <= 2) & (sel_col < 240)
    own_piece = iota((48, K1), 0) // CH == iota((48, K1), 1) // 80
    base = jnp.zeros((rows, K1), F32)
    for a in range(3):
        select = (sel_t == 3 * a + sel_b) & in_grid
        picked = dot(stacked, select.astype(F32).astype(BF16))
        picked = jnp.where(own_piece, picked, 0.0).astype(BF16)
        base = base + jnp.where(col_i - row_r == a, dot(spread, picked), 0.0)
    spread_bias = iota((rows, CH), 0) % CH == iota((rows, CH), 1)
    tail = jnp.zeros((rows, K1), F32)
    for k, piece in enumerate(pieces(bias_ref[...])):
        tail = jnp.where(col == 240 + k, column(piece.astype(F32), spread_bias), tail)
    tail = jnp.where((col == 245) & (row_r < 7), FAR, tail)
    tail = jnp.where((col == 246) & (row_r == 7), FAR, tail)
    for dw in range(3):
        total = jnp.where(col < 240, pltpu.roll(base, 16 * dw, 1) if dw else base, tail)
        if dw == 0:
            total = jnp.where(col == 243, FAR, total)
        if dw == 2:
            total = jnp.where(col == 244, FAR, total)
        w1_ref[dw * rows : (dw + 1) * rows, :] = total.astype(BF16)
    row = iota((16, TILE), 0)
    lane = iota((16, TILE), 1)
    keep = row < 3
    keep = keep | ((row == 3) & (lane == 0) & end_of("gx", False))
    keep = keep | ((row == 4) & (lane == TILE - 1) & end_of("gx", True))
    top = keep | ((row == 5) & end_of("gy", False))
    bottom = keep | ((row == 6) & end_of("gy", True))
    for k, mask in enumerate((keep, top, bottom)):
        rows_out[16 * k : 16 * k + 16, :] = jnp.where(mask, 1.0, 0.0).astype(BF16)


def second_weights_kernel(second_ref, bias_ref, head_ref, w2_ref, head_out):
    rows = CH * BAND
    row_r = iota((rows, K2), 0) % BAND
    col = iota((rows, K2), 1)
    col_r = col % 160 // CH
    spread = (iota((rows, CH), 0) // BAND == iota((rows, CH), 1)).astype(F32).astype(BF16)
    f_c = iota((CH, K2), 0)
    f_col = iota((CH, K2), 1)
    second = second_ref[...].reshape(9 * CH, CH)
    by_dw = [
        dot(second, ((f_col // 160 == dw) & (f_col % CH == f_c)).astype(F32).astype(BF16)) for dw in range(3)
    ]
    total = jnp.zeros((rows, K2), F32)
    for a in range(3):
        picked = sum(by_dw[dw][(3 * a + dw) * CH : (3 * a + dw + 1) * CH] for dw in range(3))
        total = total + jnp.where(col_r - row_r == a, dot(spread, picked.astype(BF16)), 0.0)
    total = jnp.where(col >= 480, 0.0, total)
    spread_bias = iota((rows, CH), 0) // BAND == iota((rows, CH), 1)
    for k, piece in enumerate(pieces(bias_ref[...])):
        total = jnp.where(col == 480 + k, column(piece.astype(F32), spread_bias), total)
    w2_ref[...] = total.astype(BF16)
    head_out[...] = jnp.broadcast_to(column(head_ref[...], spread_bias), (rows, LANES))


def sides_kernel(own_ref, core_ref, chip_ref, sides_ref, head_ref, tail_ref):
    odd = lax.axis_index("gx") % 2 == 1
    for r in range(0, TILE, 16):
        core, chip, own = core_ref[r : r + 16, :], chip_ref[r : r + 16, :], own_ref[r : r + 16, :]
        left = jnp.where(odd, core[:, LANES:], chip[:, LANES:])
        right = jnp.where(odd, chip[:, :LANES], core[:, :LANES])
        sides_ref[r : r + 16, :] = jnp.concatenate([left, right], axis=1)
        if r == 0:
            head_ref[...] = jnp.concatenate([left, own, right], axis=1)
        if r == TILE - 16:
            tail_ref[...] = jnp.concatenate([left, own, right], axis=1)


def shifted(left, own, right):
    wide = jnp.concatenate([left, own, right], axis=1)
    return [wide[:, LANES - 2 + s : LANES - 2 + s + TILE] for s in range(5)]


def ones_rows():
    return jnp.where(iota((16, TILE), 0) < 3, 1.0, 0.0).astype(BF16)


def hidden_band(w1, shifts, last_rows):
    raw = [x.astype(BF16) for x in shifts]
    grid = jnp.concatenate(raw * 3 + [last_rows], axis=0)
    return jnp.maximum(dot(w1, grid), 0.0).astype(BF16)


def restored_band(w2, hidden, ones, head, center):
    deep = dot(w2, jnp.concatenate(hidden + [ones, jnp.zeros((16, TILE), BF16)], axis=0))
    deep = jnp.maximum(deep, 0.0) * jnp.concatenate([head, head], axis=1)
    parts = [deep[o * BAND : (o + 1) * BAND] for o in range(CH)]
    while len(parts) > 1:
        parts = [parts[i] + parts[i + 1] for i in range(0, len(parts), 2)]
    return center + parts[0]


def inner_kernel(
    own_ref, sides_ref, w1_ref, w2_ref, head_ref, rows_ref, out_ref, raw_ref, hid_ref, res_ref
):
    band_rows = BAND * CH
    for r in range(0, TILE, 16):
        own = own_ref[r : r + 16, :].astype(F32)
        left = sides_ref[r : r + 16, :LANES].astype(F32)
        right = sides_ref[r : r + 16, LANES:].astype(F32)
        for s, x in enumerate(shifted(left, own, right)):
            raw_ref[s, r : r + 16, :] = x
    ones = ones_rows()
    last_rows = rows_ref[0:16, :]

    def first(j):
        start = pl.multiple_of((j - 1) * BAND, BAND)
        return hidden_band(
            w1_ref[...], [raw_ref[s, pl.ds(start, 16), :] for s in range(5)], last_rows
        )

    def keep(j, hidden):
        start = pl.multiple_of(j * band_rows, band_rows)
        for dw in range(3):
            hid_ref[dw, pl.ds(start, band_rows), :] = hidden[dw * band_rows : (dw + 1) * band_rows]

    def second(b):
        start = pl.multiple_of((b * BAND + 6) * CH, CH)
        hidden = [hid_ref[dw, pl.ds(start, 160), :] for dw in range(3)]
        center_start = pl.multiple_of(b * BAND, BAND)
        res_ref[pl.ds(center_start, BAND), :] = restored_band(
            w2_ref[...], hidden, ones, head_ref[...], raw_ref[2, pl.ds(center_start, BAND), :]
        )

    def body1(j, carry):
        keep(j, first(j))
        return carry

    def body2(b, carry):
        second(b)
        return carry

    lax.fori_loop(1, BANDS, body1, 0, unroll=UNROLL)
    lax.fori_loop(1, BANDS - 1, body2, 0, unroll=UNROLL2)
    res_ref[0:BAND, :] = jnp.zeros((BAND, TILE), F32)
    res_ref[TILE - BAND :, :] = jnp.zeros((BAND, TILE), F32)
    out_ref[...] = res_ref[...].astype(BF16)


UNROLL = 31
UNROLL2 = 30


def outer_kernel(
    own_ref, sides_ref, below_ref, above_ref, w1_ref, w2_ref, head_ref, rows_ref, inner_ref, out_ref
):
    band_rows = BAND * CH
    ones = ones_rows()
    out_ref[16 : TILE - 16, :] = inner_ref[16 : TILE - 16, :]
    for top in (True, False):
        if top:
            near = slice(0, 16)
            far = above_ref[...].astype(F32)[8:16]
        else:
            near = slice(TILE - 16, TILE)
            far = below_ref[...].astype(F32)[0:8]
        own = own_ref[near, :].astype(F32)
        parts = [sides_ref[near, :LANES].astype(F32), own, sides_ref[near, LANES:].astype(F32)]
        halo = [far[:, :LANES], far[:, LANES : LANES + TILE], far[:, LANES + TILE :]]
        order = (halo, parts) if top else (parts, halo)
        shifts = shifted(*[jnp.concatenate([u, v], axis=0) for u, v in zip(*order)])
        blocks = []
        for k in range(2):
            kind = 1 if top and k == 0 else 2 if k == 1 and not top else 0
            last_rows = rows_ref[16 * kind : 16 * kind + 16, :]
            blocks.append(hidden_band(w1_ref[...], [x[8 * k : 8 * k + 16] for x in shifts], last_rows))
        hidden = [
            jnp.concatenate([blk[dw * band_rows : (dw + 1) * band_rows] for blk in blocks], axis=0)[96:]
            for dw in range(3)
        ]
        center = own[0:8] if top else own[8:16]
        band = restored_band(w2_ref[...], hidden, ones, head_ref[...], center)
        inner = inner_ref[near, :].astype(F32)
        pair = [band, inner[8:16]] if top else [inner[0:8], band]
        out_ref[near, :] = jnp.concatenate(pair, axis=0).astype(BF16)


def transform(image_ref, across_ref, down_ref):
    halves = [
        dot(image_ref[:, q * PATCH : (q + 1) * PATCH], across_ref[...]).astype(BF16) for q in range(2)
    ]
    results = []
    for a in range(2):
        rows = slice(a * PATCH, (a + 1) * PATCH)
        cos_rows = jnp.concatenate([h[rows, :PATCH] for h in halves], axis=1)
        sin_rows = jnp.concatenate([h[rows, PATCH:] for h in halves], axis=1)
        both = dot(down_ref[...], jnp.concatenate([cos_rows, sin_rows], axis=0))
        results.append((both[:PATCH], both[PATCH:]))
    return results


def own_kernel(image_ref, across_ref, down_ref, out_ref):
    for a, (real, imag) in enumerate(transform(image_ref, across_ref, down_ref)):
        rows = slice(a * PATCH, (a + 1) * PATCH)
        out_ref[0, rows, :] = real
        out_ref[1, rows, :] = imag


def cross_kernel(image_ref, across_ref, down_ref, own_ref, out_ref, held_ref, sems):
    copies = []
    for a, (real, imag) in enumerate(transform(image_ref, across_ref, down_ref)):
        rows = slice(a * PATCH, (a + 1) * PATCH)
        own_real, own_imag = own_ref[0, rows, :], own_ref[1, rows, :]
        for part, value in enumerate(
            (own_real * real + own_imag * imag, own_imag * real - own_real * imag)
        ):
            held_ref[part, rows, :] = value
            copies.append(
                pltpu.make_async_copy(held_ref.at[part, rows], out_ref.at[0, part, rows], sems.at[a, part])
            )
            copies[-1].start()
    for copy in copies:
        copy.wait()


def full(shape):
    return pl.BlockSpec(shape, lambda: (0,) * len(shape), memory_space=VMEM)


def call(kernel, name, out_shape, args, scratch=(), flops=0, in_specs=None, out_specs=None):
    return pl.pallas_call(
        kernel,
        name=name,
        out_shape=out_shape,
        in_specs=in_specs or [full(a.shape) for a in args],
        out_specs=out_specs or jax.tree.map(lambda o: full(o.shape), out_shape),
        scratch_shapes=list(scratch),
        compiler_params=PARAMS,
        cost_estimate=pl.CostEstimate(flops=flops, bytes_accessed=1 << 20, transcendentals=0),
    )(*args)


def shaped(*shape, dtype=BF16):
    return jax.ShapeDtypeStruct(shape, dtype)


def prepare(first_kernel, first_bias, second_kernel, second_bias, head):
    w2, head = call(
        second_weights_kernel,
        "second_weights",
        (shaped(CH * BAND, K2), shaped(CH * BAND, LANES, dtype=F32)),
        (second_kernel, second_bias[None], head[None]),
        flops=1 << 31,
    )
    w1, rows = call(
        first_weights_kernel,
        "first_weights",
        (shaped(3 * BAND * CH, K1), shaped(48, TILE)),
        (first_kernel, first_bias[None]),
        flops=1 << 31,
    )
    return w1, w2, head, rows


def sides(own, core, chip):
    slab = shaped(16, TILE + 2 * LANES)
    return call(sides_kernel, "sides", (shaped(TILE, TILE), slab, slab), (own, core, chip), flops=1 << 26)


def inner(own, side, weights):
    return call(
        inner_kernel,
        "inner_rows",
        shaped(TILE, TILE),
        (own, side, *weights),
        scratch=[
            pltpu.VMEM((5, TILE, TILE), F32),
            pltpu.VMEM((3, (BANDS + 1) * BAND * CH, TILE), BF16),
            pltpu.VMEM((TILE, TILE), F32),
        ],
        flops=3 << 30,
    )


def outer(own, side, above, below, weights, inside):
    return call(
        outer_kernel,
        "outer_rows",
        shaped(TILE, TILE),
        (own, side, below, above, *weights, inside),
        flops=1 << 28,
    )


def own_spectrum(image, across, down):
    return call(
        own_kernel, "own_spectrum", shaped(2, TILE, TILE, dtype=F32), (image, across, down), flops=1 << 29
    )


def cross_spectrum(image, across, down, own):
    return call(
        cross_kernel,
        "cross_spectrum",
        shaped(1, 2, TILE, TILE, dtype=F32),
        (image, across, down, own),
        scratch=[pltpu.VMEM((2, TILE, TILE), F32), pltpu.SemaphoreType.DMA((2, 2))],
        flops=1 << 29,
        out_specs=pl.BlockSpec(memory_space=pl.ANY),
    )


def from_step(value, axis, step):
    count = lax.axis_size(axis)
    pairs = [(i, i + step) for i in range(count) if 0 <= i + step < count]
    return lax.ppermute(value, axis, pairs)


def swap(value, axis, offset):
    count = lax.axis_size(axis)
    pairs = [(i, i + 1) for i in range(offset, count - 1, 2)]
    return lax.ppermute(value, axis, pairs + [(j, i) for i, j in pairs])


def on_device(section, first_kernel, first_bias, second_kernel, second_bias, head_weight):
    own = section[0]
    chip = swap(own, "gx", 1)
    core = swap(own, "gx", 0)
    weights = prepare(first_kernel, first_bias, second_kernel, second_bias, head_weight)
    side, head, tail = sides(own, core, chip)
    below = from_step(head, "gy", -1)
    above = from_step(tail, "gy", 1)
    inside = inner(own, side, weights)
    restored = outer(own, side, above, below, weights, inside)
    across, down = dft_tables()
    later = from_step(restored, "gz", -1)
    spectrum = own_spectrum(restored, across, down)
    return cross_spectrum(later, across, down, spectrum)


def solution(mesh):
    placed = (P("gz", "gy", "gx"), P(), P(), P(), P(), P())
    return jax.shard_map(
        on_device, mesh=mesh, in_specs=placed, out_specs=P("gz", None, "gy", "gx"), check_vma=False
    )
```

time: 42.9 us -> 33.7 us (0.79)
  the two profiles are of different devices: /device:TPU:152 before, /device:TPU:472 now
where the time goes in v2:
time: 33.7 us; the launch traced here: 33.4 us
  starting transfers between devices  15.8 us (47%)
  waiting for transfers between devices  9.21 us (27%)
  Pallas kernels  6.4 us (19%)
  local copies, waits for them, and re-layouts  1.78 us (5%)
    ppermute x3, starting transfers between devices, from_step(): return lax.ppermute(value, axis, pairs)  9.5 us
    ppermute x3, waiting for transfers between devices, from_step(): return lax.ppermute(value, axis, pairs)  9.2 us
    pallas_call x7, Pallas kernels, call(): pl.pallas_call(kernel, name=name, out_shape=out_shape, in_specs=in_specs...  6.4 us
    ppermute x2, starting transfers between devices, swap(): return lax.ppermute(value, axis, pairs + [(j, i) for i, j in pairs])  6.33 us
    unnamed x16, local copies, waits for them, and re-layouts  1.78 us
  transfers between devices with their start and end apart: 5, of which 2 were waited for; matrix products, arithmetic and copies ran while one was open for 0% of the time, Pallas kernels for 13%

profile of v2, /device:TPU:472, one launch (start us, length us, event | category | flops | bytes accessed | tf_op | source)
XLA Modules:
  0.0 33.4 jit_solution(4634757181127104401)
XLA Ops:
  0.0 4.4 %collective-permute-start.1 = (bf16[256,256]{1,0:T(8,128)(2,1)}, bf16[256,256]{1,0:T(8,128)(2,1)S(1)}, u32[]{:S(2)}, u32[]{:S(2)}) collective-permute-start(bf16[256,256]{1,0:T(8,128)(2,1)} %bitcast.4), channel_id=1, source_target_pairs={{1,2},{3,4},{5,6},{7,8},{9,10},{11,12},{13,14},{15,16},{17,18},{19... | collective-permute-start | bytes 393224 | tf_op jit(solution)/shard_map/ppermute | solution.py:386
  4.4 1.9 %collective-permute-start = (bf16[256,256]{1,0:T(8,128)(2,1)}, bf16[256,256]{1,0:T(8,128)(2,1)S(1)}, u32[]{:S(2)}, u32[]{:S(2)}) collective-permute-start(bf16[256,256]{1,0:T(8,128)(2,1)} %bitcast.5), channel_id=1, source_target_pairs={{0,1},{2,3},{4,5},{6,7},{8,9},{10,11},{12,13},{14,15},{16,17},{18,... | collective-permute-start | bytes 393224 | tf_op jit(solution)/shard_map/ppermute | solution.py:386
  6.4 0.7 %copy-done.2 = f32[16,9]{1,0:T(8,128)S(1)} copy-done((f32[16,9]{1,0:T(8,128)S(1)}, f32[16,9]{1,0:T(8,128)}, u32[]{:S(2)}) %copy-start.2) | copy-done | bytes 600
  7.1 0.5 %first_weights.1 = (bf16[384,256]{1,0:T(8,128)(2,1)S(1)}, bf16[48,256]{1,0:T(8,128)(2,1)S(1)}) custom-call(f32[16,9]{1,0:T(8,128)S(1)} %copy-done.2, f32[1,16]{1,0:T(1,128)S(1)} %bitcast.9), custom_call_target="tpu_custom_call" | custom-call | flops 2147483648 | bytes 1048576 | tf_op jit(solution)/shard_map/first_weights/pallas_call | solution.py:295
  7.6 0.0 copy-start.4
  7.6 0.0 copy-start.5
  7.6 0.2 copy-done.1
  7.8 0.4 %copy-done.4 = f32[16]{0:T(128)S(1)} copy-done((f32[16]{0:T(128)S(1)}, f32[16]{0:T(128)}, u32[]{:S(2)}) %copy-start.4) | copy-done | bytes 88
  8.3 0.0 copy-done.5
  8.3 0.5 %second_weights.1 = (bf16[128,512]{1,0:T(8,128)(2,1)S(1)}, f32[128,128]{1,0:T(8,128)S(1)}) custom-call(bf16[9,16,16]{2,1,0:T(8,128)(2,1)S(1)} %copy-done.1, f32[1,16]{1,0:T(1,128)S(1)} %bitcast.10, f32[1,16]{1,0:T(1,128)S(1)} %bitcast.11), custom_call_target="tpu_custom_call" | custom-call | flops 2147483648 | bytes 1048576 | tf_op jit(solution)/shard_map/second_weights/pallas_call | solution.py:295
  8.8 0.0 collective-permute-done.1.chip_ref
  8.8 0.0 collective-permute-done.core_ref
  8.8 0.4 %copy-done = bf16[1,256,256]{2,1,0:T(8,128)(2,1)S(1)} copy-done((bf16[1,256,256]{2,1,0:T(8,128)(2,1)S(1)}, bf16[1,256,256]{2,1,0:T(8,128)(2,1)}, u32[]{:S(2)}) %copy-start) | copy-done | bytes 131096
  9.2 5.5 %collective-permute-start.2 = (bf16[16,512]{1,0:T(8,128)(2,1)S(1)}, bf16[16,512]{1,0:T(8,128)(2,1)S(1)}, u32[]{:S(2)}, u32[]{:S(2)}) collective-permute-start(bf16[16,512]{1,0:T(8,128)(2,1)S(1)} %get-tuple-element.13), channel_id=1, source_target_pairs={{32,0},{64,32},{96,64},{33,1},{65,33},{97,65},{34,2},{66,34},{98,6... | collective-permute-start | bytes 49160 | tf_op jit(solution)/shard_map/ppermute | solution.py:380
  14.7 1.3 %collective-permute-start.3 = (bf16[16,512]{1,0:T(8,128)(2,1)S(1)}, bf16[16,512]{1,0:T(8,128)(2,1)S(1)}, u32[]{:S(2)}, u32[]{:S(2)}) collective-permute-start(bf16[16,512]{1,0:T(8,128)(2,1)S(1)} %get-tuple-element.14), channel_id=1, source_target_pairs={{0,32},{32,64},{64,96},{1,33},{33,65},{65,97},{2,34},{34,66},{66,9... | collective-permute-start | bytes 49160 | tf_op jit(solution)/shard_map/ppermute | solution.py:380
  16.0 2.9 %inner_rows.1.inner_ref = bf16[256,256]{1,0:T(8,128)(2,1)S(1)} custom-call(bf16[256,256]{1,0:T(8,128)(2,1)S(1)} %bitcast.7, bf16[256,256]{1,0:T(8,128)(2,1)S(1)} %get-tuple-element.12.sides_ref, bf16[384,256]{1,0:T(8,128)(2,1)S(1)} %get-tuple-element.15.w1_ref, bf16[128,512]{1,0:T(8,128)(2,1)S(1)} %get-tuple-element.16.w2_ref, ...), custom_call_target="tpu_custom_call" | custom-call | flops 3221225472 | bytes 1048576 | tf_op jit(solution)/shard_map/inner_rows/pallas_call | solution.py:295
  18.9 0.0 copy-start.6
  18.9 0.0 copy-start.7
  18.9 5.5 %collective-permute-done.3.above_ref = bf16[16,512]{1,0:T(8,128)(2,1)S(1)} collective-permute-done((bf16[16,512]{1,0:T(8,128)(2,1)S(1)}, bf16[16,512]{1,0:T(8,128)(2,1)S(1)}, u32[]{:S(2)}, u32[]{:S(2)}) %collective-permute-start.3) | collective-permute-done | bytes 16416 | tf_op jit(solution)/shard_map/ppermute | solution.py:380
  24.4 0.9 %outer_rows.1.image_ref = bf16[256,256]{1,0:T(8,128)(2,1)S(1)} custom-call(bf16[256,256]{1,0:T(8,128)(2,1)S(1)} %bitcast.8, bf16[256,256]{1,0:T(8,128)(2,1)S(1)} %get-tuple-element.12.sides_ref, bf16[16,512]{1,0:T(8,128)(2,1)S(1)} %collective-permute-done.2.below_ref, bf16[16,512]{1,0:T(8,128)(2,1)S(1)} %collective-permute-done.3.above_ref, ...), custom_call_target="tpu_custom_call" | custom-call | flops 268435456 | bytes 1048576 | tf_op jit(solution)/shard_map/outer_rows/pallas_call | solution.py:295
  25.3 2.8 %collective-permute-start.4 = (bf16[256,256]{1,0:T(8,128)(2,1)S(1)}, bf16[256,256]{1,0:T(8,128)(2,1)S(1)}, u32[]{:S(2)}, u32[]{:S(2)}) collective-permute-start(bf16[256,256]{1,0:T(8,128)(2,1)S(1)} %outer_rows.1.image_ref), channel_id=1, source_target_pairs={{128,0},{256,128},{384,256},{129,1},{257,129},{385,257},{130,2},{2... | collective-permute-start | bytes 393224 | tf_op jit(solution)/shard_map/ppermute | solution.py:380
  28.1 0.4 %own_spectrum.1.own_ref = f32[2,256,256]{2,1,0:T(8,128)S(1)} custom-call(bf16[256,256]{1,0:T(8,128)(2,1)S(1)} %outer_rows.1.image_ref, bf16[128,256]{1,0:T(8,128)(2,1)S(1)} %copy-done.7, bf16[256,256]{1,0:T(8,128)(2,1)S(1)} %copy-done.6), custom_call_target="tpu_custom_call" | custom-call | flops 536870912 | bytes 1048576 | tf_op jit(solution)/shard_map/own_spectrum/pallas_call | solution.py:295
  28.5 3.7 %collective-permute-done.4.image_ref = bf16[256,256]{1,0:T(8,128)(2,1)S(1)} collective-permute-done((bf16[256,256]{1,0:T(8,128)(2,1)S(1)}, bf16[256,256]{1,0:T(8,128)(2,1)S(1)}, u32[]{:S(2)}, u32[]{:S(2)}) %collective-permute-start.4) | collective-permute-done | bytes 131104 | tf_op jit(solution)/shard_map/ppermute | solution.py:380
  32.2 1.2 %cross_spectrum.1 = f32[1,2,256,256]{3,2,1,0:T(8,128)} custom-call(bf16[256,256]{1,0:T(8,128)(2,1)S(1)} %collective-permute-done.4.image_ref, bf16[128,256]{1,0:T(8,128)(2,1)S(1)} %copy-done.7, bf16[256,256]{1,0:T(8,128)(2,1)S(1)} %copy-done.6, f32[2,256,256]{2,1,0:T(8,128)S(1)} %own_spectrum.1.own_ref), custom_call_target="tpu_custom_call" | custom-call | flops 536870912 | bytes 1048576 | tf_op jit(solution)/shard_map/cross_spectrum/pallas_call | solution.py:295
  (9 shorter events, 0.1 us)
Async XLA Ops:
  0.0 6.3 %copy-start.3 = (f32[16]{0:T(128)S(1)}, f32[16]{0:T(128)}, u32[]{:S(2)}) copy-start(f32[16]{0:T(128)} %param.10) | copy-start | bytes 196
  0.0 8.8 %collective-permute-start.1 = (bf16[256,256]{1,0:T(8,128)(2,1)}, bf16[256,256]{1,0:T(8,128)(2,1)S(1)}, u32[]{:S(2)}, u32[]{:S(2)}) collective-permute-start(bf16[256,256]{1,0:T(8,128)(2,1)} %bitcast.4), channel_id=1, source_target_pairs={{1,2},{3,4},{5,6},{7,8},{9,10},{11,12},{13,14},{15,16},{17,18},{19... | collective-permute-start | bytes 393224 | tf_op jit(solution)/shard_map/ppermute | solution.py:386
  4.4 4.4 %collective-permute-start = (bf16[256,256]{1,0:T(8,128)(2,1)}, bf16[256,256]{1,0:T(8,128)(2,1)S(1)}, u32[]{:S(2)}, u32[]{:S(2)}) collective-permute-start(bf16[256,256]{1,0:T(8,128)(2,1)} %bitcast.5), channel_id=1, source_target_pairs={{0,1},{2,3},{4,5},{6,7},{8,9},{10,11},{12,13},{14,15},{16,17},{18,... | collective-permute-start | bytes 393224 | tf_op jit(solution)/shard_map/ppermute | solution.py:386
  6.4 0.7 %copy-start.2 = (f32[16,9]{1,0:T(8,128)S(1)}, f32[16,9]{1,0:T(8,128)}, u32[]{:S(2)}) copy-start(f32[16,9]{1,0:T(8,128)} %first_ref.1) | copy-start | bytes 1732
  7.1 0.8 %copy-start.1 = (bf16[9,16,16]{2,1,0:T(8,128)(2,1)S(1)}, bf16[9,16,16]{2,1,0:T(8,128)(2,1)}, u32[]{:S(2)}) copy-start(bf16[9,16,16]{2,1,0:T(8,128)(2,1)} %second_ref.1) | copy-start | bytes 13828
  7.6 0.7 %copy-start.4 = (f32[16]{0:T(128)S(1)}, f32[16]{0:T(128)}, u32[]{:S(2)}) copy-start(f32[16]{0:T(128)} %param.12) | copy-start | bytes 196
  7.6 0.7 %copy-start.5 = (f32[16]{0:T(128)S(1)}, f32[16]{0:T(128)}, u32[]{:S(2)}) copy-start(f32[16]{0:T(128)} %param.13) | copy-start | bytes 196
  8.3 0.9 %copy-start = (bf16[1,256,256]{2,1,0:T(8,128)(2,1)S(1)}, bf16[1,256,256]{2,1,0:T(8,128)(2,1)}, u32[]{:S(2)}) copy-start(bf16[1,256,256]{2,1,0:T(8,128)(2,1)} %param.8) | copy-start | bytes 393220
  9.2 9.7 %collective-permute-start.2 = (bf16[16,512]{1,0:T(8,128)(2,1)S(1)}, bf16[16,512]{1,0:T(8,128)(2,1)S(1)}, u32[]{:S(2)}, u32[]{:S(2)}) collective-permute-start(bf16[16,512]{1,0:T(8,128)(2,1)S(1)} %get-tuple-element.13), channel_id=1, source_target_pairs={{32,0},{64,32},{96,64},{33,1},{65,33},{97,65},{34,2},{66,34},{98,6... | collective-permute-start | bytes 49160 | tf_op jit(solution)/shard_map/ppermute | solution.py:380
  14.7 9.8 %collective-permute-start.3 = (bf16[16,512]{1,0:T(8,128)(2,1)S(1)}, bf16[16,512]{1,0:T(8,128)(2,1)S(1)}, u32[]{:S(2)}, u32[]{:S(2)}) collective-permute-start(bf16[16,512]{1,0:T(8,128)(2,1)S(1)} %get-tuple-element.14), channel_id=1, source_target_pairs={{0,32},{32,64},{64,96},{1,33},{33,65},{65,97},{2,34},{34,66},{66,9... | collective-permute-start | bytes 49160 | tf_op jit(solution)/shard_map/ppermute | solution.py:380
  18.9 9.2 %copy-start.6 = (bf16[256,256]{1,0:T(8,128)(2,1)S(1)}, bf16[256,256]{1,0:T(8,128)(2,1)}, u32[]{:S(2)}) copy-start(bf16[256,256]{1,0:T(8,128)(2,1)} %constant.5.clone.down_ref) | copy-start | bytes 393220
  18.9 9.2 %copy-start.7 = (bf16[128,256]{1,0:T(8,128)(2,1)S(1)}, bf16[128,256]{1,0:T(8,128)(2,1)}, u32[]{:S(2)}) copy-start(bf16[128,256]{1,0:T(8,128)(2,1)} %constant.4.clone.across_ref) | copy-start | bytes 196612
  25.3 6.9 %collective-permute-start.4 = (bf16[256,256]{1,0:T(8,128)(2,1)S(1)}, bf16[256,256]{1,0:T(8,128)(2,1)S(1)}, u32[]{:S(2)}, u32[]{:S(2)}) collective-permute-start(bf16[256,256]{1,0:T(8,128)(2,1)S(1)} %outer_rows.1.image_ref), channel_id=1, source_target_pairs={{128,0},{256,128},{384,256},{129,1},{257,129},{385,257},{130,2},{2... | collective-permute-start | bytes 393224 | tf_op jit(solution)/shard_map/ppermute | solution.py:380

commit v3 on v2

--- a/solution.py
+++ b/solution.py
@@ -61,7 +61,23 @@
     return lax.axis_index(axis) == (lax.axis_size(axis) - 1 if last else 0)
 
 
-def first_weights_kernel(first_ref, bias_ref, w1_ref, rows_out):
+def waits():
+    return lax.axis_index("gy") > 0
+
+
+def last_rows_kernel(rows_out):
+    row = iota((16, TILE), 0)
+    lane = iota((16, TILE), 1)
+    keep = row < 3
+    keep = keep | ((row == 3) & (lane == 0) & end_of("gx", False))
+    keep = keep | ((row == 4) & (lane == TILE - 1) & end_of("gx", True))
+    top = keep | ((row == 5) & end_of("gy", False))
+    bottom = keep | ((row == 6) & end_of("gy", True))
+    for k, mask in enumerate((keep, top, bottom)):
+        rows_out[16 * k : 16 * k + 16, :] = jnp.where(mask, 1.0, 0.0).astype(BF16)
+
+
+def first_weights(first_ref, bias_ref, rows_ref, w1_ref, rows_out):
     rows = BAND * CH
     row_r = iota((rows, K1), 0) // CH
     col = iota((rows, K1), 1)
@@ -92,18 +108,10 @@
         if dw == 2:
             total = jnp.where(col == 244, FAR, total)
         w1_ref[dw * rows : (dw + 1) * rows, :] = total.astype(BF16)
-    row = iota((16, TILE), 0)
-    lane = iota((16, TILE), 1)
-    keep = row < 3
-    keep = keep | ((row == 3) & (lane == 0) & end_of("gx", False))
-    keep = keep | ((row == 4) & (lane == TILE - 1) & end_of("gx", True))
-    top = keep | ((row == 5) & end_of("gy", False))
-    bottom = keep | ((row == 6) & end_of("gy", True))
-    for k, mask in enumerate((keep, top, bottom)):
-        rows_out[16 * k : 16 * k + 16, :] = jnp.where(mask, 1.0, 0.0).astype(BF16)
-
-
-def second_weights_kernel(second_ref, bias_ref, head_ref, w2_ref, head_out):
+    rows_out[...] = rows_ref[...]
+
+
+def second_weights(second_ref, bias_ref, head_ref, w2_ref, head_out):
     rows = CH * BAND
     row_r = iota((rows, K2), 0) % BAND
     col = iota((rows, K2), 1)
@@ -127,17 +135,22 @@
     head_out[...] = jnp.broadcast_to(column(head_ref[...], spread_bias), (rows, LANES))
 
 
-def sides_kernel(own_ref, core_ref, chip_ref, sides_ref, head_ref, tail_ref):
+def weights_kernel(first_ref, first_bias_ref, rows_ref, second_ref, second_bias_ref, head_ref, *outs):
+    first_weights(first_ref, first_bias_ref, rows_ref, *outs[:2])
+    second_weights(second_ref, second_bias_ref, head_ref, *outs[2:])
+
+
+def sides_kernel(own_ref, core_ref, chip_ref, sides_ref, *slab_refs):
     odd = lax.axis_index("gx") % 2 == 1
+    ends = {}
     for r in range(0, TILE, 16):
         core, chip, own = core_ref[r : r + 16, :], chip_ref[r : r + 16, :], own_ref[r : r + 16, :]
         left = jnp.where(odd, core[:, LANES:], chip[:, LANES:])
         right = jnp.where(odd, chip[:, :LANES], core[:, :LANES])
         sides_ref[r : r + 16, :] = jnp.concatenate([left, right], axis=1)
-        if r == 0:
-            head_ref[...] = jnp.concatenate([left, own, right], axis=1)
-        if r == TILE - 16:
-            tail_ref[...] = jnp.concatenate([left, own, right], axis=1)
+        ends[r] = jnp.concatenate([left, own, right], axis=1)
+    for k, slab_ref in enumerate(slab_refs):
+        slab_ref[...] = jnp.where(lax.axis_index("gy") == k, ends[TILE - 16], ends[0])
 
 
 def shifted(left, own, right):
@@ -164,89 +177,139 @@
     return center + parts[0]
 
 
+def stage(raw_ref, start, left, own, right):
+    for k, x in enumerate(shifted(left, own, right)):
+        raw_ref[k, start : start + own.shape[0], :] = x
+
+
+def stage_own(raw_ref, own_ref, sides_ref):
+    for r in range(0, TILE, 16):
+        rows = slice(r, r + 16)
+        stage(
+            raw_ref,
+            BAND + r,
+            sides_ref[rows, :LANES].astype(F32),
+            own_ref[rows, :].astype(F32),
+            sides_ref[rows, LANES:].astype(F32),
+        )
+
+
+def first_bands(bands, w1_ref, rows_ref, raw_ref, hid_ref):
+    size = BAND * CH
+    for j in bands:
+        kind = 16 * (1 if j == 0 else 2 if j == BANDS else 0)
+        raw = [raw_ref[k, BAND * j : BAND * j + 16, :] for k in range(5)]
+        hidden = hidden_band(w1_ref[...], raw, rows_ref[kind : kind + 16, :])
+        for dw in range(3):
+            hid_ref[dw, j * size : (j + 1) * size, :] = hidden[dw * size : (dw + 1) * size]
+
+
+def second_bands(bands, w2_ref, head_ref, raw_ref, hid_ref, res_ref):
+    ones = ones_rows()
+    for b in bands:
+        start = (b * BAND + 6) * CH
+        hidden = [hid_ref[dw, start : start + 160, :] for dw in range(3)]
+        center = raw_ref[2, BAND * (b + 1) : BAND * (b + 2), :]
+        res_ref[b * BAND : (b + 1) * BAND, :] = restored_band(w2_ref[...], hidden, ones, head_ref[...], center)
+
+
 def inner_kernel(
-    own_ref, sides_ref, w1_ref, w2_ref, head_ref, rows_ref, out_ref, raw_ref, hid_ref, res_ref
+    own_ref,
+    sides_ref,
+    w1_ref,
+    rows_ref,
+    w2_ref,
+    head_ref,
+    out_ref,
+    top_ref,
+    bottom_ref,
+    raw_ref,
+    hid_ref,
+    res_ref,
 ):
-    band_rows = BAND * CH
-    for r in range(0, TILE, 16):
-        own = own_ref[r : r + 16, :].astype(F32)
-        left = sides_ref[r : r + 16, :LANES].astype(F32)
-        right = sides_ref[r : r + 16, LANES:].astype(F32)
-        for s, x in enumerate(shifted(left, own, right)):
-            raw_ref[s, r : r + 16, :] = x
-    ones = ones_rows()
-    last_rows = rows_ref[0:16, :]
-
-    def first(j):
-        start = pl.multiple_of((j - 1) * BAND, BAND)
-        return hidden_band(
-            w1_ref[...], [raw_ref[s, pl.ds(start, 16), :] for s in range(5)], last_rows
-        )
-
-    def keep(j, hidden):
-        start = pl.multiple_of(j * band_rows, band_rows)
-        for dw in range(3):
-            hid_ref[dw, pl.ds(start, band_rows), :] = hidden[dw * band_rows : (dw + 1) * band_rows]
-
-    def second(b):
-        start = pl.multiple_of((b * BAND + 6) * CH, CH)
-        hidden = [hid_ref[dw, pl.ds(start, 160), :] for dw in range(3)]
-        center_start = pl.multiple_of(b * BAND, BAND)
-        res_ref[pl.ds(center_start, BAND), :] = restored_band(
-            w2_ref[...], hidden, ones, head_ref[...], raw_ref[2, pl.ds(center_start, BAND), :]
-        )
-
-    def body1(j, carry):
-        keep(j, first(j))
-        return carry
-
-    def body2(b, carry):
-        second(b)
-        return carry
-
-    lax.fori_loop(1, BANDS, body1, 0, unroll=UNROLL)
-    lax.fori_loop(1, BANDS - 1, body2, 0, unroll=UNROLL2)
-    res_ref[0:BAND, :] = jnp.zeros((BAND, TILE), F32)
-    res_ref[TILE - BAND :, :] = jnp.zeros((BAND, TILE), F32)
-    out_ref[...] = res_ref[...].astype(BF16)
-
-
-UNROLL = 31
-UNROLL2 = 30
+    size = BAND * CH
+
+    @pl.when(waits())
+    def _():
+        stage_own(raw_ref, own_ref, sides_ref)
+        first_bands(range(1, BANDS), w1_ref, rows_ref, raw_ref, hid_ref)
+        top_ref[...] = hid_ref[:, size : 2 * size, :]
+        bottom_ref[...] = hid_ref[:, BANDS * size - 2 * CH : BANDS * size, :]
+        second_bands(range(1, BANDS - 1), w2_ref, head_ref, raw_ref, hid_ref, res_ref)
+        res_ref[0:BAND, :] = jnp.zeros((BAND, TILE), F32)
+        res_ref[TILE - BAND :, :] = jnp.zeros((BAND, TILE), F32)
+        out_ref[...] = res_ref[...].astype(BF16)
+
+
+def border(border_refs, place):
+    value = jnp.zeros((16, TILE + 2 * LANES), F32)
+    for k, ref in enumerate(border_refs):
+        value = jnp.where(place == k, ref[...].astype(F32), value)
+    return value
 
 
 def outer_kernel(
-    own_ref, sides_ref, below_ref, above_ref, w1_ref, w2_ref, head_ref, rows_ref, inner_ref, out_ref
+    own_ref,
+    sides_ref,
+    w1_ref,
+    rows_ref,
+    w2_ref,
+    head_ref,
+    inner_ref,
+    top_ref,
+    bottom_ref,
+    *refs,
 ):
-    band_rows = BAND * CH
-    ones = ones_rows()
-    out_ref[16 : TILE - 16, :] = inner_ref[16 : TILE - 16, :]
-    for top in (True, False):
-        if top:
-            near = slice(0, 16)
-            far = above_ref[...].astype(F32)[8:16]
-        else:
-            near = slice(TILE - 16, TILE)
-            far = below_ref[...].astype(F32)[0:8]
-        own = own_ref[near, :].astype(F32)
-        parts = [sides_ref[near, :LANES].astype(F32), own, sides_ref[near, LANES:].astype(F32)]
-        halo = [far[:, :LANES], far[:, LANES : LANES + TILE], far[:, LANES + TILE :]]
-        order = (halo, parts) if top else (parts, halo)
-        shifts = shifted(*[jnp.concatenate([u, v], axis=0) for u, v in zip(*order)])
-        blocks = []
-        for k in range(2):
-            kind = 1 if top and k == 0 else 2 if k == 1 and not top else 0
-            last_rows = rows_ref[16 * kind : 16 * kind + 16, :]
-            blocks.append(hidden_band(w1_ref[...], [x[8 * k : 8 * k + 16] for x in shifts], last_rows))
-        hidden = [
-            jnp.concatenate([blk[dw * band_rows : (dw + 1) * band_rows] for blk in blocks], axis=0)[96:]
-            for dw in range(3)
-        ]
-        center = own[0:8] if top else own[8:16]
-        band = restored_band(w2_ref[...], hidden, ones, head_ref[...], center)
-        inner = inner_ref[near, :].astype(F32)
-        pair = [band, inner[8:16]] if top else [inner[0:8], band]
-        out_ref[near, :] = jnp.concatenate(pair, axis=0).astype(BF16)
+    borders, (out_ref, raw_ref, hid_ref, res_ref) = refs[:-4], refs[-4:]
+    gy = lax.axis_index("gy")
+    size = BAND * CH
+
+    def split(rows):
+        return rows[:, :LANES], rows[:, LANES : LANES + TILE], rows[:, LANES + TILE :]
+
+    @pl.when(jnp.logical_not(waits()))
+    def _():
+        stage(raw_ref, 0, *split(border(borders, gy - 1)[8:16]))
+        stage(raw_ref, BAND + TILE, *split(border(borders, gy)[0:8]))
+        stage_own(raw_ref, own_ref, sides_ref)
+        first_bands(range(BANDS + 1), w1_ref, rows_ref, raw_ref, hid_ref)
+        second_bands(range(BANDS), w2_ref, head_ref, raw_ref, hid_ref, res_ref)
+        out_ref[...] = res_ref[...].astype(BF16)
+
+    @pl.when(waits())
+    def _():
+        ones = ones_rows()
+
+        def edge(top):
+            near = slice(0, 16) if top else slice(TILE - 16, TILE)
+            half = slice(0, 8) if top else slice(8, 16)
+            far = split(border(borders, gy - 1)[8:16] if top else border(borders, gy)[0:8])
+            own = own_ref[near, :].astype(F32)[half]
+            side = sides_ref[near, :].astype(F32)[half]
+            parts = (side[:, :LANES], own, side[:, LANES:])
+            raw = shifted(*[jnp.concatenate((u, v) if top else (v, u), axis=0) for u, v in zip(far, parts)])
+            if top:
+                w1 = jnp.concatenate(
+                    [w1_ref[(dw + 1) * size - 2 * CH : (dw + 1) * size, :] for dw in range(3)], axis=0
+                )
+                found = hidden_band(w1, raw, rows_ref[16:32, :])
+                hidden = [
+                    jnp.concatenate([found[dw * 2 * CH : (dw + 1) * 2 * CH], top_ref[dw]], axis=0)
+                    for dw in range(3)
+                ]
+            else:
+                found = hidden_band(w1_ref[...], raw, rows_ref[32:48, :])
+                hidden = [
+                    jnp.concatenate([bottom_ref[dw], found[dw * size : (dw + 1) * size]], axis=0)
+                    for dw in range(3)
+                ]
+            band = restored_band(w2_ref[...], hidden, ones, head_ref[...], own)
+            inner = inner_ref[near, :].astype(F32)
+            pair = [band, inner[8:16]] if top else [inner[0:8], band]
+            out_ref[near, :] = jnp.concatenate(pair, axis=0).astype(BF16)
+
+        edge(True)
+        edge(False)
 
 
 def transform(image_ref, across_ref, down_ref):
@@ -291,16 +354,17 @@
     return pl.BlockSpec(shape, lambda: (0,) * len(shape), memory_space=VMEM)
 
 
-def call(kernel, name, out_shape, args, scratch=(), flops=0, in_specs=None, out_specs=None):
+def call(kernel, name, out_shape, args, scratch=(), flops=0, in_specs=None, out_specs=None, aliases=None):
     return pl.pallas_call(
         kernel,
         name=name,
         out_shape=out_shape,
         in_specs=in_specs or [full(a.shape) for a in args],
         out_specs=out_specs or jax.tree.map(lambda o: full(o.shape), out_shape),
+        input_output_aliases=aliases or {},
         scratch_shapes=list(scratch),
         compiler_params=PARAMS,
-        cost_estimate=pl.CostEstimate(flops=flops, bytes_accessed=1 << 20, transcendentals=0),
+        cost_estimate=pl.CostEstimate(flops=flops, bytes_accessed=0, transcendentals=0),
     )(*args)
 
 
@@ -308,51 +372,51 @@
     return jax.ShapeDtypeStruct(shape, dtype)
 
 
-def prepare(first_kernel, first_bias, second_kernel, second_bias, head):
-    w2, head = call(
-        second_weights_kernel,
-        "second_weights",
-        (shaped(CH * BAND, K2), shaped(CH * BAND, LANES, dtype=F32)),
-        (second_kernel, second_bias[None], head[None]),
-        flops=1 << 31,
-    )
-    w1, rows = call(
-        first_weights_kernel,
-        "first_weights",
-        (shaped(3 * BAND * CH, K1), shaped(48, TILE)),
-        (first_kernel, first_bias[None]),
-        flops=1 << 31,
-    )
-    return w1, w2, head, rows
-
-
-def sides(own, core, chip):
+WEIGHTS = (
+    shaped(3 * BAND * CH, K1),
+    shaped(48, TILE),
+    shaped(CH * BAND, K2),
+    shaped(CH * BAND, LANES, dtype=F32),
+)
+ROOM = (
+    pltpu.VMEM((5, TILE + 2 * BAND, TILE), F32),
+    pltpu.VMEM((3, (BANDS + 1) * BAND * CH, TILE), BF16),
+    pltpu.VMEM((TILE, TILE), F32),
+)
+
+
+def prepare(first, first_bias, second, second_bias, head):
+    rows = call(last_rows_kernel, "last_rows", WEIGHTS[1], (), flops=1 << 31)
+    given = (first, first_bias, rows, second, second_bias, head)
+    return call(weights_kernel, "weights", WEIGHTS, given)
+
+
+def sides(own, core, chip, borders):
     slab = shaped(16, TILE + 2 * LANES)
-    return call(sides_kernel, "sides", (shaped(TILE, TILE), slab, slab), (own, core, chip), flops=1 << 26)
+    shapes = (shaped(TILE, TILE),) + (slab,) * borders
+    return call(sides_kernel, "sides", shapes, (own, core, chip))
 
 
 def inner(own, side, weights):
     return call(
         inner_kernel,
         "inner_rows",
-        shaped(TILE, TILE),
+        (shaped(TILE, TILE), shaped(3, BAND * CH, TILE), shaped(3, 2 * CH, TILE)),
         (own, side, *weights),
-        scratch=[
-            pltpu.VMEM((5, TILE, TILE), F32),
-            pltpu.VMEM((3, (BANDS + 1) * BAND * CH, TILE), BF16),
-            pltpu.VMEM((TILE, TILE), F32),
-        ],
+        scratch=ROOM,
         flops=3 << 30,
     )
 
 
-def outer(own, side, above, below, weights, inside):
+def outer(own, side, weights, inside, borders):
     return call(
         outer_kernel,
         "outer_rows",
         shaped(TILE, TILE),
-        (own, side, below, above, *weights, inside),
-        flops=1 << 28,
+        (own, side, *weights, *inside, *borders),
+        scratch=ROOM,
+        flops=3 << 30,
+        aliases={6: 0},
     )
 
 
@@ -380,22 +444,22 @@
     return lax.ppermute(value, axis, pairs)
 
 
-def swap(value, axis, offset):
-    count = lax.axis_size(axis)
-    pairs = [(i, i + 1) for i in range(offset, count - 1, 2)]
+def swap(value, axis, starts):
+    pairs = [(i, i + 1) for i in starts]
     return lax.ppermute(value, axis, pairs + [(j, i) for i, j in pairs])
 
 
 def on_device(section, first_kernel, first_bias, second_kernel, second_bias, head_weight):
     own = section[0]
-    chip = swap(own, "gx", 1)
-    core = swap(own, "gx", 0)
-    weights = prepare(first_kernel, first_bias, second_kernel, second_bias, head_weight)
-    side, head, tail = sides(own, core, chip)
-    below = from_step(head, "gy", -1)
-    above = from_step(tail, "gy", 1)
+    columns, rows = lax.axis_size("gx"), lax.axis_size("gy")
+    chip = swap(own, "gx", range(1, columns - 1, 2))
+    core = swap(own, "gx", range(0, columns - 1, 2))
+    given = (first_kernel, first_bias[None], second_kernel, second_bias[None], head_weight[None])
+    weights = prepare(*given)
+    side, *slabs = sides(own, core, chip, rows - 1)
+    borders = [swap(slab, "gy", [k]) for k, slab in enumerate(slabs)]
     inside = inner(own, side, weights)
-    restored = outer(own, side, above, below, weights, inside)
+    restored = outer(own, side, weights, inside, borders)
     across, down = dft_tables()
     later = from_step(restored, "gz", -1)
     spectrum = own_spectrum(restored, across, down)

time: 33.7 us -> 31.7 us (0.941)
  the two profiles are of different devices: /device:TPU:472 before, /device:TPU:344 now
where the time goes in v3:
time: 31.7 us; the launch traced here: 31.4 us
  starting transfers between devices  14.6 us (46%)
  waiting for transfers between devices  9.93 us (31%)
  Pallas kernels  6 us (19%)
  local copies, waits for them, and re-layouts  0.7 us (2%)
    ppermute x5, starting transfers between devices, swap(): return lax.ppermute(value, axis, pairs + [(j, i) for i, j in pairs])  12.6 us
    pallas_call x7, Pallas kernels, call(): pl.pallas_call(kernel, name=name, out_shape=out_shape, in_specs=in_specs...  6 us
    ppermute x5, waiting for transfers between devices, swap(): return lax.ppermute(value, axis, pairs + [(j, i) for i, j in pairs])  5.52 us
    ppermute x1, waiting for transfers between devices, from_step(): return lax.ppermute(value, axis, pairs)  4.4 us
    ppermute x1, starting transfers between devices, from_step(): return lax.ppermute(value, axis, pairs)  2.02 us
    unnamed x16, local copies, waits for them, and re-layouts  0.7 us
  transfers between devices with their start and end apart: 6, of which 4 were waited for; matrix products, arithmetic and copies ran while one was open for 0% of the time, Pallas kernels for 13%

profile of v3, /device:TPU:344, one launch (start us, length us, event | category | flops | bytes accessed | tf_op | source)
XLA Modules:
  0.0 31.4 jit_solution(16247167348222807102)
XLA Ops:
  0.0 4.4 %collective-permute-start.1 = (bf16[256,256]{1,0:T(8,128)(2,1)}, bf16[256,256]{1,0:T(8,128)(2,1)S(1)}, u32[]{:S(2)}, u32[]{:S(2)}) collective-permute-start(bf16[256,256]{1,0:T(8,128)(2,1)} %bitcast.4), channel_id=1, source_target_pairs={{1,2},{3,4},{5,6},{7,8},{9,10},{11,12},{13,14},{15,16},{17,18},{19... | collective-permute-start | bytes 393224 | tf_op jit(solution)/shard_map/ppermute | solution.py:449
  4.4 1.9 %collective-permute-start = (bf16[256,256]{1,0:T(8,128)(2,1)}, bf16[256,256]{1,0:T(8,128)(2,1)S(1)}, u32[]{:S(2)}, u32[]{:S(2)}) collective-permute-start(bf16[256,256]{1,0:T(8,128)(2,1)} %bitcast.5), channel_id=1, source_target_pairs={{0,1},{2,3},{4,5},{6,7},{8,9},{10,11},{12,13},{14,15},{16,17},{18,... | collective-permute-start | bytes 393224 | tf_op jit(solution)/shard_map/ppermute | solution.py:449
  6.4 0.0 copy-start.3
  6.4 0.0 copy-start.4
  6.4 0.0 copy-start.5
  6.4 0.6 %copy-done.2 = f32[16,9]{1,0:T(8,128)S(1)} copy-done((f32[16,9]{1,0:T(8,128)S(1)}, f32[16,9]{1,0:T(8,128)}, u32[]{:S(2)}) %copy-start.2) | copy-done | bytes 600
  7.0 0.0 copy-done.3
  7.1 0.0 copy-done.4
  7.1 0.0 copy-done.5
  7.1 0.8 %weights.1 = (bf16[384,256]{1,0:T(8,128)(2,1)S(1)}, bf16[48,256]{1,0:T(8,128)(2,1)S(1)}, bf16[128,512]{1,0:T(8,128)(2,1)S(1)}, f32[128,128]{1,0:T(8,128)S(1)}) custom-call(f32[16,9]{1,0:T(8,128)S(1)} %copy-done.2, f32[1,16]{1,0:T(1,128)S(1)} %bitcast.9, bf16[48,256]{1,0:T(8,128)(2,1)S(1)} %last_rows.1.rows_ref, bf16[9,16,16]{2,1,0:T(8,128)(2,1)S(1)} %copy-done.1, ...), custom_call_target="tpu_custom_call" | custom-call | tf_op jit(solution)/shard_map/weights/pallas_call | solution.py:358
  7.9 0.8 %collective-permute-done.1.chip_ref = bf16[256,256]{1,0:T(8,128)(2,1)S(1)} collective-permute-done((bf16[256,256]{1,0:T(8,128)(2,1)}, bf16[256,256]{1,0:T(8,128)(2,1)S(1)}, u32[]{:S(2)}, u32[]{:S(2)}) %collective-permute-start.1) | collective-permute-done | bytes 131104 | tf_op jit(solution)/shard_map/ppermute | solution.py:449
  8.7 0.0 collective-permute-done.core_ref
  8.8 0.7 %collective-permute-start.2 = (bf16[16,512]{1,0:T(8,128)(2,1)S(1)}, bf16[16,512]{1,0:T(8,128)(2,1)S(1)}, u32[]{:S(2)}, u32[]{:S(2)}) collective-permute-start(bf16[16,512]{1,0:T(8,128)(2,1)S(1)} %get-tuple-element.24), channel_id=1, source_target_pairs={{0,32},{32,0},{1,33},{33,1},{2,34},{34,2},{3,35},{35,3},{4,36},{36... | collective-permute-start | bytes 49160 | tf_op jit(solution)/shard_map/ppermute | solution.py:449
  9.5 3.7 %collective-permute-start.3 = (bf16[16,512]{1,0:T(8,128)(2,1)S(1)}, bf16[16,512]{1,0:T(8,128)(2,1)S(1)}, u32[]{:S(2)}, u32[]{:S(2)}) collective-permute-start(bf16[16,512]{1,0:T(8,128)(2,1)S(1)} %get-tuple-element.25), channel_id=1, source_target_pairs={{32,64},{64,32},{33,65},{65,33},{34,66},{66,34},{35,67},{67,35},{3... | collective-permute-start | bytes 49160 | tf_op jit(solution)/shard_map/ppermute | solution.py:449
  13.2 1.9 %collective-permute-start.4 = (bf16[16,512]{1,0:T(8,128)(2,1)S(1)}, bf16[16,512]{1,0:T(8,128)(2,1)S(1)}, u32[]{:S(2)}, u32[]{:S(2)}) collective-permute-start(bf16[16,512]{1,0:T(8,128)(2,1)S(1)} %get-tuple-element.26), channel_id=1, source_target_pairs={{64,96},{96,64},{65,97},{97,65},{66,98},{98,66},{67,99},{99,67},{6... | collective-permute-start | bytes 49160 | tf_op jit(solution)/shard_map/ppermute | solution.py:449
  15.1 2.9 %inner_rows.1 = (bf16[256,256]{1,0:T(8,128)(2,1)S(1)}, bf16[3,128,256]{2,1,0:T(8,128)(2,1)S(1)}, bf16[3,32,256]{2,1,0:T(8,128)(2,1)S(1)}) custom-call(bf16[256,256]{1,0:T(8,128)(2,1)S(1)} %bitcast.7, bf16[256,256]{1,0:T(8,128)(2,1)S(1)} %get-tuple-element.16.sides_ref, bf16[384,256]{1,0:T(8,128)(2,1)S(1)} %get-tuple-element.17.w1_ref, ...), custom_call_target="tpu_custom_call" | custom-call | flops 3221225472 | tf_op jit(solution)/shard_map/inner_rows/pallas_call | solution.py:358
  18.0 0.0 collective-permute-done.2.refs_0_
  18.0 1.0 %collective-permute-done.3.refs_1_ = bf16[16,512]{1,0:T(8,128)(2,1)S(1)} collective-permute-done((bf16[16,512]{1,0:T(8,128)(2,1)S(1)}, bf16[16,512]{1,0:T(8,128)(2,1)S(1)}, u32[]{:S(2)}, u32[]{:S(2)}) %collective-permute-start.3) | collective-permute-done | bytes 16416 | tf_op jit(solution)/shard_map/ppermute | solution.py:449
  19.0 3.7 %collective-permute-done.4.refs_2_ = bf16[16,512]{1,0:T(8,128)(2,1)S(1)} collective-permute-done((bf16[16,512]{1,0:T(8,128)(2,1)S(1)}, bf16[16,512]{1,0:T(8,128)(2,1)S(1)}, u32[]{:S(2)}, u32[]{:S(2)}) %collective-permute-start.4) | collective-permute-done | bytes 16416 | tf_op jit(solution)/shard_map/ppermute | solution.py:449
  22.7 0.6 %outer_rows.1.image_ref = bf16[256,256]{1,0:T(8,128)(2,1)S(1)} custom-call(bf16[256,256]{1,0:T(8,128)(2,1)S(1)} %bitcast.8, bf16[256,256]{1,0:T(8,128)(2,1)S(1)} %get-tuple-element.16.sides_ref, bf16[384,256]{1,0:T(8,128)(2,1)S(1)} %get-tuple-element.17.w1_ref, bf16[48,256]{1,0:T(8,128)(2,1)S(1)} %get-tuple-element.18.rows_ref, ...), custom_call_target="tpu_custom_call", output_to_operand_aliasing={{}: (6, {})} | custom-call | flops 3221225472 | tf_op jit(solution)/shard_map/outer_rows/pallas_call | solution.py:358
  23.4 2.0 %collective-permute-start.5 = (bf16[256,256]{1,0:T(8,128)(2,1)S(1)}, bf16[256,256]{1,0:T(8,128)(2,1)S(1)}, u32[]{:S(2)}, u32[]{:S(2)}) collective-permute-start(bf16[256,256]{1,0:T(8,128)(2,1)S(1)} %outer_rows.1.image_ref), channel_id=1, source_target_pairs={{128,0},{256,128},{384,256},{129,1},{257,129},{385,257},{130,2},{2... | collective-permute-start | bytes 393224 | tf_op jit(solution)/shard_map/ppermute | solution.py:444
  25.4 0.4 %own_spectrum.1.own_ref = f32[2,256,256]{2,1,0:T(8,128)S(1)} custom-call(bf16[256,256]{1,0:T(8,128)(2,1)S(1)} %outer_rows.1.image_ref, bf16[128,256]{1,0:T(8,128)(2,1)S(1)} %copy-done.7, bf16[256,256]{1,0:T(8,128)(2,1)S(1)} %copy-done.6), custom_call_target="tpu_custom_call" | custom-call | flops 536870912 | tf_op jit(solution)/shard_map/own_spectrum/pallas_call | solution.py:358
  25.8 4.4 %collective-permute-done.5.image_ref = bf16[256,256]{1,0:T(8,128)(2,1)S(1)} collective-permute-done((bf16[256,256]{1,0:T(8,128)(2,1)S(1)}, bf16[256,256]{1,0:T(8,128)(2,1)S(1)}, u32[]{:S(2)}, u32[]{:S(2)}) %collective-permute-start.5) | collective-permute-done | bytes 131104 | tf_op jit(solution)/shard_map/ppermute | solution.py:444
  30.2 1.2 %cross_spectrum.1 = f32[1,2,256,256]{3,2,1,0:T(8,128)} custom-call(bf16[256,256]{1,0:T(8,128)(2,1)S(1)} %collective-permute-done.5.image_ref, bf16[128,256]{1,0:T(8,128)(2,1)S(1)} %copy-done.7, bf16[256,256]{1,0:T(8,128)(2,1)S(1)} %copy-done.6, f32[2,256,256]{2,1,0:T(8,128)S(1)} %own_spectrum.1.own_ref), custom_call_target="tpu_custom_call" | custom-call | flops 536870912 | tf_op jit(solution)/shard_map/cross_spectrum/pallas_call | solution.py:358
  (11 shorter events, 0.1 us)
Async XLA Ops:
  0.0 6.4 %copy-start.1 = (bf16[9,16,16]{2,1,0:T(8,128)(2,1)S(1)}, bf16[9,16,16]{2,1,0:T(8,128)(2,1)}, u32[]{:S(2)}) copy-start(bf16[9,16,16]{2,1,0:T(8,128)(2,1)} %second_ref.1) | copy-start | bytes 13828
  0.0 8.7 %collective-permute-start.1 = (bf16[256,256]{1,0:T(8,128)(2,1)}, bf16[256,256]{1,0:T(8,128)(2,1)S(1)}, u32[]{:S(2)}, u32[]{:S(2)}) collective-permute-start(bf16[256,256]{1,0:T(8,128)(2,1)} %bitcast.4), channel_id=1, source_target_pairs={{1,2},{3,4},{5,6},{7,8},{9,10},{11,12},{13,14},{15,16},{17,18},{19... | collective-permute-start | bytes 393224 | tf_op jit(solution)/shard_map/ppermute | solution.py:449
  4.4 4.3 %collective-permute-start = (bf16[256,256]{1,0:T(8,128)(2,1)}, bf16[256,256]{1,0:T(8,128)(2,1)S(1)}, u32[]{:S(2)}, u32[]{:S(2)}) collective-permute-start(bf16[256,256]{1,0:T(8,128)(2,1)} %bitcast.5), channel_id=1, source_target_pairs={{0,1},{2,3},{4,5},{6,7},{8,9},{10,11},{12,13},{14,15},{16,17},{18,... | collective-permute-start | bytes 393224 | tf_op jit(solution)/shard_map/ppermute | solution.py:449
  6.3 0.7 %copy-start.2 = (f32[16,9]{1,0:T(8,128)S(1)}, f32[16,9]{1,0:T(8,128)}, u32[]{:S(2)}) copy-start(f32[16,9]{1,0:T(8,128)} %first_ref.1) | copy-start | bytes 1732
  6.4 2.4 %copy-start = (bf16[1,256,256]{2,1,0:T(8,128)(2,1)S(1)}, bf16[1,256,256]{2,1,0:T(8,128)(2,1)}, u32[]{:S(2)}) copy-start(bf16[1,256,256]{2,1,0:T(8,128)(2,1)} %param.8) | copy-start | bytes 393220
  6.4 0.7 %copy-start.3 = (f32[16]{0:T(128)S(1)}, f32[16]{0:T(128)}, u32[]{:S(2)}) copy-start(f32[16]{0:T(128)} %param.10) | copy-start | bytes 196
  6.4 0.7 %copy-start.4 = (f32[16]{0:T(128)S(1)}, f32[16]{0:T(128)}, u32[]{:S(2)}) copy-start(f32[16]{0:T(128)} %param.12) | copy-start | bytes 196
  6.4 0.7 %copy-start.5 = (f32[16]{0:T(128)S(1)}, f32[16]{0:T(128)}, u32[]{:S(2)}) copy-start(f32[16]{0:T(128)} %param.13) | copy-start | bytes 196
  8.8 9.2 %collective-permute-start.2 = (bf16[16,512]{1,0:T(8,128)(2,1)S(1)}, bf16[16,512]{1,0:T(8,128)(2,1)S(1)}, u32[]{:S(2)}, u32[]{:S(2)}) collective-permute-start(bf16[16,512]{1,0:T(8,128)(2,1)S(1)} %get-tuple-element.24), channel_id=1, source_target_pairs={{0,32},{32,0},{1,33},{33,1},{2,34},{34,2},{3,35},{35,3},{4,36},{36... | collective-permute-start | bytes 49160 | tf_op jit(solution)/shard_map/ppermute | solution.py:449
  9.5 9.5 %collective-permute-start.3 = (bf16[16,512]{1,0:T(8,128)(2,1)S(1)}, bf16[16,512]{1,0:T(8,128)(2,1)S(1)}, u32[]{:S(2)}, u32[]{:S(2)}) collective-permute-start(bf16[16,512]{1,0:T(8,128)(2,1)S(1)} %get-tuple-element.25), channel_id=1, source_target_pairs={{32,64},{64,32},{33,65},{65,33},{34,66},{66,34},{35,67},{67,35},{3... | collective-permute-start | bytes 49160 | tf_op jit(solution)/shard_map/ppermute | solution.py:449
  13.2 9.5 %collective-permute-start.4 = (bf16[16,512]{1,0:T(8,128)(2,1)S(1)}, bf16[16,512]{1,0:T(8,128)(2,1)S(1)}, u32[]{:S(2)}, u32[]{:S(2)}) collective-permute-start(bf16[16,512]{1,0:T(8,128)(2,1)S(1)} %get-tuple-element.26), channel_id=1, source_target_pairs={{64,96},{96,64},{65,97},{97,65},{66,98},{98,66},{67,99},{99,67},{6... | collective-permute-start | bytes 49160 | tf_op jit(solution)/shard_map/ppermute | solution.py:449
  22.7 2.7 %copy-start.6 = (bf16[256,256]{1,0:T(8,128)(2,1)S(1)}, bf16[256,256]{1,0:T(8,128)(2,1)}, u32[]{:S(2)}) copy-start(bf16[256,256]{1,0:T(8,128)(2,1)} %constant.5.clone.down_ref) | copy-start | bytes 393220
  22.7 2.7 %copy-start.7 = (bf16[128,256]{1,0:T(8,128)(2,1)S(1)}, bf16[128,256]{1,0:T(8,128)(2,1)}, u32[]{:S(2)}) copy-start(bf16[128,256]{1,0:T(8,128)(2,1)} %constant.4.clone.across_ref) | copy-start | bytes 196612
  23.4 6.9 %collective-permute-start.5 = (bf16[256,256]{1,0:T(8,128)(2,1)S(1)}, bf16[256,256]{1,0:T(8,128)(2,1)S(1)}, u32[]{:S(2)}, u32[]{:S(2)}) collective-permute-start(bf16[256,256]{1,0:T(8,128)(2,1)S(1)} %outer_rows.1.image_ref), channel_id=1, source_target_pairs={{128,0},{256,128},{384,256},{129,1},{257,129},{385,257},{130,2},{2... | collective-permute-start | bytes 393224 | tf_op jit(solution)/shard_map/ppermute | solution.py:444

commit v4 on v3

--- a/solution.py
+++ b/solution.py
@@ -140,17 +140,36 @@
     second_weights(second_ref, second_bias_ref, head_ref, *outs[2:])
 
 
+def packed(r0, r1):
+    order = [r0[:, LANES : 2 * LANES], r0[:, 2 * LANES : 3 * LANES], r1[:, LANES : 2 * LANES]]
+    order += [r1[:, 2 * LANES : 3 * LANES], r0[:, :LANES], r0[:, 3 * LANES :], r1[:, :LANES], r1[:, 3 * LANES :]]
+    rows = jnp.concatenate(order, axis=0)
+    return jnp.concatenate([rows, rows], axis=0)
+
+
+def unpacked(block, at):
+    def place(r0, r1):
+        zeros = [jnp.zeros((n, r0.shape[1]), F32) for n in (at, 6 - at)]
+        return jnp.concatenate([x for x in (zeros[0], r0, r1, zeros[1]) if x.shape[0]], axis=0)
+
+    row = [block[k : k + 1] for k in range(8)]
+    own = place(jnp.concatenate(row[0:2], axis=1), jnp.concatenate(row[2:4], axis=1))
+    return place(row[4], row[6]), own, place(row[5], row[7])
+
+
 def sides_kernel(own_ref, core_ref, chip_ref, sides_ref, *slab_refs):
     odd = lax.axis_index("gx") % 2 == 1
     ends = {}
     for r in range(0, TILE, 16):
-        core, chip, own = core_ref[r : r + 16, :], chip_ref[r : r + 16, :], own_ref[r : r + 16, :]
+        core, chip = core_ref[r : r + 16, :], chip_ref[r : r + 16, :]
         left = jnp.where(odd, core[:, LANES:], chip[:, LANES:])
         right = jnp.where(odd, chip[:, :LANES], core[:, :LANES])
         sides_ref[r : r + 16, :] = jnp.concatenate([left, right], axis=1)
-        ends[r] = jnp.concatenate([left, own, right], axis=1)
+        if r in (0, TILE - 16):
+            wide = jnp.concatenate([left, own_ref[r : r + 16, :], right], axis=1).astype(F32)
+            ends[r] = packed(wide[0:1], wide[1:2]) if r == 0 else packed(wide[14:15], wide[15:16])
     for k, slab_ref in enumerate(slab_refs):
-        slab_ref[...] = jnp.where(lax.axis_index("gy") == k, ends[TILE - 16], ends[0])
+        slab_ref[...] = jnp.where(lax.axis_index("gy") == k, ends[TILE - 16], ends[0]).astype(BF16)
 
 
 def shifted(left, own, right):
@@ -168,13 +187,16 @@
     return jnp.maximum(dot(w1, grid), 0.0).astype(BF16)
 
 
+def add_up(parts):
+    while len(parts) > 1:
+        parts = [parts[i] + parts[i + 1] for i in range(0, len(parts), 2)]
+    return parts[0]
+
+
 def restored_band(w2, hidden, ones, head, center):
     deep = dot(w2, jnp.concatenate(hidden + [ones, jnp.zeros((16, TILE), BF16)], axis=0))
     deep = jnp.maximum(deep, 0.0) * jnp.concatenate([head, head], axis=1)
-    parts = [deep[o * BAND : (o + 1) * BAND] for o in range(CH)]
-    while len(parts) > 1:
-        parts = [parts[i] + parts[i + 1] for i in range(0, len(parts), 2)]
-    return center + parts[0]
+    return center + add_up([deep[o * BAND : (o + 1) * BAND] for o in range(CH)])
 
 
 def stage(raw_ref, start, left, own, right):
@@ -232,9 +254,11 @@
     @pl.when(waits())
     def _():
         stage_own(raw_ref, own_ref, sides_ref)
-        first_bands(range(1, BANDS), w1_ref, rows_ref, raw_ref, hid_ref)
+        for k in range(5):
+            raw_ref[k, BAND + TILE :, :] = jnp.zeros((BAND, TILE), F32)
+        first_bands(range(1, BANDS + 1), w1_ref, rows_ref, raw_ref, hid_ref)
         top_ref[...] = hid_ref[:, size : 2 * size, :]
-        bottom_ref[...] = hid_ref[:, BANDS * size - 2 * CH : BANDS * size, :]
+        bottom_ref[...] = hid_ref[:, BANDS * size - 2 * CH : (BANDS + 1) * size - 2 * CH, :]
         second_bands(range(1, BANDS - 1), w2_ref, head_ref, raw_ref, hid_ref, res_ref)
         res_ref[0:BAND, :] = jnp.zeros((BAND, TILE), F32)
         res_ref[TILE - BAND :, :] = jnp.zeros((BAND, TILE), F32)
@@ -242,7 +266,7 @@
 
 
 def border(border_refs, place):
-    value = jnp.zeros((16, TILE + 2 * LANES), F32)
+    value = jnp.zeros((16, LANES), F32)
     for k, ref in enumerate(border_refs):
         value = jnp.where(place == k, ref[...].astype(F32), value)
     return value
@@ -264,13 +288,16 @@
     gy = lax.axis_index("gy")
     size = BAND * CH
 
-    def split(rows):
-        return rows[:, :LANES], rows[:, LANES : LANES + TILE], rows[:, LANES + TILE :]
+    def above():
+        return unpacked(border(borders, gy - 1), 6)
+
+    def below():
+        return unpacked(border(borders, gy), 0)
 
     @pl.when(jnp.logical_not(waits()))
     def _():
-        stage(raw_ref, 0, *split(border(borders, gy - 1)[8:16]))
-        stage(raw_ref, BAND + TILE, *split(border(borders, gy)[0:8]))
+        stage(raw_ref, 0, *above())
+        stage(raw_ref, BAND + TILE, *below())
         stage_own(raw_ref, own_ref, sides_ref)
         first_bands(range(BANDS + 1), w1_ref, rows_ref, raw_ref, hid_ref)
         second_bands(range(BANDS), w2_ref, head_ref, raw_ref, hid_ref, res_ref)
@@ -278,38 +305,32 @@
 
     @pl.when(waits())
     def _():
-        ones = ones_rows()
-
-        def edge(top):
-            near = slice(0, 16) if top else slice(TILE - 16, TILE)
-            half = slice(0, 8) if top else slice(8, 16)
-            far = split(border(borders, gy - 1)[8:16] if top else border(borders, gy)[0:8])
-            own = own_ref[near, :].astype(F32)[half]
-            side = sides_ref[near, :].astype(F32)[half]
-            parts = (side[:, :LANES], own, side[:, LANES:])
-            raw = shifted(*[jnp.concatenate((u, v) if top else (v, u), axis=0) for u, v in zip(far, parts)])
-            if top:
-                w1 = jnp.concatenate(
-                    [w1_ref[(dw + 1) * size - 2 * CH : (dw + 1) * size, :] for dw in range(3)], axis=0
-                )
-                found = hidden_band(w1, raw, rows_ref[16:32, :])
-                hidden = [
-                    jnp.concatenate([found[dw * 2 * CH : (dw + 1) * 2 * CH], top_ref[dw]], axis=0)
-                    for dw in range(3)
-                ]
-            else:
-                found = hidden_band(w1_ref[...], raw, rows_ref[32:48, :])
-                hidden = [
-                    jnp.concatenate([bottom_ref[dw], found[dw * size : (dw + 1) * size]], axis=0)
-                    for dw in range(3)
-                ]
-            band = restored_band(w2_ref[...], hidden, ones, head_ref[...], own)
-            inner = inner_ref[near, :].astype(F32)
-            pair = [band, inner[8:16]] if top else [inner[0:8], band]
-            out_ref[near, :] = jnp.concatenate(pair, axis=0).astype(BF16)
-
-        edge(True)
-        edge(False)
+        first, last = slice(0, 16), slice(TILE - 16, TILE)
+        own = own_ref[first, :].astype(F32)[0:8], own_ref[last, :].astype(F32)[8:16]
+        side = sides_ref[first, :].astype(F32)[0:8], sides_ref[last, :].astype(F32)[8:16]
+        near = [(s[:, :LANES], o, s[:, LANES:]) for s, o in zip(side, own)]
+        top = shifted(*[jnp.concatenate(pair, axis=0) for pair in zip(above(), near[0])])
+        bottom = shifted(*[jnp.concatenate(pair, axis=0) for pair in zip(near[1], below())])
+        grids = []
+        for raw, rows in ((top, rows_ref[16:32, :]), (bottom, rows_ref[32:48, :])):
+            grids.append(jnp.concatenate([x.astype(BF16) for x in raw] * 3 + [rows], axis=0))
+        w1 = jnp.concatenate([w1_ref[(dw + 1) * size - 2 * CH : (dw + 1) * size, :] for dw in range(3)], axis=0)
+        found = jnp.maximum(dot(w1, jnp.concatenate(grids, axis=1)), 0.0).astype(BF16)
+        hidden = []
+        for dw in range(3):
+            two = found[dw * 2 * CH : (dw + 1) * 2 * CH]
+            upper = jnp.concatenate([two[:, :TILE], top_ref[dw]], axis=0)
+            lower = jnp.concatenate([bottom_ref[dw], two[:, TILE:]], axis=0)
+            hidden.append(jnp.concatenate([upper, lower], axis=1))
+        tail = jnp.concatenate([ones_rows(), jnp.zeros((16, TILE), BF16)], axis=0)
+        hidden.append(jnp.concatenate([tail, tail], axis=1))
+        deep = jnp.maximum(dot(w2_ref[...], jnp.concatenate(hidden, axis=0)), 0.0)
+        deep = deep * jnp.concatenate([head_ref[...]] * 4, axis=1)
+        total = add_up([deep[o * BAND : (o + 1) * BAND] for o in range(CH)])
+        upper = own[0] + total[:, :TILE]
+        lower = own[1] + total[:, TILE:]
+        out_ref[first, :] = jnp.concatenate([upper, inner_ref[first, :].astype(F32)[8:16]], axis=0).astype(BF16)
+        out_ref[last, :] = jnp.concatenate([inner_ref[last, :].astype(F32)[0:8], lower], axis=0).astype(BF16)
 
 
 def transform(image_ref, across_ref, down_ref):
@@ -392,7 +413,7 @@
 
 
 def sides(own, core, chip, borders):
-    slab = shaped(16, TILE + 2 * LANES)
+    slab = shaped(16, LANES)
     shapes = (shaped(TILE, TILE),) + (slab,) * borders
     return call(sides_kernel, "sides", shapes, (own, core, chip))
 
@@ -401,7 +422,7 @@
     return call(
         inner_kernel,
         "inner_rows",
-        (shaped(TILE, TILE), shaped(3, BAND * CH, TILE), shaped(3, 2 * CH, TILE)),
+        (shaped(TILE, TILE), shaped(3, BAND * CH, TILE), shaped(3, BAND * CH, TILE)),
         (own, side, *weights),
         scratch=ROOM,
         flops=3 << 30,

time: 31.7 us -> 31.5 us (level)
  transfers between devices with their start and end apart: 6 -> 6, of which waited for: 4 -> 4; matrix products, arithmetic and copies ran while one was open for 0% -> 0% of each run, Pallas kernels for 13% -> 14%
where the time goes in v4:
time: 31.5 us; the launch traced here: 31.2 us
  starting transfers between devices  14.6 us (46%)
  waiting for transfers between devices  9.68 us (31%)
  Pallas kernels  6.04 us (19%)
  local copies, waits for them, and re-layouts  0.7 us (2%)
    ppermute x5, starting transfers between devices, swap(): return lax.ppermute(value, axis, pairs + [(j, i) for i, j in pairs])  12.6 us
    pallas_call x7, Pallas kernels, call(): pl.pallas_call(kernel, name=name, out_shape=out_shape, in_specs=in_specs...  6.04 us
    ppermute x5, waiting for transfers between devices, swap(): return lax.ppermute(value, axis, pairs + [(j, i) for i, j in pairs])  5.27 us
    ppermute x1, waiting for transfers between devices, from_step(): return lax.ppermute(value, axis, pairs)  4.41 us
    ppermute x1, starting transfers between devices, from_step(): return lax.ppermute(value, axis, pairs)  2.02 us
    unnamed x16, local copies, waits for them, and re-layouts  0.7 us
  transfers between devices with their start and end apart: 6, of which 4 were waited for; matrix products, arithmetic and copies ran while one was open for 0% of the time, Pallas kernels for 14%

profile of v4, /device:TPU:344, one launch (start us, length us, event | category | flops | bytes accessed | tf_op | source)
XLA Modules:
  0.0 31.2 jit_solution(14173072491983267457)
XLA Ops:
  0.0 4.4 %collective-permute-start.1 = (bf16[256,256]{1,0:T(8,128)(2,1)}, bf16[256,256]{1,0:T(8,128)(2,1)S(1)}, u32[]{:S(2)}, u32[]{:S(2)}) collective-permute-start(bf16[256,256]{1,0:T(8,128)(2,1)} %bitcast.4), channel_id=1, source_target_pairs={{1,2},{3,4},{5,6},{7,8},{9,10},{11,12},{13,14},{15,16},{17,18},{19... | collective-permute-start | bytes 393224 | tf_op jit(solution)/shard_map/ppermute | solution.py:470
  4.4 1.9 %collective-permute-start = (bf16[256,256]{1,0:T(8,128)(2,1)}, bf16[256,256]{1,0:T(8,128)(2,1)S(1)}, u32[]{:S(2)}, u32[]{:S(2)}) collective-permute-start(bf16[256,256]{1,0:T(8,128)(2,1)} %bitcast.5), channel_id=1, source_target_pairs={{0,1},{2,3},{4,5},{6,7},{8,9},{10,11},{12,13},{14,15},{16,17},{18,... | collective-permute-start | bytes 393224 | tf_op jit(solution)/shard_map/ppermute | solution.py:470
  6.4 0.0 copy-start.3
  6.4 0.0 copy-start.4
  6.4 0.0 copy-start.5
  6.4 0.6 %copy-done.2 = f32[16,9]{1,0:T(8,128)S(1)} copy-done((f32[16,9]{1,0:T(8,128)S(1)}, f32[16,9]{1,0:T(8,128)}, u32[]{:S(2)}) %copy-start.2) | copy-done | bytes 600
  7.0 0.0 copy-done.3
  7.1 0.0 copy-done.4
  7.1 0.0 copy-done.5
  7.1 0.8 %weights.1 = (bf16[384,256]{1,0:T(8,128)(2,1)S(1)}, bf16[48,256]{1,0:T(8,128)(2,1)S(1)}, bf16[128,512]{1,0:T(8,128)(2,1)S(1)}, f32[128,128]{1,0:T(8,128)S(1)}) custom-call(f32[16,9]{1,0:T(8,128)S(1)} %copy-done.2, f32[1,16]{1,0:T(1,128)S(1)} %bitcast.9, bf16[48,256]{1,0:T(8,128)(2,1)S(1)} %last_rows.1.rows_ref, bf16[9,16,16]{2,1,0:T(8,128)(2,1)S(1)} %copy-done.1, ...), custom_call_target="tpu_custom_call" | custom-call | tf_op jit(solution)/shard_map/weights/pallas_call | solution.py:379
  7.9 0.8 %collective-permute-done.1.chip_ref = bf16[256,256]{1,0:T(8,128)(2,1)S(1)} collective-permute-done((bf16[256,256]{1,0:T(8,128)(2,1)}, bf16[256,256]{1,0:T(8,128)(2,1)S(1)}, u32[]{:S(2)}, u32[]{:S(2)}) %collective-permute-start.1) | collective-permute-done | bytes 131104 | tf_op jit(solution)/shard_map/ppermute | solution.py:470
  8.7 0.0 collective-permute-done.core_ref
  8.8 0.7 %collective-permute-start.2 = (bf16[16,128]{1,0:T(8,128)(2,1)S(1)}, bf16[16,128]{1,0:T(8,128)(2,1)S(1)}, u32[]{:S(2)}, u32[]{:S(2)}) collective-permute-start(bf16[16,128]{1,0:T(8,128)(2,1)S(1)} %get-tuple-element.24), channel_id=1, source_target_pairs={{0,32},{32,0},{1,33},{33,1},{2,34},{34,2},{3,35},{35,3},{4,36},{36... | collective-permute-start | bytes 12296 | tf_op jit(solution)/shard_map/ppermute | solution.py:470
  9.5 3.7 %collective-permute-start.3 = (bf16[16,128]{1,0:T(8,128)(2,1)S(1)}, bf16[16,128]{1,0:T(8,128)(2,1)S(1)}, u32[]{:S(2)}, u32[]{:S(2)}) collective-permute-start(bf16[16,128]{1,0:T(8,128)(2,1)S(1)} %get-tuple-element.25), channel_id=1, source_target_pairs={{32,64},{64,32},{33,65},{65,33},{34,66},{66,34},{35,67},{67,35},{3... | collective-permute-start | bytes 12296 | tf_op jit(solution)/shard_map/ppermute | solution.py:470
  13.2 1.9 %collective-permute-start.4 = (bf16[16,128]{1,0:T(8,128)(2,1)S(1)}, bf16[16,128]{1,0:T(8,128)(2,1)S(1)}, u32[]{:S(2)}, u32[]{:S(2)}) collective-permute-start(bf16[16,128]{1,0:T(8,128)(2,1)S(1)} %get-tuple-element.26), channel_id=1, source_target_pairs={{64,96},{96,64},{65,97},{97,65},{66,98},{98,66},{67,99},{99,67},{6... | collective-permute-start | bytes 12296 | tf_op jit(solution)/shard_map/ppermute | solution.py:470
  15.1 3.0 %inner_rows.1 = (bf16[256,256]{1,0:T(8,128)(2,1)S(1)}, bf16[3,128,256]{2,1,0:T(8,128)(2,1)S(1)}, bf16[3,128,256]{2,1,0:T(8,128)(2,1)S(1)}) custom-call(bf16[256,256]{1,0:T(8,128)(2,1)S(1)} %bitcast.7, bf16[256,256]{1,0:T(8,128)(2,1)S(1)} %get-tuple-element.16.sides_ref, bf16[384,256]{1,0:T(8,128)(2,1)S(1)} %get-tuple-element.17.w1_ref, ...), custom_call_target="tpu_custom_call" | custom-call | flops 3221225472 | tf_op jit(solution)/shard_map/inner_rows/pallas_call | solution.py:379
  18.1 0.0 collective-permute-done.2.refs_0_
  18.1 0.7 %collective-permute-done.3.refs_1_ = bf16[16,128]{1,0:T(8,128)(2,1)S(1)} collective-permute-done((bf16[16,128]{1,0:T(8,128)(2,1)S(1)}, bf16[16,128]{1,0:T(8,128)(2,1)S(1)}, u32[]{:S(2)}, u32[]{:S(2)}) %collective-permute-start.3) | collective-permute-done | bytes 4128 | tf_op jit(solution)/shard_map/ppermute | solution.py:470
  18.9 3.7 %collective-permute-done.4.refs_2_ = bf16[16,128]{1,0:T(8,128)(2,1)S(1)} collective-permute-done((bf16[16,128]{1,0:T(8,128)(2,1)S(1)}, bf16[16,128]{1,0:T(8,128)(2,1)S(1)}, u32[]{:S(2)}, u32[]{:S(2)}) %collective-permute-start.4) | collective-permute-done | bytes 4128 | tf_op jit(solution)/shard_map/ppermute | solution.py:470
  22.6 0.6 %outer_rows.1.image_ref = bf16[256,256]{1,0:T(8,128)(2,1)S(1)} custom-call(bf16[256,256]{1,0:T(8,128)(2,1)S(1)} %bitcast.8, bf16[256,256]{1,0:T(8,128)(2,1)S(1)} %get-tuple-element.16.sides_ref, bf16[384,256]{1,0:T(8,128)(2,1)S(1)} %get-tuple-element.17.w1_ref, bf16[48,256]{1,0:T(8,128)(2,1)S(1)} %get-tuple-element.18.rows_ref, ...), custom_call_target="tpu_custom_call", output_to_operand_aliasing={{}: (6, {})} | custom-call | flops 3221225472 | tf_op jit(solution)/shard_map/outer_rows/pallas_call | solution.py:379
  23.2 2.0 %collective-permute-start.5 = (bf16[256,256]{1,0:T(8,128)(2,1)S(1)}, bf16[256,256]{1,0:T(8,128)(2,1)S(1)}, u32[]{:S(2)}, u32[]{:S(2)}) collective-permute-start(bf16[256,256]{1,0:T(8,128)(2,1)S(1)} %outer_rows.1.image_ref), channel_id=1, source_target_pairs={{128,0},{256,128},{384,256},{129,1},{257,129},{385,257},{130,2},{2... | collective-permute-start | bytes 393224 | tf_op jit(solution)/shard_map/ppermute | solution.py:465
  25.2 0.4 %own_spectrum.1.own_ref = f32[2,256,256]{2,1,0:T(8,128)S(1)} custom-call(bf16[256,256]{1,0:T(8,128)(2,1)S(1)} %outer_rows.1.image_ref, bf16[128,256]{1,0:T(8,128)(2,1)S(1)} %copy-done.7, bf16[256,256]{1,0:T(8,128)(2,1)S(1)} %copy-done.6), custom_call_target="tpu_custom_call" | custom-call | flops 536870912 | tf_op jit(solution)/shard_map/own_spectrum/pallas_call | solution.py:379
  25.6 4.4 %collective-permute-done.5.image_ref = bf16[256,256]{1,0:T(8,128)(2,1)S(1)} collective-permute-done((bf16[256,256]{1,0:T(8,128)(2,1)S(1)}, bf16[256,256]{1,0:T(8,128)(2,1)S(1)}, u32[]{:S(2)}, u32[]{:S(2)}) %collective-permute-start.5) | collective-permute-done | bytes 131104 | tf_op jit(solution)/shard_map/ppermute | solution.py:465
  30.0 1.2 %cross_spectrum.1 = f32[1,2,256,256]{3,2,1,0:T(8,128)} custom-call(bf16[256,256]{1,0:T(8,128)(2,1)S(1)} %collective-permute-done.5.image_ref, bf16[128,256]{1,0:T(8,128)(2,1)S(1)} %copy-done.7, bf16[256,256]{1,0:T(8,128)(2,1)S(1)} %copy-done.6, f32[2,256,256]{2,1,0:T(8,128)S(1)} %own_spectrum.1.own_ref), custom_call_target="tpu_custom_call" | custom-call | flops 536870912 | tf_op jit(solution)/shard_map/cross_spectrum/pallas_call | solution.py:379
  (11 shorter events, 0.1 us)
Async XLA Ops:
  0.0 6.4 %copy-start.1 = (bf16[9,16,16]{2,1,0:T(8,128)(2,1)S(1)}, bf16[9,16,16]{2,1,0:T(8,128)(2,1)}, u32[]{:S(2)}) copy-start(bf16[9,16,16]{2,1,0:T(8,128)(2,1)} %second_ref.1) | copy-start | bytes 13828
  0.0 8.7 %collective-permute-start.1 = (bf16[256,256]{1,0:T(8,128)(2,1)}, bf16[256,256]{1,0:T(8,128)(2,1)S(1)}, u32[]{:S(2)}, u32[]{:S(2)}) collective-permute-start(bf16[256,256]{1,0:T(8,128)(2,1)} %bitcast.4), channel_id=1, source_target_pairs={{1,2},{3,4},{5,6},{7,8},{9,10},{11,12},{13,14},{15,16},{17,18},{19... | collective-permute-start | bytes 393224 | tf_op jit(solution)/shard_map/ppermute | solution.py:470
  4.4 4.3 %collective-permute-start = (bf16[256,256]{1,0:T(8,128)(2,1)}, bf16[256,256]{1,0:T(8,128)(2,1)S(1)}, u32[]{:S(2)}, u32[]{:S(2)}) collective-permute-start(bf16[256,256]{1,0:T(8,128)(2,1)} %bitcast.5), channel_id=1, source_target_pairs={{0,1},{2,3},{4,5},{6,7},{8,9},{10,11},{12,13},{14,15},{16,17},{18,... | collective-permute-start | bytes 393224 | tf_op jit(solution)/shard_map/ppermute | solution.py:470
  6.3 0.7 %copy-start.2 = (f32[16,9]{1,0:T(8,128)S(1)}, f32[16,9]{1,0:T(8,128)}, u32[]{:S(2)}) copy-start(f32[16,9]{1,0:T(8,128)} %first_ref.1) | copy-start | bytes 1732
  6.4 2.4 %copy-start = (bf16[1,256,256]{2,1,0:T(8,128)(2,1)S(1)}, bf16[1,256,256]{2,1,0:T(8,128)(2,1)}, u32[]{:S(2)}) copy-start(bf16[1,256,256]{2,1,0:T(8,128)(2,1)} %param.8) | copy-start | bytes 393220
  6.4 0.7 %copy-start.3 = (f32[16]{0:T(128)S(1)}, f32[16]{0:T(128)}, u32[]{:S(2)}) copy-start(f32[16]{0:T(128)} %param.10) | copy-start | bytes 196
  6.4 0.7 %copy-start.4 = (f32[16]{0:T(128)S(1)}, f32[16]{0:T(128)}, u32[]{:S(2)}) copy-start(f32[16]{0:T(128)} %param.12) | copy-start | bytes 196
  6.4 0.7 %copy-start.5 = (f32[16]{0:T(128)S(1)}, f32[16]{0:T(128)}, u32[]{:S(2)}) copy-start(f32[16]{0:T(128)} %param.13) | copy-start | bytes 196
  8.8 9.3 %collective-permute-start.2 = (bf16[16,128]{1,0:T(8,128)(2,1)S(1)}, bf16[16,128]{1,0:T(8,128)(2,1)S(1)}, u32[]{:S(2)}, u32[]{:S(2)}) collective-permute-start(bf16[16,128]{1,0:T(8,128)(2,1)S(1)} %get-tuple-element.24), channel_id=1, source_target_pairs={{0,32},{32,0},{1,33},{33,1},{2,34},{34,2},{3,35},{35,3},{4,36},{36... | collective-permute-start | bytes 12296 | tf_op jit(solution)/shard_map/ppermute | solution.py:470
  9.5 9.4 %collective-permute-start.3 = (bf16[16,128]{1,0:T(8,128)(2,1)S(1)}, bf16[16,128]{1,0:T(8,128)(2,1)S(1)}, u32[]{:S(2)}, u32[]{:S(2)}) collective-permute-start(bf16[16,128]{1,0:T(8,128)(2,1)S(1)} %get-tuple-element.25), channel_id=1, source_target_pairs={{32,64},{64,32},{33,65},{65,33},{34,66},{66,34},{35,67},{67,35},{3... | collective-permute-start | bytes 12296 | tf_op jit(solution)/shard_map/ppermute | solution.py:470
  13.2 9.4 %collective-permute-start.4 = (bf16[16,128]{1,0:T(8,128)(2,1)S(1)}, bf16[16,128]{1,0:T(8,128)(2,1)S(1)}, u32[]{:S(2)}, u32[]{:S(2)}) collective-permute-start(bf16[16,128]{1,0:T(8,128)(2,1)S(1)} %get-tuple-element.26), channel_id=1, source_target_pairs={{64,96},{96,64},{65,97},{97,65},{66,98},{98,66},{67,99},{99,67},{6... | collective-permute-start | bytes 12296 | tf_op jit(solution)/shard_map/ppermute | solution.py:470
  22.6 2.6 %copy-start.6 = (bf16[256,256]{1,0:T(8,128)(2,1)S(1)}, bf16[256,256]{1,0:T(8,128)(2,1)}, u32[]{:S(2)}) copy-start(bf16[256,256]{1,0:T(8,128)(2,1)} %constant.5.clone.down_ref) | copy-start | bytes 393220
  22.6 2.6 %copy-start.7 = (bf16[128,256]{1,0:T(8,128)(2,1)S(1)}, bf16[128,256]{1,0:T(8,128)(2,1)}, u32[]{:S(2)}) copy-start(bf16[128,256]{1,0:T(8,128)(2,1)} %constant.4.clone.across_ref) | copy-start | bytes 196612
  23.2 6.9 %collective-permute-start.5 = (bf16[256,256]{1,0:T(8,128)(2,1)S(1)}, bf16[256,256]{1,0:T(8,128)(2,1)S(1)}, u32[]{:S(2)}, u32[]{:S(2)}) collective-permute-start(bf16[256,256]{1,0:T(8,128)(2,1)S(1)} %outer_rows.1.image_ref), channel_id=1, source_target_pairs={{128,0},{256,128},{384,256},{129,1},{257,129},{385,257},{130,2},{2... | collective-permute-start | bytes 393224 | tf_op jit(solution)/shard_map/ppermute | solution.py:465

commit v5 on v4

--- a/solution.py
+++ b/solution.py
@@ -14,7 +14,8 @@
 BAND = 8
 BANDS = TILE // BAND
 LANES = 128
-K1 = 256
+K1 = 160
+RING = TILE + LANES
 K2 = 512
 FAR = -65536.0
 
@@ -66,11 +67,11 @@
 
 
 def last_rows_kernel(rows_out):
-    row = iota((16, TILE), 0)
-    lane = iota((16, TILE), 1)
+    row = iota((16, RING), 0)
+    lane = iota((16, RING), 1)
     keep = row < 3
-    keep = keep | ((row == 3) & (lane == 0) & end_of("gx", False))
-    keep = keep | ((row == 4) & (lane == TILE - 1) & end_of("gx", True))
+    keep = keep | ((row == 3) & (lane == RING - 1) & end_of("gx", False))
+    keep = keep | ((row == 3) & (lane == TILE) & end_of("gx", True))
     top = keep | ((row == 5) & end_of("gy", False))
     bottom = keep | ((row == 6) & end_of("gy", True))
     for k, mask in enumerate((keep, top, bottom)):
@@ -86,28 +87,22 @@
     spread = (iota((rows, 48), 0) % CH == iota((rows, 48), 1) % CH).astype(F32).astype(BF16)
     sel_t = iota((9, K1), 0)
     sel_col = iota((9, K1), 1)
-    sel_b = sel_col % 80 // 16
-    in_grid = (sel_b <= 2) & (sel_col < 240)
-    own_piece = iota((48, K1), 0) // CH == iota((48, K1), 1) // 80
-    base = jnp.zeros((rows, K1), F32)
+    sel_b = sel_col % 48 // 16
+    own_piece = iota((48, K1), 0) // CH == iota((48, K1), 1) // 48
+    total = jnp.zeros((rows, K1), F32)
     for a in range(3):
-        select = (sel_t == 3 * a + sel_b) & in_grid
+        select = (sel_t == 3 * a + sel_b) & (sel_col < 144)
         picked = dot(stacked, select.astype(F32).astype(BF16))
         picked = jnp.where(own_piece, picked, 0.0).astype(BF16)
-        base = base + jnp.where(col_i - row_r == a, dot(spread, picked), 0.0)
+        total = total + jnp.where(col_i - row_r == a, dot(spread, picked), 0.0)
     spread_bias = iota((rows, CH), 0) % CH == iota((rows, CH), 1)
-    tail = jnp.zeros((rows, K1), F32)
+    total = jnp.where(col < 144, total, 0.0)
     for k, piece in enumerate(pieces(bias_ref[...])):
-        tail = jnp.where(col == 240 + k, column(piece.astype(F32), spread_bias), tail)
-    tail = jnp.where((col == 245) & (row_r < 7), FAR, tail)
-    tail = jnp.where((col == 246) & (row_r == 7), FAR, tail)
-    for dw in range(3):
-        total = jnp.where(col < 240, pltpu.roll(base, 16 * dw, 1) if dw else base, tail)
-        if dw == 0:
-            total = jnp.where(col == 243, FAR, total)
-        if dw == 2:
-            total = jnp.where(col == 244, FAR, total)
-        w1_ref[dw * rows : (dw + 1) * rows, :] = total.astype(BF16)
+        total = jnp.where(col == 144 + k, column(piece.astype(F32), spread_bias), total)
+    total = jnp.where(col == 147, FAR, total)
+    total = jnp.where((col == 149) & (row_r < 7), FAR, total)
+    total = jnp.where((col == 150) & (row_r == 7), FAR, total)
+    w1_ref[...] = total.astype(BF16)
     rows_out[...] = rows_ref[...]
 
 
@@ -141,50 +136,40 @@
 
 
 def packed(r0, r1):
-    order = [r0[:, LANES : 2 * LANES], r0[:, 2 * LANES : 3 * LANES], r1[:, LANES : 2 * LANES]]
-    order += [r1[:, 2 * LANES : 3 * LANES], r0[:, :LANES], r0[:, 3 * LANES :], r1[:, :LANES], r1[:, 3 * LANES :]]
-    rows = jnp.concatenate(order, axis=0)
+    rows = [r[:, k * LANES : (k + 1) * LANES] for r in (r0, r1) for k in range(3)]
+    rows = jnp.concatenate(rows + [jnp.zeros((2, LANES), F32)], axis=0)
     return jnp.concatenate([rows, rows], axis=0)
 
 
 def unpacked(block, at):
-    def place(r0, r1):
-        zeros = [jnp.zeros((n, r0.shape[1]), F32) for n in (at, 6 - at)]
-        return jnp.concatenate([x for x in (zeros[0], r0, r1, zeros[1]) if x.shape[0]], axis=0)
-
-    row = [block[k : k + 1] for k in range(8)]
-    own = place(jnp.concatenate(row[0:2], axis=1), jnp.concatenate(row[2:4], axis=1))
-    return place(row[4], row[6]), own, place(row[5], row[7])
+    r0, r1 = (jnp.concatenate([block[k + j : k + j + 1] for j in range(3)], axis=1) for k in (0, 3))
+    zeros = [jnp.zeros((n, RING), F32) for n in (at, 6 - at)]
+    return jnp.concatenate([x for x in (zeros[0], r0, r1, zeros[1]) if x.shape[0]], axis=0)
 
 
 def sides_kernel(own_ref, core_ref, chip_ref, sides_ref, *slab_refs):
     odd = lax.axis_index("gx") % 2 == 1
+    first = iota((16, LANES), 1) < LANES // 2
     ends = {}
     for r in range(0, TILE, 16):
-        core, chip = core_ref[r : r + 16, :], chip_ref[r : r + 16, :]
+        core, chip = core_ref[r : r + 16, :].astype(F32), chip_ref[r : r + 16, :].astype(F32)
         left = jnp.where(odd, core[:, LANES:], chip[:, LANES:])
         right = jnp.where(odd, chip[:, :LANES], core[:, :LANES])
-        sides_ref[r : r + 16, :] = jnp.concatenate([left, right], axis=1)
+        side = jnp.where(first, right, left)
+        sides_ref[r : r + 16, :] = side.astype(BF16)
         if r in (0, TILE - 16):
-            wide = jnp.concatenate([left, own_ref[r : r + 16, :], right], axis=1).astype(F32)
-            ends[r] = packed(wide[0:1], wide[1:2]) if r == 0 else packed(wide[14:15], wide[15:16])
+            ring = jnp.concatenate([own_ref[r : r + 16, :].astype(F32), side], axis=1)
+            ends[r] = packed(ring[0:1], ring[1:2]) if r == 0 else packed(ring[14:15], ring[15:16])
     for k, slab_ref in enumerate(slab_refs):
         slab_ref[...] = jnp.where(lax.axis_index("gy") == k, ends[TILE - 16], ends[0]).astype(BF16)
 
 
-def shifted(left, own, right):
-    wide = jnp.concatenate([left, own, right], axis=1)
-    return [wide[:, LANES - 2 + s : LANES - 2 + s + TILE] for s in range(5)]
+def around(ring):
+    return [pltpu.roll(ring, 1, 1), ring, pltpu.roll(ring, RING - 1, 1)]
 
 
 def ones_rows():
     return jnp.where(iota((16, TILE), 0) < 3, 1.0, 0.0).astype(BF16)
-
-
-def hidden_band(w1, shifts, last_rows):
-    raw = [x.astype(BF16) for x in shifts]
-    grid = jnp.concatenate(raw * 3 + [last_rows], axis=0)
-    return jnp.maximum(dot(w1, grid), 0.0).astype(BF16)
 
 
 def add_up(parts):
@@ -193,46 +178,57 @@
     return parts[0]
 
 
-def restored_band(w2, hidden, ones, head, center):
-    deep = dot(w2, jnp.concatenate(hidden + [ones, jnp.zeros((16, TILE), BF16)], axis=0))
-    deep = jnp.maximum(deep, 0.0) * jnp.concatenate([head, head], axis=1)
-    return center + add_up([deep[o * BAND : (o + 1) * BAND] for o in range(CH)])
-
-
-def stage(raw_ref, start, left, own, right):
-    for k, x in enumerate(shifted(left, own, right)):
-        raw_ref[k, start : start + own.shape[0], :] = x
+def stage(raw_ref, start, ring):
+    for k, x in enumerate(around(ring)):
+        raw_ref[k, start : start + ring.shape[0], :] = x
 
 
 def stage_own(raw_ref, own_ref, sides_ref):
     for r in range(0, TILE, 16):
         rows = slice(r, r + 16)
-        stage(
-            raw_ref,
-            BAND + r,
-            sides_ref[rows, :LANES].astype(F32),
-            own_ref[rows, :].astype(F32),
-            sides_ref[rows, LANES:].astype(F32),
-        )
+        ring = jnp.concatenate([own_ref[rows, :].astype(F32), sides_ref[rows, :].astype(F32)], axis=1)
+        stage(raw_ref, BAND + r, ring)
 
 
 def first_bands(bands, w1_ref, rows_ref, raw_ref, hid_ref):
     size = BAND * CH
-    for j in bands:
+
+    def grid(j):
         kind = 16 * (1 if j == 0 else 2 if j == BANDS else 0)
-        raw = [raw_ref[k, BAND * j : BAND * j + 16, :] for k in range(5)]
-        hidden = hidden_band(w1_ref[...], raw, rows_ref[kind : kind + 16, :])
-        for dw in range(3):
-            hid_ref[dw, j * size : (j + 1) * size, :] = hidden[dw * size : (dw + 1) * size]
+        raw = [raw_ref[k, BAND * j : BAND * j + 16, :].astype(BF16) for k in range(3)]
+        return jnp.concatenate(raw * 3 + [rows_ref[kind : kind + 16, :]], axis=0)
+
+    def keep(j, ring):
+        for dw, x in enumerate(around(ring)):
+            hid_ref[dw, j * size : (j + 1) * size, :] = x[:, :TILE]
+
+    bands = list(bands)
+    while bands:
+        now, bands = bands[:2], bands[2:]
+        grids = [grid(j) for j in now]
+        if len(now) == 2:
+            grids[1] = jnp.concatenate([grids[1][:, TILE:], grids[1][:, :TILE]], axis=1)
+        found = jnp.maximum(dot(w1_ref[...], jnp.concatenate(grids, axis=1)), 0.0).astype(BF16)
+        keep(now[0], found[:, :RING])
+        if len(now) == 2:
+            keep(now[1], jnp.concatenate([found[:, RING + LANES :], found[:, RING : RING + LANES]], axis=1))
 
 
 def second_bands(bands, w2_ref, head_ref, raw_ref, hid_ref, res_ref):
-    ones = ones_rows()
-    for b in bands:
-        start = (b * BAND + 6) * CH
-        hidden = [hid_ref[dw, start : start + 160, :] for dw in range(3)]
-        center = raw_ref[2, BAND * (b + 1) : BAND * (b + 2), :]
-        res_ref[b * BAND : (b + 1) * BAND, :] = restored_band(w2_ref[...], hidden, ones, head_ref[...], center)
+    tail = jnp.concatenate([ones_rows(), jnp.zeros((16, TILE), BF16)], axis=0)
+    bands = list(bands)
+    while bands:
+        now, bands = bands[:2], bands[2:]
+        grids = []
+        for b in now:
+            start = (b * BAND + 6) * CH
+            grids.append(jnp.concatenate([hid_ref[dw, start : start + 160, :] for dw in range(3)] + [tail], axis=0))
+        deep = jnp.maximum(dot(w2_ref[...], jnp.concatenate(grids, axis=1)), 0.0)
+        deep = deep * jnp.concatenate([head_ref[...]] * (2 * len(now)), axis=1)
+        total = add_up([deep[o * BAND : (o + 1) * BAND] for o in range(CH)])
+        for n, b in enumerate(now):
+            center = raw_ref[1, BAND * (b + 1) : BAND * (b + 2), :TILE]
+            res_ref[b * BAND : (b + 1) * BAND, :] = center + total[:, n * TILE : (n + 1) * TILE]
 
 
 def inner_kernel(
@@ -254,8 +250,8 @@
     @pl.when(waits())
     def _():
         stage_own(raw_ref, own_ref, sides_ref)
-        for k in range(5):
-            raw_ref[k, BAND + TILE :, :] = jnp.zeros((BAND, TILE), F32)
+        for k in range(3):
+            raw_ref[k, BAND + TILE :, :] = jnp.zeros((BAND, RING), F32)
         first_bands(range(1, BANDS + 1), w1_ref, rows_ref, raw_ref, hid_ref)
         top_ref[...] = hid_ref[:, size : 2 * size, :]
         bottom_ref[...] = hid_ref[:, BANDS * size - 2 * CH : (BANDS + 1) * size - 2 * CH, :]
@@ -296,8 +292,8 @@
 
     @pl.when(jnp.logical_not(waits()))
     def _():
-        stage(raw_ref, 0, *above())
-        stage(raw_ref, BAND + TILE, *below())
+        stage(raw_ref, 0, above())
+        stage(raw_ref, BAND + TILE, below())
         stage_own(raw_ref, own_ref, sides_ref)
         first_bands(range(BANDS + 1), w1_ref, rows_ref, raw_ref, hid_ref)
         second_bands(range(BANDS), w2_ref, head_ref, raw_ref, hid_ref, res_ref)
@@ -308,19 +304,19 @@
         first, last = slice(0, 16), slice(TILE - 16, TILE)
         own = own_ref[first, :].astype(F32)[0:8], own_ref[last, :].astype(F32)[8:16]
         side = sides_ref[first, :].astype(F32)[0:8], sides_ref[last, :].astype(F32)[8:16]
-        near = [(s[:, :LANES], o, s[:, LANES:]) for s, o in zip(side, own)]
-        top = shifted(*[jnp.concatenate(pair, axis=0) for pair in zip(above(), near[0])])
-        bottom = shifted(*[jnp.concatenate(pair, axis=0) for pair in zip(near[1], below())])
+        near = [jnp.concatenate(pair, axis=1) for pair in zip(own, side)]
         grids = []
-        for raw, rows in ((top, rows_ref[16:32, :]), (bottom, rows_ref[32:48, :])):
-            grids.append(jnp.concatenate([x.astype(BF16) for x in raw] * 3 + [rows], axis=0))
-        w1 = jnp.concatenate([w1_ref[(dw + 1) * size - 2 * CH : (dw + 1) * size, :] for dw in range(3)], axis=0)
-        found = jnp.maximum(dot(w1, jnp.concatenate(grids, axis=1)), 0.0).astype(BF16)
+        for ring, rows in (
+            (jnp.concatenate([above(), near[0]], axis=0), rows_ref[16:32, :]),
+            (jnp.concatenate([near[1], below()], axis=0), rows_ref[32:48, :]),
+        ):
+            grids.append(jnp.concatenate([x.astype(BF16) for x in around(ring)] * 3 + [rows], axis=0))
+        found = jnp.maximum(dot(w1_ref[size - 2 * CH :, :], jnp.concatenate(grids, axis=1)), 0.0)
+        found = [[x[:, :TILE].astype(BF16) for x in around(found[:, n * RING : (n + 1) * RING])] for n in range(2)]
         hidden = []
         for dw in range(3):
-            two = found[dw * 2 * CH : (dw + 1) * 2 * CH]
-            upper = jnp.concatenate([two[:, :TILE], top_ref[dw]], axis=0)
-            lower = jnp.concatenate([bottom_ref[dw], two[:, TILE:]], axis=0)
+            upper = jnp.concatenate([found[0][dw], top_ref[dw]], axis=0)
+            lower = jnp.concatenate([bottom_ref[dw], found[1][dw]], axis=0)
             hidden.append(jnp.concatenate([upper, lower], axis=1))
         tail = jnp.concatenate([ones_rows(), jnp.zeros((16, TILE), BF16)], axis=0)
         hidden.append(jnp.concatenate([tail, tail], axis=1))
@@ -394,13 +390,13 @@
 
 
 WEIGHTS = (
-    shaped(3 * BAND * CH, K1),
-    shaped(48, TILE),
+    shaped(BAND * CH, K1),
+    shaped(48, RING),
     shaped(CH * BAND, K2),
     shaped(CH * BAND, LANES, dtype=F32),
 )
 ROOM = (
-    pltpu.VMEM((5, TILE + 2 * BAND, TILE), F32),
+    pltpu.VMEM((3, TILE + 2 * BAND, RING), F32),
     pltpu.VMEM((3, (BANDS + 1) * BAND * CH, TILE), BF16),
     pltpu.VMEM((TILE, TILE), F32),
 )
@@ -414,7 +410,7 @@
 
 def sides(own, core, chip, borders):
     slab = shaped(16, LANES)
-    shapes = (shaped(TILE, TILE),) + (slab,) * borders
+    shapes = (shaped(TILE, LANES),) + (slab,) * borders
     return call(sides_kernel, "sides", shapes, (own, core, chip))
 
 

time: 31.5 us -> 31.5 us (level)
  the two profiles are of different devices: /device:TPU:344 before, /device:TPU:328 now
where the time goes in v5:
time: 31.5 us; the launch traced here: 31.2 us
  starting transfers between devices  14.3 us (45%)
  waiting for transfers between devices  10.9 us (35%)
  Pallas kernels  5.15 us (16%)
  local copies, waits for them, and re-layouts  0.7 us (2%)
    ppermute x5, starting transfers between devices, swap(): return lax.ppermute(value, axis, pairs + [(j, i) for i, j in pairs])  12.3 us
    ppermute x5, waiting for transfers between devices, swap(): return lax.ppermute(value, axis, pairs + [(j, i) for i, j in pairs])  6.46 us
    pallas_call x7, Pallas kernels, call(): pl.pallas_call(kernel, name=name, out_shape=out_shape, in_specs=in_specs...  5.15 us
    ppermute x1, waiting for transfers between devices, from_step(): return lax.ppermute(value, axis, pairs)  4.4 us
    ppermute x1, starting transfers between devices, from_step(): return lax.ppermute(value, axis, pairs)  2.01 us
    unnamed x16, local copies, waits for them, and re-layouts  0.7 us
  transfers between devices with their start and end apart: 6, of which 4 were waited for; matrix products, arithmetic and copies ran while one was open for 0% of the time, Pallas kernels for 11%

profile of v5, /device:TPU:328, one launch (start us, length us, event | category | flops | bytes accessed | tf_op | source)
XLA Modules:
  0.0 31.2 jit_solution(10098071799617086896)
XLA Ops:
  0.0 4.1 %collective-permute-start.1 = (bf16[256,256]{1,0:T(8,128)(2,1)}, bf16[256,256]{1,0:T(8,128)(2,1)S(1)}, u32[]{:S(2)}, u32[]{:S(2)}) collective-permute-start(bf16[256,256]{1,0:T(8,128)(2,1)} %bitcast.4), channel_id=1, source_target_pairs={{1,2},{3,4},{5,6},{7,8},{9,10},{11,12},{13,14},{15,16},{17,18},{19... | collective-permute-start | bytes 393224 | tf_op jit(solution)/shard_map/ppermute | solution.py:466
  4.1 1.9 %collective-permute-start = (bf16[256,256]{1,0:T(8,128)(2,1)}, bf16[256,256]{1,0:T(8,128)(2,1)S(1)}, u32[]{:S(2)}, u32[]{:S(2)}) collective-permute-start(bf16[256,256]{1,0:T(8,128)(2,1)} %bitcast.5), channel_id=1, source_target_pairs={{0,1},{2,3},{4,5},{6,7},{8,9},{10,11},{12,13},{14,15},{16,17},{18,... | collective-permute-start | bytes 393224 | tf_op jit(solution)/shard_map/ppermute | solution.py:466
  6.1 0.0 copy-start.3
  6.1 0.0 copy-start.4
  6.1 0.0 copy-start.5
  6.1 0.6 %copy-done.2 = f32[16,9]{1,0:T(8,128)S(1)} copy-done((f32[16,9]{1,0:T(8,128)S(1)}, f32[16,9]{1,0:T(8,128)}, u32[]{:S(2)}) %copy-start.2) | copy-done | bytes 600
  6.7 0.0 copy-done.3
  6.8 0.0 copy-done.4
  6.8 0.0 copy-done.5
  6.8 0.8 %weights.1 = (bf16[128,160]{1,0:T(8,128)(2,1)S(1)}, bf16[48,384]{1,0:T(8,128)(2,1)S(1)}, bf16[128,512]{1,0:T(8,128)(2,1)S(1)}, f32[128,128]{1,0:T(8,128)S(1)}) custom-call(f32[16,9]{1,0:T(8,128)S(1)} %copy-done.2, f32[1,16]{1,0:T(1,128)S(1)} %bitcast.9, bf16[48,384]{1,0:T(8,128)(2,1)S(1)} %last_rows.1.rows_ref, bf16[9,16,16]{2,1,0:T(8,128)(2,1)S(1)} %copy-done.1, ...), custom_call_target="tpu_custom_call" | custom-call | tf_op jit(solution)/shard_map/weights/pallas_call | solution.py:375
  7.6 1.1 %collective-permute-done.1.chip_ref = bf16[256,256]{1,0:T(8,128)(2,1)S(1)} collective-permute-done((bf16[256,256]{1,0:T(8,128)(2,1)}, bf16[256,256]{1,0:T(8,128)(2,1)S(1)}, u32[]{:S(2)}, u32[]{:S(2)}) %collective-permute-start.1) | collective-permute-done | bytes 131104 | tf_op jit(solution)/shard_map/ppermute | solution.py:466
  8.7 0.0 collective-permute-done.core_ref
  8.7 0.1 sides.1
  8.8 0.7 %collective-permute-start.2 = (bf16[16,128]{1,0:T(8,128)(2,1)S(1)}, bf16[16,128]{1,0:T(8,128)(2,1)S(1)}, u32[]{:S(2)}, u32[]{:S(2)}) collective-permute-start(bf16[16,128]{1,0:T(8,128)(2,1)S(1)} %get-tuple-element.24), channel_id=1, source_target_pairs={{0,32},{32,0},{1,33},{33,1},{2,34},{34,2},{3,35},{35,3},{4,36},{36... | collective-permute-start | bytes 12296 | tf_op jit(solution)/shard_map/ppermute | solution.py:466
  9.5 3.7 %collective-permute-start.3 = (bf16[16,128]{1,0:T(8,128)(2,1)S(1)}, bf16[16,128]{1,0:T(8,128)(2,1)S(1)}, u32[]{:S(2)}, u32[]{:S(2)}) collective-permute-start(bf16[16,128]{1,0:T(8,128)(2,1)S(1)} %get-tuple-element.25), channel_id=1, source_target_pairs={{32,64},{64,32},{33,65},{65,33},{34,66},{66,34},{35,67},{67,35},{3... | collective-permute-start | bytes 12296 | tf_op jit(solution)/shard_map/ppermute | solution.py:466
  13.2 1.9 %collective-permute-start.4 = (bf16[16,128]{1,0:T(8,128)(2,1)S(1)}, bf16[16,128]{1,0:T(8,128)(2,1)S(1)}, u32[]{:S(2)}, u32[]{:S(2)}) collective-permute-start(bf16[16,128]{1,0:T(8,128)(2,1)S(1)} %get-tuple-element.26), channel_id=1, source_target_pairs={{64,96},{96,64},{65,97},{97,65},{66,98},{98,66},{67,99},{99,67},{6... | collective-permute-start | bytes 12296 | tf_op jit(solution)/shard_map/ppermute | solution.py:466
  15.1 2.1 %inner_rows.1 = (bf16[256,256]{1,0:T(8,128)(2,1)S(1)}, bf16[3,128,256]{2,1,0:T(8,128)(2,1)S(1)}, bf16[3,128,256]{2,1,0:T(8,128)(2,1)S(1)}) custom-call(bf16[256,256]{1,0:T(8,128)(2,1)S(1)} %bitcast.7, bf16[256,128]{1,0:T(8,128)(2,1)S(1)} %get-tuple-element.16.sides_ref, bf16[128,160]{1,0:T(8,128)(2,1)S(1)} %get-tuple-element.17.w1_ref, ...), custom_call_target="tpu_custom_call" | custom-call | flops 3221225472 | tf_op jit(solution)/shard_map/inner_rows/pallas_call | solution.py:375
  17.2 1.6 %collective-permute-done.3.refs_1_ = bf16[16,128]{1,0:T(8,128)(2,1)S(1)} collective-permute-done((bf16[16,128]{1,0:T(8,128)(2,1)S(1)}, bf16[16,128]{1,0:T(8,128)(2,1)S(1)}, u32[]{:S(2)}, u32[]{:S(2)}) %collective-permute-start.3) | collective-permute-done | bytes 4128 | tf_op jit(solution)/shard_map/ppermute | solution.py:466
  18.9 3.7 %collective-permute-done.4.refs_2_ = bf16[16,128]{1,0:T(8,128)(2,1)S(1)} collective-permute-done((bf16[16,128]{1,0:T(8,128)(2,1)S(1)}, bf16[16,128]{1,0:T(8,128)(2,1)S(1)}, u32[]{:S(2)}, u32[]{:S(2)}) %collective-permute-start.4) | collective-permute-done | bytes 4128 | tf_op jit(solution)/shard_map/ppermute | solution.py:466
  22.6 0.6 %outer_rows.1.image_ref = bf16[256,256]{1,0:T(8,128)(2,1)S(1)} custom-call(bf16[256,256]{1,0:T(8,128)(2,1)S(1)} %bitcast.8, bf16[256,128]{1,0:T(8,128)(2,1)S(1)} %get-tuple-element.16.sides_ref, bf16[128,160]{1,0:T(8,128)(2,1)S(1)} %get-tuple-element.17.w1_ref, bf16[48,384]{1,0:T(8,128)(2,1)S(1)} %get-tuple-element.18.rows_ref, ...), custom_call_target="tpu_custom_call", output_to_operand_aliasing={{}: (6, {})} | custom-call | flops 3221225472 | tf_op jit(solution)/shard_map/outer_rows/pallas_call | solution.py:375
  23.2 2.0 %collective-permute-start.5 = (bf16[256,256]{1,0:T(8,128)(2,1)S(1)}, bf16[256,256]{1,0:T(8,128)(2,1)S(1)}, u32[]{:S(2)}, u32[]{:S(2)}) collective-permute-start(bf16[256,256]{1,0:T(8,128)(2,1)S(1)} %outer_rows.1.image_ref), channel_id=1, source_target_pairs={{128,0},{256,128},{384,256},{129,1},{257,129},{385,257},{130,2},{2... | collective-permute-start | bytes 393224 | tf_op jit(solution)/shard_map/ppermute | solution.py:461
  25.2 0.4 %own_spectrum.1.own_ref = f32[2,256,256]{2,1,0:T(8,128)S(1)} custom-call(bf16[256,256]{1,0:T(8,128)(2,1)S(1)} %outer_rows.1.image_ref, bf16[128,256]{1,0:T(8,128)(2,1)S(1)} %copy-done.7, bf16[256,256]{1,0:T(8,128)(2,1)S(1)} %copy-done.6), custom_call_target="tpu_custom_call" | custom-call | flops 536870912 | tf_op jit(solution)/shard_map/own_spectrum/pallas_call | solution.py:375
  25.6 4.4 %collective-permute-done.5.image_ref = bf16[256,256]{1,0:T(8,128)(2,1)S(1)} collective-permute-done((bf16[256,256]{1,0:T(8,128)(2,1)S(1)}, bf16[256,256]{1,0:T(8,128)(2,1)S(1)}, u32[]{:S(2)}, u32[]{:S(2)}) %collective-permute-start.5) | collective-permute-done | bytes 131104 | tf_op jit(solution)/shard_map/ppermute | solution.py:461
  30.0 1.2 %cross_spectrum.1 = f32[1,2,256,256]{3,2,1,0:T(8,128)} custom-call(bf16[256,256]{1,0:T(8,128)(2,1)S(1)} %collective-permute-done.5.image_ref, bf16[128,256]{1,0:T(8,128)(2,1)S(1)} %copy-done.7, bf16[256,256]{1,0:T(8,128)(2,1)S(1)} %copy-done.6, f32[2,256,256]{2,1,0:T(8,128)S(1)} %own_spectrum.1.own_ref), custom_call_target="tpu_custom_call" | custom-call | flops 536870912 | tf_op jit(solution)/shard_map/cross_spectrum/pallas_call | solution.py:375
  (11 shorter events, 0.0 us)
Async XLA Ops:
  0.0 6.1 %copy-start.1 = (bf16[9,16,16]{2,1,0:T(8,128)(2,1)S(1)}, bf16[9,16,16]{2,1,0:T(8,128)(2,1)}, u32[]{:S(2)}) copy-start(bf16[9,16,16]{2,1,0:T(8,128)(2,1)} %second_ref.1) | copy-start | bytes 13828
  0.0 8.7 %collective-permute-start.1 = (bf16[256,256]{1,0:T(8,128)(2,1)}, bf16[256,256]{1,0:T(8,128)(2,1)S(1)}, u32[]{:S(2)}, u32[]{:S(2)}) collective-permute-start(bf16[256,256]{1,0:T(8,128)(2,1)} %bitcast.4), channel_id=1, source_target_pairs={{1,2},{3,4},{5,6},{7,8},{9,10},{11,12},{13,14},{15,16},{17,18},{19... | collective-permute-start | bytes 393224 | tf_op jit(solution)/shard_map/ppermute | solution.py:466
  4.1 4.6 %collective-permute-start = (bf16[256,256]{1,0:T(8,128)(2,1)}, bf16[256,256]{1,0:T(8,128)(2,1)S(1)}, u32[]{:S(2)}, u32[]{:S(2)}) collective-permute-start(bf16[256,256]{1,0:T(8,128)(2,1)} %bitcast.5), channel_id=1, source_target_pairs={{0,1},{2,3},{4,5},{6,7},{8,9},{10,11},{12,13},{14,15},{16,17},{18,... | collective-permute-start | bytes 393224 | tf_op jit(solution)/shard_map/ppermute | solution.py:466
  6.0 0.7 %copy-start.2 = (f32[16,9]{1,0:T(8,128)S(1)}, f32[16,9]{1,0:T(8,128)}, u32[]{:S(2)}) copy-start(f32[16,9]{1,0:T(8,128)} %first_ref.1) | copy-start | bytes 1732
  6.1 2.7 %copy-start = (bf16[1,256,256]{2,1,0:T(8,128)(2,1)S(1)}, bf16[1,256,256]{2,1,0:T(8,128)(2,1)}, u32[]{:S(2)}) copy-start(bf16[1,256,256]{2,1,0:T(8,128)(2,1)} %param.8) | copy-start | bytes 393220
  6.1 0.7 %copy-start.3 = (f32[16]{0:T(128)S(1)}, f32[16]{0:T(128)}, u32[]{:S(2)}) copy-start(f32[16]{0:T(128)} %param.10) | copy-start | bytes 196
  6.1 0.7 %copy-start.4 = (f32[16]{0:T(128)S(1)}, f32[16]{0:T(128)}, u32[]{:S(2)}) copy-start(f32[16]{0:T(128)} %param.12) | copy-start | bytes 196
  6.1 0.7 %copy-start.5 = (f32[16]{0:T(128)S(1)}, f32[16]{0:T(128)}, u32[]{:S(2)}) copy-start(f32[16]{0:T(128)} %param.13) | copy-start | bytes 196
  8.8 8.4 %collective-permute-start.2 = (bf16[16,128]{1,0:T(8,128)(2,1)S(1)}, bf16[16,128]{1,0:T(8,128)(2,1)S(1)}, u32[]{:S(2)}, u32[]{:S(2)}) collective-permute-start(bf16[16,128]{1,0:T(8,128)(2,1)S(1)} %get-tuple-element.24), channel_id=1, source_target_pairs={{0,32},{32,0},{1,33},{33,1},{2,34},{34,2},{3,35},{35,3},{4,36},{36... | collective-permute-start | bytes 12296 | tf_op jit(solution)/shard_map/ppermute | solution.py:466
  9.5 9.4 %collective-permute-start.3 = (bf16[16,128]{1,0:T(8,128)(2,1)S(1)}, bf16[16,128]{1,0:T(8,128)(2,1)S(1)}, u32[]{:S(2)}, u32[]{:S(2)}) collective-permute-start(bf16[16,128]{1,0:T(8,128)(2,1)S(1)} %get-tuple-element.25), channel_id=1, source_target_pairs={{32,64},{64,32},{33,65},{65,33},{34,66},{66,34},{35,67},{67,35},{3... | collective-permute-start | bytes 12296 | tf_op jit(solution)/shard_map/ppermute | solution.py:466
  13.2 9.4 %collective-permute-start.4 = (bf16[16,128]{1,0:T(8,128)(2,1)S(1)}, bf16[16,128]{1,0:T(8,128)(2,1)S(1)}, u32[]{:S(2)}, u32[]{:S(2)}) collective-permute-start(bf16[16,128]{1,0:T(8,128)(2,1)S(1)} %get-tuple-element.26), channel_id=1, source_target_pairs={{64,96},{96,64},{65,97},{97,65},{66,98},{98,66},{67,99},{99,67},{6... | collective-permute-start | bytes 12296 | tf_op jit(solution)/shard_map/ppermute | solution.py:466
  22.6 2.6 %copy-start.6 = (bf16[256,256]{1,0:T(8,128)(2,1)S(1)}, bf16[256,256]{1,0:T(8,128)(2,1)}, u32[]{:S(2)}) copy-start(bf16[256,256]{1,0:T(8,128)(2,1)} %constant.5.clone.down_ref) | copy-start | bytes 393220
  22.6 2.6 %copy-start.7 = (bf16[128,256]{1,0:T(8,128)(2,1)S(1)}, bf16[128,256]{1,0:T(8,128)(2,1)}, u32[]{:S(2)}) copy-start(bf16[128,256]{1,0:T(8,128)(2,1)} %constant.4.clone.across_ref) | copy-start | bytes 196612
  23.2 6.9 %collective-permute-start.5 = (bf16[256,256]{1,0:T(8,128)(2,1)S(1)}, bf16[256,256]{1,0:T(8,128)(2,1)S(1)}, u32[]{:S(2)}, u32[]{:S(2)}) collective-permute-start(bf16[256,256]{1,0:T(8,128)(2,1)S(1)} %outer_rows.1.image_ref), channel_id=1, source_target_pairs={{128,0},{256,128},{384,256},{129,1},{257,129},{385,257},{130,2},{2... | collective-permute-start | bytes 393224 | tf_op jit(solution)/shard_map/ppermute | solution.py:461

commit v6 on v5

--- a/solution.py
+++ b/solution.py
@@ -62,8 +62,16 @@
     return lax.axis_index(axis) == (lax.axis_size(axis) - 1 if last else 0)
 
 
+def deep_half():
+    return lax.axis_index("gz") >= lax.axis_size("gz") // 2
+
+
+def early():
+    return (lax.axis_index("gy") == 0) & deep_half()
+
+
 def waits():
-    return lax.axis_index("gy") > 0
+    return (lax.axis_index("gy") > 0) | deep_half()
 
 
 def last_rows_kernel(rows_out):
@@ -135,6 +143,42 @@
     second_weights(second_ref, second_bias_ref, head_ref, *outs[2:])
 
 
+def exchanges(borders, deep):
+    order = [[(k, k + 1), (k + 1, k)] for k in range(borders)]
+    if deep and borders > 1:
+        order[0] = [(1, 0), (2, 1)]
+        order[1] = [(0, 1), (1, 2)]
+    return order
+
+
+def downward(borders):
+    gy = lax.axis_index("gy")
+
+    def member(pairs, down):
+        found = False
+        for i, j in pairs:
+            if (j > i) == down:
+                found = found | (gy == i)
+        return found
+
+    plain, deep = exchanges(borders, False), exchanges(borders, True)
+    return [jnp.where(deep_half(), member(b, True), member(a, True)) for a, b in zip(plain, deep)]
+
+
+def arrived(borders, above):
+    gy = lax.axis_index("gy")
+
+    def member(pairs):
+        found = False
+        for i, j in pairs:
+            if (j > i) == above:
+                found = found | (gy == j)
+        return found
+
+    plain, deep = exchanges(borders, False), exchanges(borders, True)
+    return [jnp.where(deep_half(), member(b), member(a)) for a, b in zip(plain, deep)]
+
+
 def packed(r0, r1):
     rows = [r[:, k * LANES : (k + 1) * LANES] for r in (r0, r1) for k in range(3)]
     rows = jnp.concatenate(rows + [jnp.zeros((2, LANES), F32)], axis=0)
@@ -160,8 +204,8 @@
         if r in (0, TILE - 16):
             ring = jnp.concatenate([own_ref[r : r + 16, :].astype(F32), side], axis=1)
             ends[r] = packed(ring[0:1], ring[1:2]) if r == 0 else packed(ring[14:15], ring[15:16])
-    for k, slab_ref in enumerate(slab_refs):
-        slab_ref[...] = jnp.where(lax.axis_index("gy") == k, ends[TILE - 16], ends[0]).astype(BF16)
+    for slab_ref, down in zip(slab_refs, downward(len(slab_refs))):
+        slab_ref[...] = jnp.where(down, ends[TILE - 16], ends[0]).astype(BF16)
 
 
 def around(ring):
@@ -231,40 +275,45 @@
             res_ref[b * BAND : (b + 1) * BAND, :] = center + total[:, n * TILE : (n + 1) * TILE]
 
 
-def inner_kernel(
-    own_ref,
-    sides_ref,
-    w1_ref,
-    rows_ref,
-    w2_ref,
-    head_ref,
-    out_ref,
-    top_ref,
-    bottom_ref,
-    raw_ref,
-    hid_ref,
-    res_ref,
-):
+def inner_rows(own_ref, sides_ref, w1_ref, rows_ref, w2_ref, head_ref, outs, room):
     size = BAND * CH
-
-    @pl.when(waits())
+    out_ref, top_ref, bottom_ref = outs
+    raw_ref, hid_ref, res_ref = room
+    stage_own(raw_ref, own_ref, sides_ref)
+    for k in range(3):
+        raw_ref[k, BAND + TILE :, :] = jnp.zeros((BAND, RING), F32)
+    first_bands(range(1, BANDS + 1), w1_ref, rows_ref, raw_ref, hid_ref)
+    top_ref[...] = hid_ref[:, size : 2 * size, :]
+    bottom_ref[...] = hid_ref[:, BANDS * size - 2 * CH : (BANDS + 1) * size - 2 * CH, :]
+    second_bands(range(1, BANDS - 1), w2_ref, head_ref, raw_ref, hid_ref, res_ref)
+    res_ref[0:BAND, :] = jnp.zeros((BAND, TILE), F32)
+    res_ref[TILE - BAND :, :] = jnp.zeros((BAND, TILE), F32)
+    out_ref[...] = res_ref[...].astype(BF16)
+
+
+def early_kernel(*refs):
+    ins, refs = refs[:6], refs[6:]
+    count = (len(refs) - 6) // 2
+    slabs, outs, slab_outs, room = refs[:count], refs[count : count + 3], refs[count + 3 : -3], refs[-3:]
+
+    @pl.when(early())
     def _():
-        stage_own(raw_ref, own_ref, sides_ref)
-        for k in range(3):
-            raw_ref[k, BAND + TILE :, :] = jnp.zeros((BAND, RING), F32)
-        first_bands(range(1, BANDS + 1), w1_ref, rows_ref, raw_ref, hid_ref)
-        top_ref[...] = hid_ref[:, size : 2 * size, :]
-        bottom_ref[...] = hid_ref[:, BANDS * size - 2 * CH : (BANDS + 1) * size - 2 * CH, :]
-        second_bands(range(1, BANDS - 1), w2_ref, head_ref, raw_ref, hid_ref, res_ref)
-        res_ref[0:BAND, :] = jnp.zeros((BAND, TILE), F32)
-        res_ref[TILE - BAND :, :] = jnp.zeros((BAND, TILE), F32)
-        out_ref[...] = res_ref[...].astype(BF16)
-
-
-def border(border_refs, place):
+        inner_rows(*ins, outs, room)
+
+    for slab, out in zip(slabs, slab_outs):
+        out[...] = slab[...]
+
+
+def inner_kernel(*refs):
+    @pl.when(waits() & jnp.logical_not(early()))
+    def _():
+        inner_rows(*refs[:6], refs[9:12], refs[12:])
+
+
+def border(border_refs, above):
     value = jnp.zeros((16, LANES), F32)
-    for k, ref in enumerate(border_refs):
-        value = jnp.where(place == k, ref[...].astype(F32), value)
+    for ref, here in zip(border_refs, arrived(len(border_refs), above)):
+        value = jnp.where(here, ref[...].astype(F32), value)
     return value
 
 
@@ -285,10 +334,10 @@
     size = BAND * CH
 
     def above():
-        return unpacked(border(borders, gy - 1), 6)
+        return unpacked(border(borders, True), 6)
 
     def below():
-        return unpacked(border(borders, gy), 0)
+        return unpacked(border(borders, False), 0)
 
     @pl.when(jnp.logical_not(waits()))
     def _():
@@ -414,14 +463,19 @@
     return call(sides_kernel, "sides", shapes, (own, core, chip))
 
 
-def inner(own, side, weights):
+INSIDE = (shaped(TILE, TILE), shaped(3, BAND * CH, TILE), shaped(3, BAND * CH, TILE))
+
+
+def inner_early(own, side, weights, slabs):
+    shapes = INSIDE + (shaped(16, LANES),) * len(slabs)
+    outs = call(early_kernel, "early_rows", shapes, (own, side, *weights, *slabs), scratch=ROOM)
+    return outs[:3], outs[3:]
+
+
+def inner(own, side, weights, inside):
+    args = (own, side, *weights, *inside)
     return call(
-        inner_kernel,
-        "inner_rows",
-        (shaped(TILE, TILE), shaped(3, BAND * CH, TILE), shaped(3, BAND * CH, TILE)),
-        (own, side, *weights),
-        scratch=ROOM,
-        flops=3 << 30,
+        inner_kernel, "inner_rows", INSIDE, args, scratch=ROOM, flops=3 << 30, aliases={6: 0, 7: 1, 8: 2}
     )
 
 
@@ -466,6 +520,15 @@
     return lax.ppermute(value, axis, pairs + [(j, i) for i, j in pairs])
 
 
+def exchange(slab, place):
+    depth, rows = lax.axis_size("gz"), lax.axis_size("gy")
+    pairs = []
+    for z in range(depth):
+        for i, j in exchanges(rows - 1, z >= depth // 2)[place]:
+            pairs.append((z * rows + i, z * rows + j))
+    return lax.ppermute(slab, ("gz", "gy"), pairs)
+
+
 def on_device(section, first_kernel, first_bias, second_kernel, second_bias, head_weight):
     own = section[0]
     columns, rows = lax.axis_size("gx"), lax.axis_size("gy")
@@ -474,8 +537,9 @@
     given = (first_kernel, first_bias[None], second_kernel, second_bias[None], head_weight[None])
     weights = prepare(*given)
     side, *slabs = sides(own, core, chip, rows - 1)
-    borders = [swap(slab, "gy", [k]) for k, slab in enumerate(slabs)]
-    inside = inner(own, side, weights)
+    inside, slabs = inner_early(own, side, weights, slabs)
+    borders = [exchange(slab, k) for k, slab in enumerate(slabs)]
+    inside = inner(own, side, weights, inside)
     restored = outer(own, side, weights, inside, borders)
     across, down = dft_tables()
     later = from_step(restored, "gz", -1)

time: 31.5 us -> 31.1 us (0.987)
  the two profiles are of different devices: /device:TPU:328 before, /device:TPU:72 now
where the time goes in v6:
time: 31.1 us; the launch traced here: 30.8 us
  starting transfers between devices  18.4 us (59%)
  waiting for transfers between devices  6.23 us (20%)
  Pallas kernels  5.31 us (17%)
  local copies, waits for them, and re-layouts  0.7 us (2%)
    ppermute x3, starting transfers between devices, exchange(): return lax.ppermute(slab, ('gz', 'gy'), pairs)  10.4 us
    ppermute x2, starting transfers between devices, swap(): return lax.ppermute(value, axis, pairs + [(j, i) for i, j in pairs])  6.03 us
    pallas_call x8, Pallas kernels, call(): pl.pallas_call(kernel, name=name, out_shape=out_shape, in_specs=in_specs...  5.31 us
    ppermute x1, waiting for transfers between devices, from_step(): return lax.ppermute(value, axis, pairs)  4.5 us
    ppermute x1, starting transfers between devices, from_step(): return lax.ppermute(value, axis, pairs)  1.92 us
    ppermute x2, waiting for transfers between devices, swap(): return lax.ppermute(value, axis, pairs + [(j, i) for i, j in pairs])  1.12 us
    unnamed x16, local copies, waits for them, and re-layouts  0.7 us
  transfers between devices with their start and end apart: 6, of which 3 were waited for; matrix products, arithmetic and copies ran while one was open for 0% of the time, Pallas kernels for 4%

profile of v6, /device:TPU:72, one launch (start us, length us, event | category | flops | bytes accessed | tf_op | source)
XLA Modules:
  0.0 30.8 jit_solution(14241698834056988833)
XLA Ops:
  0.0 4.1 %collective-permute-start.1 = (bf16[256,256]{1,0:T(8,128)(2,1)}, bf16[256,256]{1,0:T(8,128)(2,1)S(1)}, u32[]{:S(2)}, u32[]{:S(2)}) collective-permute-start(bf16[256,256]{1,0:T(8,128)(2,1)} %bitcast.4), channel_id=1, source_target_pairs={{1,2},{3,4},{5,6},{7,8},{9,10},{11,12},{13,14},{15,16},{17,18},{19... | collective-permute-start | bytes 393224 | tf_op jit(solution)/shard_map/ppermute | solution.py:520
  4.1 1.9 %collective-permute-start = (bf16[256,256]{1,0:T(8,128)(2,1)}, bf16[256,256]{1,0:T(8,128)(2,1)S(1)}, u32[]{:S(2)}, u32[]{:S(2)}) collective-permute-start(bf16[256,256]{1,0:T(8,128)(2,1)} %bitcast.5), channel_id=1, source_target_pairs={{0,1},{2,3},{4,5},{6,7},{8,9},{10,11},{12,13},{14,15},{16,17},{18,... | collective-permute-start | bytes 393224 | tf_op jit(solution)/shard_map/ppermute | solution.py:520
  6.1 0.0 copy-start.3
  6.1 0.0 copy-start.4
  6.1 0.0 copy-start.5
  6.1 0.6 %copy-done.2 = f32[16,9]{1,0:T(8,128)S(1)} copy-done((f32[16,9]{1,0:T(8,128)S(1)}, f32[16,9]{1,0:T(8,128)}, u32[]{:S(2)}) %copy-start.2) | copy-done | bytes 600
  6.7 0.0 copy-done.3
  6.8 0.0 copy-done.4
  6.8 0.0 copy-done.5
  6.8 0.8 %weights.1 = (bf16[128,160]{1,0:T(8,128)(2,1)S(1)}, bf16[48,384]{1,0:T(8,128)(2,1)S(1)}, bf16[128,512]{1,0:T(8,128)(2,1)S(1)}, f32[128,128]{1,0:T(8,128)S(1)}) custom-call(f32[16,9]{1,0:T(8,128)S(1)} %copy-done.2, f32[1,16]{1,0:T(1,128)S(1)} %bitcast.10, bf16[48,384]{1,0:T(8,128)(2,1)S(1)} %last_rows.1.rows_ref, bf16[9,16,16]{2,1,0:T(8,128)(2,1)S(1)} %copy-done.1, ...), custom_call_target="tpu_custom_call" | custom-call | tf_op jit(solution)/shard_map/weights/pallas_call | solution.py:424
  7.6 1.1 %collective-permute-done.1.chip_ref = bf16[256,256]{1,0:T(8,128)(2,1)S(1)} collective-permute-done((bf16[256,256]{1,0:T(8,128)(2,1)}, bf16[256,256]{1,0:T(8,128)(2,1)S(1)}, u32[]{:S(2)}, u32[]{:S(2)}) %collective-permute-start.1) | collective-permute-done | bytes 131104 | tf_op jit(solution)/shard_map/ppermute | solution.py:520
  8.7 0.0 collective-permute-done.core_ref
  8.7 0.1 sides.1
  8.8 2.3 %early_rows.1 = (bf16[256,256]{1,0:T(8,128)(2,1)S(1)}, bf16[3,128,256]{2,1,0:T(8,128)(2,1)S(1)}, bf16[3,128,256]{2,1,0:T(8,128)(2,1)S(1)}, bf16[16,128]{1,0:T(8,...) custom-call(bf16[256,256]{1,0:T(8,128)(2,1)S(1)} %bitcast.7, ...), custom_call_target="tpu_custom_call" | custom-call | tf_op jit(solution)/shard_map/early_rows/pallas_call | solution.py:424
  11.1 1.3 %collective-permute-start.2 = (bf16[16,128]{1,0:T(8,128)(2,1)S(1)}, bf16[16,128]{1,0:T(8,128)(2,1)S(1)}, u32[]{:S(2)}, u32[]{:S(2)}) collective-permute-start(bf16[16,128]{1,0:T(8,128)(2,1)S(1)} %get-tuple-element.36), channel_id=1, source_target_pairs={{0,32},{32,0},{128,160},{160,128},{288,256},{320,288},{416,384},{4... | collective-permute-start | bytes 12296 | tf_op jit(solution)/shard_map/ppermute | solution.py:529
  12.4 8.5 %collective-permute-start.3 = (bf16[16,128]{1,0:T(8,128)(2,1)S(1)}, bf16[16,128]{1,0:T(8,128)(2,1)S(1)}, u32[]{:S(2)}, u32[]{:S(2)}) collective-permute-start(bf16[16,128]{1,0:T(8,128)(2,1)S(1)} %get-tuple-element.37), channel_id=1, source_target_pairs={{32,64},{64,32},{160,192},{192,160},{256,288},{288,320},{384,416},... | collective-permute-start | bytes 12296 | tf_op jit(solution)/shard_map/ppermute | solution.py:529
  20.8 0.7 %collective-permute-start.4 = (bf16[16,128]{1,0:T(8,128)(2,1)S(1)}, bf16[16,128]{1,0:T(8,128)(2,1)S(1)}, u32[]{:S(2)}, u32[]{:S(2)}) collective-permute-start(bf16[16,128]{1,0:T(8,128)(2,1)S(1)} %get-tuple-element.38), channel_id=1, source_target_pairs={{64,96},{96,64},{192,224},{224,192},{320,352},{352,320},{448,480},... | collective-permute-start | bytes 12296 | tf_op jit(solution)/shard_map/ppermute | solution.py:529
  21.5 0.0 collective-permute-done.2.refs_0_
  21.5 0.6 %collective-permute-done.3.refs_1_ = bf16[16,128]{1,0:T(8,128)(2,1)S(1)} collective-permute-done((bf16[16,128]{1,0:T(8,128)(2,1)S(1)}, bf16[16,128]{1,0:T(8,128)(2,1)S(1)}, u32[]{:S(2)}, u32[]{:S(2)}) %collective-permute-start.3) | collective-permute-done | bytes 4128 | tf_op jit(solution)/shard_map/ppermute | solution.py:529
  22.1 0.6 %outer_rows.1.image_ref = bf16[256,256]{1,0:T(8,128)(2,1)S(1)} custom-call(bf16[256,256]{1,0:T(8,128)(2,1)S(1)} %bitcast.9, bf16[256,128]{1,0:T(8,128)(2,1)S(1)} %get-tuple-element.22.refs_1_.sides_ref, bf16[128,160]{1,0:T(8,128)(2,1)S(1)} %get-tuple-element.23.refs_2_.w1_ref, ...), custom_call_target="tpu_custom_call", output_to_operand_aliasing={{}: (6, {})} | custom-call | flops 3221225472 | tf_op jit(solution)/shard_map/outer_rows/pallas_call | solution.py:424
  22.7 1.9 %collective-permute-start.5 = (bf16[256,256]{1,0:T(8,128)(2,1)S(1)}, bf16[256,256]{1,0:T(8,128)(2,1)S(1)}, u32[]{:S(2)}, u32[]{:S(2)}) collective-permute-start(bf16[256,256]{1,0:T(8,128)(2,1)S(1)} %outer_rows.1.image_ref), channel_id=1, source_target_pairs={{128,0},{256,128},{384,256},{129,1},{257,129},{385,257},{130,2},{2... | collective-permute-start | bytes 393224 | tf_op jit(solution)/shard_map/ppermute | solution.py:515
  24.7 0.4 %own_spectrum.1.own_ref = f32[2,256,256]{2,1,0:T(8,128)S(1)} custom-call(bf16[256,256]{1,0:T(8,128)(2,1)S(1)} %outer_rows.1.image_ref, bf16[128,256]{1,0:T(8,128)(2,1)S(1)} %copy-done.7, bf16[256,256]{1,0:T(8,128)(2,1)S(1)} %copy-done.6), custom_call_target="tpu_custom_call" | custom-call | flops 536870912 | tf_op jit(solution)/shard_map/own_spectrum/pallas_call | solution.py:424
  25.1 4.5 %collective-permute-done.5.image_ref = bf16[256,256]{1,0:T(8,128)(2,1)S(1)} collective-permute-done((bf16[256,256]{1,0:T(8,128)(2,1)S(1)}, bf16[256,256]{1,0:T(8,128)(2,1)S(1)}, u32[]{:S(2)}, u32[]{:S(2)}) %collective-permute-start.5) | collective-permute-done | bytes 131104 | tf_op jit(solution)/shard_map/ppermute | solution.py:515
  29.6 1.2 %cross_spectrum.1 = f32[1,2,256,256]{3,2,1,0:T(8,128)} custom-call(bf16[256,256]{1,0:T(8,128)(2,1)S(1)} %collective-permute-done.5.image_ref, bf16[128,256]{1,0:T(8,128)(2,1)S(1)} %copy-done.7, bf16[256,256]{1,0:T(8,128)(2,1)S(1)} %copy-done.6, f32[2,256,256]{2,1,0:T(8,128)S(1)} %own_spectrum.1.own_ref), custom_call_target="tpu_custom_call" | custom-call | flops 536870912 | tf_op jit(solution)/shard_map/cross_spectrum/pallas_call | solution.py:424
  (12 shorter events, 0.1 us)
Async XLA Ops:
  0.0 6.1 %copy-start.1 = (bf16[9,16,16]{2,1,0:T(8,128)(2,1)S(1)}, bf16[9,16,16]{2,1,0:T(8,128)(2,1)}, u32[]{:S(2)}) copy-start(bf16[9,16,16]{2,1,0:T(8,128)(2,1)} %second_ref.1) | copy-start | bytes 13828
  0.0 8.7 %collective-permute-start.1 = (bf16[256,256]{1,0:T(8,128)(2,1)}, bf16[256,256]{1,0:T(8,128)(2,1)S(1)}, u32[]{:S(2)}, u32[]{:S(2)}) collective-permute-start(bf16[256,256]{1,0:T(8,128)(2,1)} %bitcast.4), channel_id=1, source_target_pairs={{1,2},{3,4},{5,6},{7,8},{9,10},{11,12},{13,14},{15,16},{17,18},{19... | collective-permute-start | bytes 393224 | tf_op jit(solution)/shard_map/ppermute | solution.py:520
  4.1 4.6 %collective-permute-start = (bf16[256,256]{1,0:T(8,128)(2,1)}, bf16[256,256]{1,0:T(8,128)(2,1)S(1)}, u32[]{:S(2)}, u32[]{:S(2)}) collective-permute-start(bf16[256,256]{1,0:T(8,128)(2,1)} %bitcast.5), channel_id=1, source_target_pairs={{0,1},{2,3},{4,5},{6,7},{8,9},{10,11},{12,13},{14,15},{16,17},{18,... | collective-permute-start | bytes 393224 | tf_op jit(solution)/shard_map/ppermute | solution.py:520
  6.0 0.7 %copy-start.2 = (f32[16,9]{1,0:T(8,128)S(1)}, f32[16,9]{1,0:T(8,128)}, u32[]{:S(2)}) copy-start(f32[16,9]{1,0:T(8,128)} %first_ref.1) | copy-start | bytes 1732
  6.1 2.7 %copy-start = (bf16[1,256,256]{2,1,0:T(8,128)(2,1)S(1)}, bf16[1,256,256]{2,1,0:T(8,128)(2,1)}, u32[]{:S(2)}) copy-start(bf16[1,256,256]{2,1,0:T(8,128)(2,1)} %param.8) | copy-start | bytes 393220
  6.1 0.7 %copy-start.3 = (f32[16]{0:T(128)S(1)}, f32[16]{0:T(128)}, u32[]{:S(2)}) copy-start(f32[16]{0:T(128)} %param.10) | copy-start | bytes 196
  6.1 0.7 %copy-start.4 = (f32[16]{0:T(128)S(1)}, f32[16]{0:T(128)}, u32[]{:S(2)}) copy-start(f32[16]{0:T(128)} %param.12) | copy-start | bytes 196
  6.1 0.7 %copy-start.5 = (f32[16]{0:T(128)S(1)}, f32[16]{0:T(128)}, u32[]{:S(2)}) copy-start(f32[16]{0:T(128)} %param.13) | copy-start | bytes 196
  11.1 10.5 %collective-permute-start.2 = (bf16[16,128]{1,0:T(8,128)(2,1)S(1)}, bf16[16,128]{1,0:T(8,128)(2,1)S(1)}, u32[]{:S(2)}, u32[]{:S(2)}) collective-permute-start(bf16[16,128]{1,0:T(8,128)(2,1)S(1)} %get-tuple-element.36), channel_id=1, source_target_pairs={{0,32},{32,0},{128,160},{160,128},{288,256},{320,288},{416,384},{4... | collective-permute-start | bytes 12296 | tf_op jit(solution)/shard_map/ppermute | solution.py:529
  12.4 9.8 %collective-permute-start.3 = (bf16[16,128]{1,0:T(8,128)(2,1)S(1)}, bf16[16,128]{1,0:T(8,128)(2,1)S(1)}, u32[]{:S(2)}, u32[]{:S(2)}) collective-permute-start(bf16[16,128]{1,0:T(8,128)(2,1)S(1)} %get-tuple-element.37), channel_id=1, source_target_pairs={{32,64},{64,32},{160,192},{192,160},{256,288},{288,320},{384,416},... | collective-permute-start | bytes 12296 | tf_op jit(solution)/shard_map/ppermute | solution.py:529
  20.8 1.3 %collective-permute-start.4 = (bf16[16,128]{1,0:T(8,128)(2,1)S(1)}, bf16[16,128]{1,0:T(8,128)(2,1)S(1)}, u32[]{:S(2)}, u32[]{:S(2)}) collective-permute-start(bf16[16,128]{1,0:T(8,128)(2,1)S(1)} %get-tuple-element.38), channel_id=1, source_target_pairs={{64,96},{96,64},{192,224},{224,192},{320,352},{352,320},{448,480},... | collective-permute-start | bytes 12296 | tf_op jit(solution)/shard_map/ppermute | solution.py:529
  22.1 2.5 %copy-start.6 = (bf16[256,256]{1,0:T(8,128)(2,1)S(1)}, bf16[256,256]{1,0:T(8,128)(2,1)}, u32[]{:S(2)}) copy-start(bf16[256,256]{1,0:T(8,128)(2,1)} %constant.5.clone.down_ref) | copy-start | bytes 393220
  22.1 2.5 %copy-start.7 = (bf16[128,256]{1,0:T(8,128)(2,1)S(1)}, bf16[128,256]{1,0:T(8,128)(2,1)}, u32[]{:S(2)}) copy-start(bf16[128,256]{1,0:T(8,128)(2,1)} %constant.4.clone.across_ref) | copy-start | bytes 196612
  22.7 6.9 %collective-permute-start.5 = (bf16[256,256]{1,0:T(8,128)(2,1)S(1)}, bf16[256,256]{1,0:T(8,128)(2,1)S(1)}, u32[]{:S(2)}, u32[]{:S(2)}) collective-permute-start(bf16[256,256]{1,0:T(8,128)(2,1)S(1)} %outer_rows.1.image_ref), channel_id=1, source_target_pairs={{128,0},{256,128},{384,256},{129,1},{257,129},{385,257},{130,2},{2... | collective-permute-start | bytes 393224 | tf_op jit(solution)/shard_map/ppermute | solution.py:515

commit v7 on v6

--- a/solution.py
+++ b/solution.py
@@ -309,6 +309,11 @@
     def _():
         inner_rows(*refs[:6], refs[9:12], refs[12:])
 
+    @pl.when(early())
+    def _():
+        for found, out in zip(refs[6:9], refs[9:12]):
+            out[...] = found[...]
+
 
 def border(border_refs, above):
     value = jnp.zeros((16, LANES), F32)
@@ -351,6 +356,7 @@
     @pl.when(waits())
     def _():
         first, last = slice(0, 16), slice(TILE - 16, TILE)
+        out_ref[16 : TILE - 16, :] = inner_ref[16 : TILE - 16, :]
         own = own_ref[first, :].astype(F32)[0:8], own_ref[last, :].astype(F32)[8:16]
         side = sides_ref[first, :].astype(F32)[0:8], sides_ref[last, :].astype(F32)[8:16]
         near = [jnp.concatenate(pair, axis=1) for pair in zip(own, side)]
@@ -420,14 +426,13 @@
     return pl.BlockSpec(shape, lambda: (0,) * len(shape), memory_space=VMEM)
 
 
-def call(kernel, name, out_shape, args, scratch=(), flops=0, in_specs=None, out_specs=None, aliases=None):
+def call(kernel, name, out_shape, args, scratch=(), flops=0, in_specs=None, out_specs=None):
     return pl.pallas_call(
         kernel,
         name=name,
         out_shape=out_shape,
         in_specs=in_specs or [full(a.shape) for a in args],
         out_specs=out_specs or jax.tree.map(lambda o: full(o.shape), out_shape),
-        input_output_aliases=aliases or {},
         scratch_shapes=list(scratch),
         compiler_params=PARAMS,
         cost_estimate=pl.CostEstimate(flops=flops, bytes_accessed=0, transcendentals=0),
@@ -475,7 +480,7 @@
 def inner(own, side, weights, inside):
     args = (own, side, *weights, *inside)
     return call(
-        inner_kernel, "inner_rows", INSIDE, args, scratch=ROOM, flops=3 << 30, aliases={6: 0, 7: 1, 8: 2}
+        inner_kernel, "inner_rows", INSIDE, args, scratch=ROOM, flops=3 << 30
     )
 
 
@@ -487,7 +492,6 @@
         (own, side, *weights, *inside, *borders),
         scratch=ROOM,
         flops=3 << 30,
-        aliases={6: 0},
     )
 
 

time: 31.1 us -> 31.1 us (level)
  no operation moved by 1% of the time
where the time goes in v7:
time: 31.1 us; the launch traced here: 30.8 us
  starting transfers between devices  18.4 us (59%)
  waiting for transfers between devices  6.2 us (20%)
  Pallas kernels  5.35 us (17%)
  local copies, waits for them, and re-layouts  0.7 us (2%)
    ppermute x3, starting transfers between devices, exchange(): return lax.ppermute(slab, ('gz', 'gy'), pairs)  10.4 us
    ppermute x2, starting transfers between devices, swap(): return lax.ppermute(value, axis, pairs + [(j, i) for i, j in pairs])  6.03 us
    pallas_call x8, Pallas kernels, call(): pl.pallas_call(kernel, name=name, out_shape=out_shape, in_specs=in_specs...  5.35 us
    ppermute x1, waiting for transfers between devices, from_step(): return lax.ppermute(value, axis, pairs)  4.5 us
    ppermute x1, starting transfers between devices, from_step(): return lax.ppermute(value, axis, pairs)  1.92 us
    ppermute x2, waiting for transfers between devices, swap(): return lax.ppermute(value, axis, pairs + [(j, i) for i, j in pairs])  1.12 us
    unnamed x16, local copies, waits for them, and re-layouts  0.7 us
  transfers between devices with their start and end apart: 6, of which 3 were waited for; matrix products, arithmetic and copies ran while one was open for 0% of the time, Pallas kernels for 4%

profile of v7, /device:TPU:72, one launch (start us, length us, event | category | flops | bytes accessed | tf_op | source)
XLA Modules:
  0.0 30.8 jit_solution(10307155901817093124)
XLA Ops:
  0.0 4.1 %collective-permute-start.1 = (bf16[256,256]{1,0:T(8,128)(2,1)}, bf16[256,256]{1,0:T(8,128)(2,1)S(1)}, u32[]{:S(2)}, u32[]{:S(2)}) collective-permute-start(bf16[256,256]{1,0:T(8,128)(2,1)} %bitcast.4), channel_id=1, source_target_pairs={{1,2},{3,4},{5,6},{7,8},{9,10},{11,12},{13,14},{15,16},{17,18},{19... | collective-permute-start | bytes 393224 | tf_op jit(solution)/shard_map/ppermute | solution.py:524
  4.1 1.9 %collective-permute-start = (bf16[256,256]{1,0:T(8,128)(2,1)}, bf16[256,256]{1,0:T(8,128)(2,1)S(1)}, u32[]{:S(2)}, u32[]{:S(2)}) collective-permute-start(bf16[256,256]{1,0:T(8,128)(2,1)} %bitcast.5), channel_id=1, source_target_pairs={{0,1},{2,3},{4,5},{6,7},{8,9},{10,11},{12,13},{14,15},{16,17},{18,... | collective-permute-start | bytes 393224 | tf_op jit(solution)/shard_map/ppermute | solution.py:524
  6.1 0.0 copy-start.3
  6.1 0.0 copy-start.4
  6.1 0.0 copy-start.5
  6.1 0.6 %copy-done.2 = f32[16,9]{1,0:T(8,128)S(1)} copy-done((f32[16,9]{1,0:T(8,128)S(1)}, f32[16,9]{1,0:T(8,128)}, u32[]{:S(2)}) %copy-start.2) | copy-done | bytes 600
  6.7 0.0 copy-done.3
  6.8 0.0 copy-done.4
  6.8 0.0 copy-done.5
  6.8 0.8 %weights.1 = (bf16[128,160]{1,0:T(8,128)(2,1)S(1)}, bf16[48,384]{1,0:T(8,128)(2,1)S(1)}, bf16[128,512]{1,0:T(8,128)(2,1)S(1)}, f32[128,128]{1,0:T(8,128)S(1)}) custom-call(f32[16,9]{1,0:T(8,128)S(1)} %copy-done.2, f32[1,16]{1,0:T(1,128)S(1)} %bitcast.10, bf16[48,384]{1,0:T(8,128)(2,1)S(1)} %last_rows.1.rows_ref, bf16[9,16,16]{2,1,0:T(8,128)(2,1)S(1)} %copy-done.1, ...), custom_call_target="tpu_custom_call" | custom-call | tf_op jit(solution)/shard_map/weights/pallas_call | solution.py:430
  7.6 1.1 %collective-permute-done.1.chip_ref = bf16[256,256]{1,0:T(8,128)(2,1)S(1)} collective-permute-done((bf16[256,256]{1,0:T(8,128)(2,1)}, bf16[256,256]{1,0:T(8,128)(2,1)S(1)}, u32[]{:S(2)}, u32[]{:S(2)}) %collective-permute-start.1) | collective-permute-done | bytes 131104 | tf_op jit(solution)/shard_map/ppermute | solution.py:524
  8.7 0.0 collective-permute-done.core_ref
  8.7 0.1 sides.1
  8.8 2.3 %early_rows.1 = (bf16[256,256]{1,0:T(8,128)(2,1)S(1)}, bf16[3,128,256]{2,1,0:T(8,128)(2,1)S(1)}, bf16[3,128,256]{2,1,0:T(8,128)(2,1)S(1)}, bf16[16,128]{1,0:T(8,...) custom-call(bf16[256,256]{1,0:T(8,128)(2,1)S(1)} %bitcast.7, ...), custom_call_target="tpu_custom_call" | custom-call | tf_op jit(solution)/shard_map/early_rows/pallas_call | solution.py:430
  11.1 1.3 %collective-permute-start.2 = (bf16[16,128]{1,0:T(8,128)(2,1)S(1)}, bf16[16,128]{1,0:T(8,128)(2,1)S(1)}, u32[]{:S(2)}, u32[]{:S(2)}) collective-permute-start(bf16[16,128]{1,0:T(8,128)(2,1)S(1)} %get-tuple-element.36), channel_id=1, source_target_pairs={{0,32},{32,0},{128,160},{160,128},{288,256},{320,288},{416,384},{4... | collective-permute-start | bytes 12296 | tf_op jit(solution)/shard_map/ppermute | solution.py:533
  12.4 8.5 %collective-permute-start.3 = (bf16[16,128]{1,0:T(8,128)(2,1)S(1)}, bf16[16,128]{1,0:T(8,128)(2,1)S(1)}, u32[]{:S(2)}, u32[]{:S(2)}) collective-permute-start(bf16[16,128]{1,0:T(8,128)(2,1)S(1)} %get-tuple-element.37), channel_id=1, source_target_pairs={{32,64},{64,32},{160,192},{192,160},{256,288},{288,320},{384,416},... | collective-permute-start | bytes 12296 | tf_op jit(solution)/shard_map/ppermute | solution.py:533
  20.8 0.7 %collective-permute-start.4 = (bf16[16,128]{1,0:T(8,128)(2,1)S(1)}, bf16[16,128]{1,0:T(8,128)(2,1)S(1)}, u32[]{:S(2)}, u32[]{:S(2)}) collective-permute-start(bf16[16,128]{1,0:T(8,128)(2,1)S(1)} %get-tuple-element.38), channel_id=1, source_target_pairs={{64,96},{96,64},{192,224},{224,192},{320,352},{352,320},{448,480},... | collective-permute-start | bytes 12296 | tf_op jit(solution)/shard_map/ppermute | solution.py:533
  21.5 0.1 inner_rows.1
  21.6 0.6 %collective-permute-done.3.refs_1_ = bf16[16,128]{1,0:T(8,128)(2,1)S(1)} collective-permute-done((bf16[16,128]{1,0:T(8,128)(2,1)S(1)}, bf16[16,128]{1,0:T(8,128)(2,1)S(1)}, u32[]{:S(2)}, u32[]{:S(2)}) %collective-permute-start.3) | collective-permute-done | bytes 4128 | tf_op jit(solution)/shard_map/ppermute | solution.py:533
  22.1 0.6 %outer_rows.1.image_ref = bf16[256,256]{1,0:T(8,128)(2,1)S(1)} custom-call(bf16[256,256]{1,0:T(8,128)(2,1)S(1)} %bitcast.9, bf16[256,128]{1,0:T(8,128)(2,1)S(1)} %get-tuple-element.22.refs_1_.sides_ref, bf16[128,160]{1,0:T(8,128)(2,1)S(1)} %get-tuple-element.23.refs_2_.w1_ref, bf16[48,384]{1,0:T(8,128)(2,1)S(1)} %get-tuple-element.24.refs_3_.rows_ref, ...), custom_call_target="tpu_custom_call" | custom-call | flops 3221225472 | tf_op jit(solution)/shard_map/outer_rows/pallas_call | solution.py:430
  22.7 1.9 %collective-permute-start.5 = (bf16[256,256]{1,0:T(8,128)(2,1)S(1)}, bf16[256,256]{1,0:T(8,128)(2,1)S(1)}, u32[]{:S(2)}, u32[]{:S(2)}) collective-permute-start(bf16[256,256]{1,0:T(8,128)(2,1)S(1)} %outer_rows.1.image_ref), channel_id=1, source_target_pairs={{128,0},{256,128},{384,256},{129,1},{257,129},{385,257},{130,2},{2... | collective-permute-start | bytes 393224 | tf_op jit(solution)/shard_map/ppermute | solution.py:519
  24.7 0.4 %own_spectrum.1.own_ref = f32[2,256,256]{2,1,0:T(8,128)S(1)} custom-call(bf16[256,256]{1,0:T(8,128)(2,1)S(1)} %outer_rows.1.image_ref, bf16[128,256]{1,0:T(8,128)(2,1)S(1)} %copy-done.7, bf16[256,256]{1,0:T(8,128)(2,1)S(1)} %copy-done.6), custom_call_target="tpu_custom_call" | custom-call | flops 536870912 | tf_op jit(solution)/shard_map/own_spectrum/pallas_call | solution.py:430
  25.1 4.5 %collective-permute-done.5.image_ref = bf16[256,256]{1,0:T(8,128)(2,1)S(1)} collective-permute-done((bf16[256,256]{1,0:T(8,128)(2,1)S(1)}, bf16[256,256]{1,0:T(8,128)(2,1)S(1)}, u32[]{:S(2)}, u32[]{:S(2)}) %collective-permute-start.5) | collective-permute-done | bytes 131104 | tf_op jit(solution)/shard_map/ppermute | solution.py:519
  29.6 1.2 %cross_spectrum.1 = f32[1,2,256,256]{3,2,1,0:T(8,128)} custom-call(bf16[256,256]{1,0:T(8,128)(2,1)S(1)} %collective-permute-done.5.image_ref, bf16[128,256]{1,0:T(8,128)(2,1)S(1)} %copy-done.7, bf16[256,256]{1,0:T(8,128)(2,1)S(1)} %copy-done.6, f32[2,256,256]{2,1,0:T(8,128)S(1)} %own_spectrum.1.own_ref), custom_call_target="tpu_custom_call" | custom-call | flops 536870912 | tf_op jit(solution)/shard_map/cross_spectrum/pallas_call | solution.py:430
  (12 shorter events, 0.0 us)
Async XLA Ops:
  0.0 6.1 %copy-start.1 = (bf16[9,16,16]{2,1,0:T(8,128)(2,1)S(1)}, bf16[9,16,16]{2,1,0:T(8,128)(2,1)}, u32[]{:S(2)}) copy-start(bf16[9,16,16]{2,1,0:T(8,128)(2,1)} %second_ref.1) | copy-start | bytes 13828
  0.0 8.7 %collective-permute-start.1 = (bf16[256,256]{1,0:T(8,128)(2,1)}, bf16[256,256]{1,0:T(8,128)(2,1)S(1)}, u32[]{:S(2)}, u32[]{:S(2)}) collective-permute-start(bf16[256,256]{1,0:T(8,128)(2,1)} %bitcast.4), channel_id=1, source_target_pairs={{1,2},{3,4},{5,6},{7,8},{9,10},{11,12},{13,14},{15,16},{17,18},{19... | collective-permute-start | bytes 393224 | tf_op jit(solution)/shard_map/ppermute | solution.py:524
  4.1 4.6 %collective-permute-start = (bf16[256,256]{1,0:T(8,128)(2,1)}, bf16[256,256]{1,0:T(8,128)(2,1)S(1)}, u32[]{:S(2)}, u32[]{:S(2)}) collective-permute-start(bf16[256,256]{1,0:T(8,128)(2,1)} %bitcast.5), channel_id=1, source_target_pairs={{0,1},{2,3},{4,5},{6,7},{8,9},{10,11},{12,13},{14,15},{16,17},{18,... | collective-permute-start | bytes 393224 | tf_op jit(solution)/shard_map/ppermute | solution.py:524
  6.0 0.7 %copy-start.2 = (f32[16,9]{1,0:T(8,128)S(1)}, f32[16,9]{1,0:T(8,128)}, u32[]{:S(2)}) copy-start(f32[16,9]{1,0:T(8,128)} %first_ref.1) | copy-start | bytes 1732
  6.1 2.7 %copy-start = (bf16[1,256,256]{2,1,0:T(8,128)(2,1)S(1)}, bf16[1,256,256]{2,1,0:T(8,128)(2,1)}, u32[]{:S(2)}) copy-start(bf16[1,256,256]{2,1,0:T(8,128)(2,1)} %param.8) | copy-start | bytes 393220
  6.1 0.7 %copy-start.3 = (f32[16]{0:T(128)S(1)}, f32[16]{0:T(128)}, u32[]{:S(2)}) copy-start(f32[16]{0:T(128)} %param.10) | copy-start | bytes 196
  6.1 0.7 %copy-start.4 = (f32[16]{0:T(128)S(1)}, f32[16]{0:T(128)}, u32[]{:S(2)}) copy-start(f32[16]{0:T(128)} %param.12) | copy-start | bytes 196
  6.1 0.7 %copy-start.5 = (f32[16]{0:T(128)S(1)}, f32[16]{0:T(128)}, u32[]{:S(2)}) copy-start(f32[16]{0:T(128)} %param.13) | copy-start | bytes 196
  11.1 10.5 %collective-permute-start.2 = (bf16[16,128]{1,0:T(8,128)(2,1)S(1)}, bf16[16,128]{1,0:T(8,128)(2,1)S(1)}, u32[]{:S(2)}, u32[]{:S(2)}) collective-permute-start(bf16[16,128]{1,0:T(8,128)(2,1)S(1)} %get-tuple-element.36), channel_id=1, source_target_pairs={{0,32},{32,0},{128,160},{160,128},{288,256},{320,288},{416,384},{4... | collective-permute-start | bytes 12296 | tf_op jit(solution)/shard_map/ppermute | solution.py:533
  12.4 9.8 %collective-permute-start.3 = (bf16[16,128]{1,0:T(8,128)(2,1)S(1)}, bf16[16,128]{1,0:T(8,128)(2,1)S(1)}, u32[]{:S(2)}, u32[]{:S(2)}) collective-permute-start(bf16[16,128]{1,0:T(8,128)(2,1)S(1)} %get-tuple-element.37), channel_id=1, source_target_pairs={{32,64},{64,32},{160,192},{192,160},{256,288},{288,320},{384,416},... | collective-permute-start | bytes 12296 | tf_op jit(solution)/shard_map/ppermute | solution.py:533
  20.8 1.3 %collective-permute-start.4 = (bf16[16,128]{1,0:T(8,128)(2,1)S(1)}, bf16[16,128]{1,0:T(8,128)(2,1)S(1)}, u32[]{:S(2)}, u32[]{:S(2)}) collective-permute-start(bf16[16,128]{1,0:T(8,128)(2,1)S(1)} %get-tuple-element.38), channel_id=1, source_target_pairs={{64,96},{96,64},{192,224},{224,192},{320,352},{352,320},{448,480},... | collective-permute-start | bytes 12296 | tf_op jit(solution)/shard_map/ppermute | solution.py:533
  22.1 2.5 %copy-start.6 = (bf16[256,256]{1,0:T(8,128)(2,1)S(1)}, bf16[256,256]{1,0:T(8,128)(2,1)}, u32[]{:S(2)}) copy-start(bf16[256,256]{1,0:T(8,128)(2,1)} %constant.5.clone.down_ref) | copy-start | bytes 393220
  22.1 2.5 %copy-start.7 = (bf16[128,256]{1,0:T(8,128)(2,1)S(1)}, bf16[128,256]{1,0:T(8,128)(2,1)}, u32[]{:S(2)}) copy-start(bf16[128,256]{1,0:T(8,128)(2,1)} %constant.4.clone.across_ref) | copy-start | bytes 196612
  22.7 6.9 %collective-permute-start.5 = (bf16[256,256]{1,0:T(8,128)(2,1)S(1)}, bf16[256,256]{1,0:T(8,128)(2,1)S(1)}, u32[]{:S(2)}, u32[]{:S(2)}) collective-permute-start(bf16[256,256]{1,0:T(8,128)(2,1)S(1)} %outer_rows.1.image_ref), channel_id=1, source_target_pairs={{128,0},{256,128},{384,256},{129,1},{257,129},{385,257},{130,2},{2... | collective-permute-start | bytes 393224 | tf_op jit(solution)/shard_map/ppermute | solution.py:519

commit v8 on v7

--- a/solution.py
+++ b/solution.py
@@ -414,10 +414,8 @@
             (own_real * real + own_imag * imag, own_imag * real - own_real * imag)
         ):
             held_ref[part, rows, :] = value
-            copies.append(
-                pltpu.make_async_copy(held_ref.at[part, rows], out_ref.at[0, part, rows], sems.at[a, part])
-            )
-            copies[-1].start()
+        copies.append(pltpu.make_async_copy(held_ref.at[:, rows], out_ref.at[0, :, rows], sems.at[a]))
+        copies[-1].start()
     for copy in copies:
         copy.wait()
 
@@ -507,7 +505,7 @@
         "cross_spectrum",
         shaped(1, 2, TILE, TILE, dtype=F32),
         (image, across, down, own),
-        scratch=[pltpu.VMEM((2, TILE, TILE), F32), pltpu.SemaphoreType.DMA((2, 2))],
+        scratch=[pltpu.VMEM((2, TILE, TILE), F32), pltpu.SemaphoreType.DMA((2,))],
         flops=1 << 29,
         out_specs=pl.BlockSpec(memory_space=pl.ANY),
     )

time: 31.1 us -> 31.1 us (level)
  no operation moved by 1% of the time
where the time goes in v8:
time: 31.1 us; the launch traced here: 30.8 us
  starting transfers between devices  18.4 us (59%)
  waiting for transfers between devices  6.2 us (20%)
  Pallas kernels  5.33 us (17%)
  local copies, waits for them, and re-layouts  0.7 us (2%)
    ppermute x3, starting transfers between devices, exchange(): return lax.ppermute(slab, ('gz', 'gy'), pairs)  10.4 us
    ppermute x2, starting transfers between devices, swap(): return lax.ppermute(value, axis, pairs + [(j, i) for i, j in pairs])  6.03 us
    pallas_call x8, Pallas kernels, call(): pl.pallas_call(kernel, name=name, out_shape=out_shape, in_specs=in_specs...  5.33 us
    ppermute x1, waiting for transfers between devices, from_step(): return lax.ppermute(value, axis, pairs)  4.5 us
    ppermute x1, starting transfers between devices, from_step(): return lax.ppermute(value, axis, pairs)  1.92 us
    ppermute x2, waiting for transfers between devices, swap(): return lax.ppermute(value, axis, pairs + [(j, i) for i, j in pairs])  1.12 us
    unnamed x16, local copies, waits for them, and re-layouts  0.7 us
  transfers between devices with their start and end apart: 6, of which 3 were waited for; matrix products, arithmetic and copies ran while one was open for 0% of the time, Pallas kernels for 4%

profile of v8, /device:TPU:72, one launch (start us, length us, event | category | flops | bytes accessed | tf_op | source)
XLA Modules:
  0.0 30.8 jit_solution(12842458791345667751)
XLA Ops:
  0.0 4.1 %collective-permute-start.1 = (bf16[256,256]{1,0:T(8,128)(2,1)}, bf16[256,256]{1,0:T(8,128)(2,1)S(1)}, u32[]{:S(2)}, u32[]{:S(2)}) collective-permute-start(bf16[256,256]{1,0:T(8,128)(2,1)} %bitcast.4), channel_id=1, source_target_pairs={{1,2},{3,4},{5,6},{7,8},{9,10},{11,12},{13,14},{15,16},{17,18},{19... | collective-permute-start | bytes 393224 | tf_op jit(solution)/shard_map/ppermute | solution.py:522
  4.1 1.9 %collective-permute-start = (bf16[256,256]{1,0:T(8,128)(2,1)}, bf16[256,256]{1,0:T(8,128)(2,1)S(1)}, u32[]{:S(2)}, u32[]{:S(2)}) collective-permute-start(bf16[256,256]{1,0:T(8,128)(2,1)} %bitcast.5), channel_id=1, source_target_pairs={{0,1},{2,3},{4,5},{6,7},{8,9},{10,11},{12,13},{14,15},{16,17},{18,... | collective-permute-start | bytes 393224 | tf_op jit(solution)/shard_map/ppermute | solution.py:522
  6.1 0.0 copy-start.3
  6.1 0.0 copy-start.4
  6.1 0.0 copy-start.5
  6.1 0.6 %copy-done.2 = f32[16,9]{1,0:T(8,128)S(1)} copy-done((f32[16,9]{1,0:T(8,128)S(1)}, f32[16,9]{1,0:T(8,128)}, u32[]{:S(2)}) %copy-start.2) | copy-done | bytes 600
  6.7 0.0 copy-done.3
  6.8 0.0 copy-done.4
  6.8 0.0 copy-done.5
  6.8 0.8 %weights.1 = (bf16[128,160]{1,0:T(8,128)(2,1)S(1)}, bf16[48,384]{1,0:T(8,128)(2,1)S(1)}, bf16[128,512]{1,0:T(8,128)(2,1)S(1)}, f32[128,128]{1,0:T(8,128)S(1)}) custom-call(f32[16,9]{1,0:T(8,128)S(1)} %copy-done.2, f32[1,16]{1,0:T(1,128)S(1)} %bitcast.10, bf16[48,384]{1,0:T(8,128)(2,1)S(1)} %last_rows.1.rows_ref, bf16[9,16,16]{2,1,0:T(8,128)(2,1)S(1)} %copy-done.1, ...), custom_call_target="tpu_custom_call" | custom-call | tf_op jit(solution)/shard_map/weights/pallas_call | solution.py:428
  7.6 1.1 %collective-permute-done.1.chip_ref = bf16[256,256]{1,0:T(8,128)(2,1)S(1)} collective-permute-done((bf16[256,256]{1,0:T(8,128)(2,1)}, bf16[256,256]{1,0:T(8,128)(2,1)S(1)}, u32[]{:S(2)}, u32[]{:S(2)}) %collective-permute-start.1) | collective-permute-done | bytes 131104 | tf_op jit(solution)/shard_map/ppermute | solution.py:522
  8.7 0.1 sides.1
  8.8 2.3 %early_rows.1 = (bf16[256,256]{1,0:T(8,128)(2,1)S(1)}, bf16[3,128,256]{2,1,0:T(8,128)(2,1)S(1)}, bf16[3,128,256]{2,1,0:T(8,128)(2,1)S(1)}, bf16[16,128]{1,0:T(8,...) custom-call(bf16[256,256]{1,0:T(8,128)(2,1)S(1)} %bitcast.7, ...), custom_call_target="tpu_custom_call" | custom-call | tf_op jit(solution)/shard_map/early_rows/pallas_call | solution.py:428
  11.1 1.3 %collective-permute-start.2 = (bf16[16,128]{1,0:T(8,128)(2,1)S(1)}, bf16[16,128]{1,0:T(8,128)(2,1)S(1)}, u32[]{:S(2)}, u32[]{:S(2)}) collective-permute-start(bf16[16,128]{1,0:T(8,128)(2,1)S(1)} %get-tuple-element.36), channel_id=1, source_target_pairs={{0,32},{32,0},{128,160},{160,128},{288,256},{320,288},{416,384},{4... | collective-permute-start | bytes 12296 | tf_op jit(solution)/shard_map/ppermute | solution.py:531
  12.4 8.5 %collective-permute-start.3 = (bf16[16,128]{1,0:T(8,128)(2,1)S(1)}, bf16[16,128]{1,0:T(8,128)(2,1)S(1)}, u32[]{:S(2)}, u32[]{:S(2)}) collective-permute-start(bf16[16,128]{1,0:T(8,128)(2,1)S(1)} %get-tuple-element.37), channel_id=1, source_target_pairs={{32,64},{64,32},{160,192},{192,160},{256,288},{288,320},{384,416},... | collective-permute-start | bytes 12296 | tf_op jit(solution)/shard_map/ppermute | solution.py:531
  20.8 0.7 %collective-permute-start.4 = (bf16[16,128]{1,0:T(8,128)(2,1)S(1)}, bf16[16,128]{1,0:T(8,128)(2,1)S(1)}, u32[]{:S(2)}, u32[]{:S(2)}) collective-permute-start(bf16[16,128]{1,0:T(8,128)(2,1)S(1)} %get-tuple-element.38), channel_id=1, source_target_pairs={{64,96},{96,64},{192,224},{224,192},{320,352},{352,320},{448,480},... | collective-permute-start | bytes 12296 | tf_op jit(solution)/shard_map/ppermute | solution.py:531
  21.5 0.1 inner_rows.1
  21.6 0.0 collective-permute-done.2.refs_0_
  21.6 0.6 %collective-permute-done.3.refs_1_ = bf16[16,128]{1,0:T(8,128)(2,1)S(1)} collective-permute-done((bf16[16,128]{1,0:T(8,128)(2,1)S(1)}, bf16[16,128]{1,0:T(8,128)(2,1)S(1)}, u32[]{:S(2)}, u32[]{:S(2)}) %collective-permute-start.3) | collective-permute-done | bytes 4128 | tf_op jit(solution)/shard_map/ppermute | solution.py:531
  22.1 0.6 %outer_rows.1.image_ref = bf16[256,256]{1,0:T(8,128)(2,1)S(1)} custom-call(bf16[256,256]{1,0:T(8,128)(2,1)S(1)} %bitcast.9, bf16[256,128]{1,0:T(8,128)(2,1)S(1)} %get-tuple-element.22.refs_1_.sides_ref, bf16[128,160]{1,0:T(8,128)(2,1)S(1)} %get-tuple-element.23.refs_2_.w1_ref, bf16[48,384]{1,0:T(8,128)(2,1)S(1)} %get-tuple-element.24.refs_3_.rows_ref, ...), custom_call_target="tpu_custom_call" | custom-call | flops 3221225472 | tf_op jit(solution)/shard_map/outer_rows/pallas_call | solution.py:428
  22.7 1.9 %collective-permute-start.5 = (bf16[256,256]{1,0:T(8,128)(2,1)S(1)}, bf16[256,256]{1,0:T(8,128)(2,1)S(1)}, u32[]{:S(2)}, u32[]{:S(2)}) collective-permute-start(bf16[256,256]{1,0:T(8,128)(2,1)S(1)} %outer_rows.1.image_ref), channel_id=1, source_target_pairs={{128,0},{256,128},{384,256},{129,1},{257,129},{385,257},{130,2},{2... | collective-permute-start | bytes 393224 | tf_op jit(solution)/shard_map/ppermute | solution.py:517
  24.7 0.4 %own_spectrum.1.own_ref = f32[2,256,256]{2,1,0:T(8,128)S(1)} custom-call(bf16[256,256]{1,0:T(8,128)(2,1)S(1)} %outer_rows.1.image_ref, bf16[128,256]{1,0:T(8,128)(2,1)S(1)} %copy-done.7, bf16[256,256]{1,0:T(8,128)(2,1)S(1)} %copy-done.6), custom_call_target="tpu_custom_call" | custom-call | flops 536870912 | tf_op jit(solution)/shard_map/own_spectrum/pallas_call | solution.py:428
  25.1 4.5 %collective-permute-done.5.image_ref = bf16[256,256]{1,0:T(8,128)(2,1)S(1)} collective-permute-done((bf16[256,256]{1,0:T(8,128)(2,1)S(1)}, bf16[256,256]{1,0:T(8,128)(2,1)S(1)}, u32[]{:S(2)}, u32[]{:S(2)}) %collective-permute-start.5) | collective-permute-done | bytes 131104 | tf_op jit(solution)/shard_map/ppermute | solution.py:517
  29.6 1.2 %cross_spectrum.1 = f32[1,2,256,256]{3,2,1,0:T(8,128)} custom-call(bf16[256,256]{1,0:T(8,128)(2,1)S(1)} %collective-permute-done.5.image_ref, bf16[128,256]{1,0:T(8,128)(2,1)S(1)} %copy-done.7, bf16[256,256]{1,0:T(8,128)(2,1)S(1)} %copy-done.6, f32[2,256,256]{2,1,0:T(8,128)S(1)} %own_spectrum.1.own_ref), custom_call_target="tpu_custom_call" | custom-call | flops 536870912 | tf_op jit(solution)/shard_map/cross_spectrum/pallas_call | solution.py:428
  (12 shorter events, 0.0 us)
Async XLA Ops:
  0.0 6.1 %copy-start.1 = (bf16[9,16,16]{2,1,0:T(8,128)(2,1)S(1)}, bf16[9,16,16]{2,1,0:T(8,128)(2,1)}, u32[]{:S(2)}) copy-start(bf16[9,16,16]{2,1,0:T(8,128)(2,1)} %second_ref.1) | copy-start | bytes 13828
  0.0 8.7 %collective-permute-start.1 = (bf16[256,256]{1,0:T(8,128)(2,1)}, bf16[256,256]{1,0:T(8,128)(2,1)S(1)}, u32[]{:S(2)}, u32[]{:S(2)}) collective-permute-start(bf16[256,256]{1,0:T(8,128)(2,1)} %bitcast.4), channel_id=1, source_target_pairs={{1,2},{3,4},{5,6},{7,8},{9,10},{11,12},{13,14},{15,16},{17,18},{19... | collective-permute-start | bytes 393224 | tf_op jit(solution)/shard_map/ppermute | solution.py:522
  4.1 4.6 %collective-permute-start = (bf16[256,256]{1,0:T(8,128)(2,1)}, bf16[256,256]{1,0:T(8,128)(2,1)S(1)}, u32[]{:S(2)}, u32[]{:S(2)}) collective-permute-start(bf16[256,256]{1,0:T(8,128)(2,1)} %bitcast.5), channel_id=1, source_target_pairs={{0,1},{2,3},{4,5},{6,7},{8,9},{10,11},{12,13},{14,15},{16,17},{18,... | collective-permute-start | bytes 393224 | tf_op jit(solution)/shard_map/ppermute | solution.py:522
  6.0 0.7 %copy-start.2 = (f32[16,9]{1,0:T(8,128)S(1)}, f32[16,9]{1,0:T(8,128)}, u32[]{:S(2)}) copy-start(f32[16,9]{1,0:T(8,128)} %first_ref.1) | copy-start | bytes 1732
  6.1 2.7 %copy-start = (bf16[1,256,256]{2,1,0:T(8,128)(2,1)S(1)}, bf16[1,256,256]{2,1,0:T(8,128)(2,1)}, u32[]{:S(2)}) copy-start(bf16[1,256,256]{2,1,0:T(8,128)(2,1)} %param.8) | copy-start | bytes 393220
  6.1 0.7 %copy-start.3 = (f32[16]{0:T(128)S(1)}, f32[16]{0:T(128)}, u32[]{:S(2)}) copy-start(f32[16]{0:T(128)} %param.10) | copy-start | bytes 196
  6.1 0.7 %copy-start.4 = (f32[16]{0:T(128)S(1)}, f32[16]{0:T(128)}, u32[]{:S(2)}) copy-start(f32[16]{0:T(128)} %param.12) | copy-start | bytes 196
  6.1 0.7 %copy-start.5 = (f32[16]{0:T(128)S(1)}, f32[16]{0:T(128)}, u32[]{:S(2)}) copy-start(f32[16]{0:T(128)} %param.13) | copy-start | bytes 196
  11.1 10.5 %collective-permute-start.2 = (bf16[16,128]{1,0:T(8,128)(2,1)S(1)}, bf16[16,128]{1,0:T(8,128)(2,1)S(1)}, u32[]{:S(2)}, u32[]{:S(2)}) collective-permute-start(bf16[16,128]{1,0:T(8,128)(2,1)S(1)} %get-tuple-element.36), channel_id=1, source_target_pairs={{0,32},{32,0},{128,160},{160,128},{288,256},{320,288},{416,384},{4... | collective-permute-start | bytes 12296 | tf_op jit(solution)/shard_map/ppermute | solution.py:531
  12.4 9.8 %collective-permute-start.3 = (bf16[16,128]{1,0:T(8,128)(2,1)S(1)}, bf16[16,128]{1,0:T(8,128)(2,1)S(1)}, u32[]{:S(2)}, u32[]{:S(2)}) collective-permute-start(bf16[16,128]{1,0:T(8,128)(2,1)S(1)} %get-tuple-element.37), channel_id=1, source_target_pairs={{32,64},{64,32},{160,192},{192,160},{256,288},{288,320},{384,416},... | collective-permute-start | bytes 12296 | tf_op jit(solution)/shard_map/ppermute | solution.py:531
  20.8 1.3 %collective-permute-start.4 = (bf16[16,128]{1,0:T(8,128)(2,1)S(1)}, bf16[16,128]{1,0:T(8,128)(2,1)S(1)}, u32[]{:S(2)}, u32[]{:S(2)}) collective-permute-start(bf16[16,128]{1,0:T(8,128)(2,1)S(1)} %get-tuple-element.38), channel_id=1, source_target_pairs={{64,96},{96,64},{192,224},{224,192},{320,352},{352,320},{448,480},... | collective-permute-start | bytes 12296 | tf_op jit(solution)/shard_map/ppermute | solution.py:531
  22.1 2.5 %copy-start.6 = (bf16[256,256]{1,0:T(8,128)(2,1)S(1)}, bf16[256,256]{1,0:T(8,128)(2,1)}, u32[]{:S(2)}) copy-start(bf16[256,256]{1,0:T(8,128)(2,1)} %constant.5.clone.down_ref) | copy-start | bytes 393220
  22.1 2.5 %copy-start.7 = (bf16[128,256]{1,0:T(8,128)(2,1)S(1)}, bf16[128,256]{1,0:T(8,128)(2,1)}, u32[]{:S(2)}) copy-start(bf16[128,256]{1,0:T(8,128)(2,1)} %constant.4.clone.across_ref) | copy-start | bytes 196612
  22.7 6.9 %collective-permute-start.5 = (bf16[256,256]{1,0:T(8,128)(2,1)S(1)}, bf16[256,256]{1,0:T(8,128)(2,1)S(1)}, u32[]{:S(2)}, u32[]{:S(2)}) collective-permute-start(bf16[256,256]{1,0:T(8,128)(2,1)S(1)} %outer_rows.1.image_ref), channel_id=1, source_target_pairs={{128,0},{256,128},{384,256},{129,1},{257,129},{385,257},{130,2},{2... | collective-permute-start | bytes 393224 | tf_op jit(solution)/shard_map/ppermute | solution.py:517
